TPU v7x, 32 devices: a whole 2x2x4 slice. The times are simulated.
32 devices in a mesh: dp: 8 (over z, x), blk: 4 (over y, core).
Axes of the slice: x: 2, y: 2, z: 4, core: 2. Of those that a mesh axis runs over, the one named last changes fastest.
Arguments:
- tokens: bfloat16 [8192, 1024], P(('dp', 'blk')), may hold values from -6 to 6
- lengths: int32 [8, 5], P('dp'), may hold values from 0 to 512, as said below
- ln1_gain: float32 [1024], replicated, may hold values from 0.5 to 1.5
- ln1_bias: float32 [1024], replicated, may hold values from -1.75 to 1.75
- w_qkv: bfloat16 [1024, 3072], replicated, may hold values from -0.1875 to 0.1875
- qv_bias: float32 [2048], replicated, may hold values from -1.75 to 1.75
- head_scale: float32 [16], replicated, may hold values from 0.5 to 2
- w_out: bfloat16 [1024, 1024], replicated, may hold values from -0.1875 to 0.1875
- out_bias: float32 [1024], replicated, may hold values from -0.625 to 0.625
- lnpa_gain: float32 [1024], replicated, may hold values from 0.5 to 1.5
- lnpa_bias: float32 [1024], replicated, may hold values from -1.75 to 1.75
- ln2_gain: float32 [1024], replicated, may hold values from 0.5 to 1.5
- ln2_bias: float32 [1024], replicated, may hold values from -1.75 to 1.75
- w_fc1: bfloat16 [1024, 4096], replicated, may hold values from -0.1875 to 0.1875
- fc1_bias: float32 [4096], replicated, may hold values from -1.75 to 1.75
- lnf_gain: float32 [4096], replicated, may hold values from 0.5 to 1.5
- lnf_bias: float32 [4096], replicated, may hold values from -1.75 to 1.75
- w_fc2: bfloat16 [4096, 1024], replicated, may hold values from -0.09375 to 0.09375
- fc2_bias: float32 [1024], replicated, may hold values from -1.75 to 1.75
- cotangent: bfloat16 [8192, 1024], P(('dp', 'blk')), may hold values from -6 to 6
Outputs:
- layer_out: bfloat16 [8192, 1024], P(('dp', 'blk'))
- grad_tokens: float32 [8192, 1024], P(('dp', 'blk'))
- grad_ln1_gain: float32 [1024], replicated
- grad_ln1_bias: float32 [1024], replicated
- grad_w_qkv: float32 [1024, 3072], P(('dp', 'blk'))
- grad_qv_bias: float32 [2048], replicated
- grad_head_scale: float32 [16], replicated
- grad_w_out: float32 [1024, 1024], P(('dp', 'blk'))
- grad_out_bias: float32 [1024], replicated
- grad_lnpa_gain: float32 [1024], replicated
- grad_lnpa_bias: float32 [1024], replicated
- grad_ln2_gain: float32 [1024], replicated
- grad_ln2_bias: float32 [1024], replicated
- grad_w_fc1: float32 [1024, 4096], P(('dp', 'blk'))
- grad_fc1_bias: float32 [4096], replicated
- grad_lnf_gain: float32 [4096], replicated
- grad_lnf_bias: float32 [4096], replicated
- grad_w_fc2: float32 [4096, 1024], P(('dp', 'blk'))
- grad_fc2_bias: float32 [1024], replicated
Inputs may be any that keep to these rules, and one draw needn't show every extreme that they name: Each row of lengths sums to 1024 and is a window of a stream of whole sequences of 512 and 256 tokens: its first entry, 1 to 255, is the end of a sequence begun before the bucket; then come whole sequences (two of 512; one of 512 and two of 256 in some order; or four of 256), the last of them cut short by the first entry; trailing entries are 0.
All inputs are finite; a program needn't handle non-finite values.
Results may differ from a plain program's by a relative error of at most 0.018.
Values may be sent and summed in bfloat16 or wider, within the bound.
A program may use at most 256 MiB of HBM per device.

v0:
```python
import math

import jax
import jax.numpy as jnp
from jax import lax
from jax.sharding import PartitionSpec as P

HEADS = 16


def norm_rows(values_in, gain_vec, bias_vec):
    row_mean = jnp.mean(values_in, axis=-1, keepdims=True)
    centered = values_in - row_mean
    variance = jnp.mean(centered * centered, axis=-1, keepdims=True)
    return centered * lax.rsqrt(variance + 1e-05) * gain_vec + bias_vec


def gelu_exact(pre_values):
    return 0.5 * pre_values * (1.0 + lax.erf(pre_values * 0.7071067811865476))


def over_rows(left, right):
    return lax.dot_general(
        left, right, (((0,), (0,)), ((), ())), preferred_element_type=jnp.float32
    )


def over_cols(left, right):
    return lax.dot_general(
        left, right, (((1,), (1,)), ((), ())), preferred_element_type=jnp.float32
    )


def shards(
    tokens,
    lengths,
    ln1_gain,
    ln1_bias,
    w_qkv,
    qv_bias,
    head_scale,
    w_out,
    out_bias,
    lnpa_gain,
    lnpa_bias,
    ln2_gain,
    ln2_bias,
    w_fc1,
    fc1_bias,
    lnf_gain,
    lnf_bias,
    w_fc2,
    fc2_bias,
    cotangent,
):
    row_count, width = tokens.shape
    head_dim = width // HEADS
    factor = head_dim ** (-0.5)
    group = row_count * lax.axis_size("blk")
    own_start = lax.axis_index("blk") * row_count
    seq_ends = jnp.cumsum(lengths[0])
    positions = jnp.arange(group, dtype=jnp.int32)
    labels = jnp.sum((positions[:, None] >= seq_ends[None, :]).astype(jnp.int32), axis=1)
    q_labels = lax.dynamic_slice_in_dim(labels, own_start, row_count, 0)
    q_spots = own_start + jnp.arange(row_count, dtype=jnp.int32)
    inputs = tokens.astype(jnp.float32)
    normed_in, ln1_back = jax.vjp(norm_rows, inputs, ln1_gain, ln1_bias)
    low_in = normed_in.astype(jnp.bfloat16)
    projected = jnp.dot(low_in, w_qkv, preferred_element_type=jnp.float32)
    queries = (projected[:, :width] + qv_bias[:width]).astype(jnp.bfloat16)
    key_rows = projected[:, width : 2 * width].astype(jnp.bfloat16)
    value_rows = (projected[:, 2 * width :] + qv_bias[width:]).astype(jnp.bfloat16)
    query_heads = queries.reshape(row_count, HEADS, head_dim)

    def scored(key_block, start):
        count = key_block.shape[0]
        key_heads = key_block.reshape(count, HEADS, head_dim)
        raw_scores = (
            jnp.einsum("qhd,khd->hqk", query_heads, key_heads, preferred_element_type=jnp.float32)
            * factor
        )
        k_labels = lax.dynamic_slice_in_dim(labels, start, count, 0)
        k_spots = start + jnp.arange(count, dtype=jnp.int32)
        visible = (k_labels[None, :] == q_labels[:, None]) & (k_spots[None, :] <= q_spots[:, None])
        return (raw_scores, visible[None], key_heads)

    def by_blocks(step_fn, carry, pieces):
        count = pieces[0].shape[0]
        unit = max(1, 1024 // row_count) * row_count
        step = count if count <= unit else math.gcd(count, unit)

        def inner(block_index, state):
            offset = block_index * step
            sub_pieces = tuple((lax.dynamic_slice_in_dim(item, offset, step, 0) for item in pieces))
            return step_fn(state, sub_pieces, offset)

        return lax.fori_loop(0, count // step, inner, carry)

    def max_step(carry, pieces, start):
        top_score, totals = carry
        raw_scores, visible, key_heads = scored(pieces[0], start)
        raw_scores = jnp.where(visible, raw_scores, -1e30)
        new_top = jnp.maximum(top_score, jnp.max(raw_scores, axis=-1))
        totals = totals * jnp.exp(top_score - new_top) + jnp.sum(
            jnp.where(visible, jnp.exp(raw_scores - new_top[..., None]), 0.0), axis=-1
        )
        return (new_top, totals)

    start_top = jnp.full((HEADS, row_count), -1e30, jnp.float32)
    start_total = jnp.zeros((HEADS, row_count), jnp.float32)
    top_score, totals = by_blocks(
        max_step, (start_top, start_total), (lax.all_gather(key_rows, "blk", axis=0, tiled=True),)
    )
    log_total = top_score + jnp.log(totals)

    def value_step(carry, pieces, start):
        weighted, leftover = carry
        raw_scores, visible, key_heads = scored(pieces[0], start)
        value_heads = pieces[1].reshape(pieces[1].shape[0], HEADS, head_dim)
        probs = jnp.where(visible, jnp.exp(raw_scores - log_total[..., None]), 0.0)
        low_probs = probs.astype(jnp.bfloat16)
        rest_probs = (probs - low_probs.astype(jnp.float32)).astype(jnp.bfloat16)
        weighted = weighted + jnp.einsum(
            "hqk,khd->qhd", low_probs, value_heads, preferred_element_type=jnp.float32
        )
        leftover = leftover + jnp.einsum(
            "hqk,khd->qhd", rest_probs, value_heads, preferred_element_type=jnp.float32
        )
        return (weighted, leftover)

    empty_heads = jnp.zeros((row_count, HEADS, head_dim), jnp.float32)
    weighted, leftover = by_blocks(
        value_step,
        (empty_heads, empty_heads),
        (
            lax.all_gather(key_rows, "blk", axis=0, tiled=True),
            lax.all_gather(value_rows, "blk", axis=0, tiled=True),
        ),
    )
    attended = weighted.reshape(row_count, width)
    head_gain = jnp.repeat(head_scale, head_dim)
    scaled = (attended * head_gain).astype(jnp.bfloat16)
    attn_out = jnp.dot(scaled, w_out, preferred_element_type=jnp.float32) + out_bias
    branch, pa_back = jax.vjp(norm_rows, attn_out, lnpa_gain, lnpa_bias)
    first_sum = inputs + branch
    normed_mid, ln2_back = jax.vjp(norm_rows, first_sum, ln2_gain, ln2_bias)
    low_mid = normed_mid.astype(jnp.bfloat16)
    pre_act = jnp.dot(low_mid, w_fc1, preferred_element_type=jnp.float32) + fc1_bias
    activated, gelu_back = jax.vjp(gelu_exact, pre_act)
    ffn_normed, lnf_back = jax.vjp(norm_rows, activated, lnf_gain, lnf_bias)
    low_ffn = ffn_normed.astype(jnp.bfloat16)
    layer_out = (
        first_sum + jnp.dot(low_ffn, w_fc2, preferred_element_type=jnp.float32) + fc2_bias
    ).astype(jnp.bfloat16)
    d_output = cotangent.astype(jnp.float32)
    grad_w2 = over_rows(low_ffn, cotangent)
    grad_c2 = jnp.sum(d_output, axis=0)
    d_ffn = over_cols(cotangent, w_fc2)
    d_active, grad_lnf_gain, grad_lnf_bias = lnf_back(d_ffn)
    (d_pre,) = gelu_back(d_active)
    low_pre = d_pre.astype(jnp.bfloat16)
    grad_w1 = over_rows(low_mid, low_pre)
    grad_c1 = jnp.sum(low_pre.astype(jnp.float32), axis=0)
    d_mid = over_cols(low_pre, w_fc1)
    d_first_norm, grad_ln2_gain, grad_ln2_bias = ln2_back(d_mid)
    d_first = d_output + d_first_norm
    d_attn, grad_pa_gain, grad_pa_bias = pa_back(d_first)
    low_attn = d_attn.astype(jnp.bfloat16)
    grad_bo = jnp.sum(low_attn.astype(jnp.float32), axis=0)
    grad_wo = over_rows(scaled, low_attn)
    d_scaled = over_cols(low_attn, w_out)
    grad_hs = jnp.sum((d_scaled * attended).reshape(row_count, HEADS, head_dim), axis=(0, 2))
    d_attended = (d_scaled * head_gain).astype(jnp.bfloat16)
    d_heads = d_attended.reshape(row_count, HEADS, head_dim)
    delta_rows = jnp.sum(d_heads.astype(jnp.float32) * (weighted + leftover), axis=-1)
    delta = delta_rows.T

    def back_step(carry, pieces, start):
        count = pieces[0].shape[0]
        raw_scores, visible, key_heads = scored(pieces[0], start)
        value_heads = pieces[1].reshape(count, HEADS, head_dim)
        probs = jnp.where(visible, jnp.exp(raw_scores - log_total[..., None]), 0.0)
        d_probs = jnp.einsum(
            "qhd,khd->hqk", d_heads, value_heads, preferred_element_type=jnp.float32
        )
        d_scores = (probs * (d_probs - delta[..., None])).astype(jnp.bfloat16)
        d_query = (
            carry[0]
            + jnp.einsum("hqk,khd->qhd", d_scores, key_heads, preferred_element_type=jnp.float32)
            * factor
        )
        key_grad, value_grad = (carry[1], carry[2])
        low_probs = probs.astype(jnp.bfloat16)
        d_value = jnp.einsum(
            "hqk,qhd->khd", low_probs, d_heads, preferred_element_type=jnp.float32
        ).reshape(count, width)
        d_key = (
            jnp.einsum("hqk,qhd->khd", d_scores, query_heads, preferred_element_type=jnp.float32)
            * factor
        ).reshape(count, width)
        key_grad = lax.dynamic_update_slice_in_dim(
            key_grad, lax.dynamic_slice_in_dim(key_grad, start, count, 0) + d_key, start, 0
        )
        value_grad = lax.dynamic_update_slice_in_dim(
            value_grad, lax.dynamic_slice_in_dim(value_grad, start, count, 0) + d_value, start, 0
        )
        return (d_query, key_grad, value_grad)

    empty_group = jnp.zeros((group, width), jnp.float32)
    start_carry = (empty_heads, empty_group, empty_group)
    results = by_blocks(
        back_step,
        start_carry,
        (
            lax.all_gather(key_rows, "blk", axis=0, tiled=True),
            lax.all_gather(value_rows, "blk", axis=0, tiled=True),
        ),
    )
    d_query = results[0]
    own_keys, own_values = (
        lax.psum_scatter(
            results[1].astype(jnp.bfloat16), "blk", scatter_dimension=0, tiled=True
        ).astype(jnp.float32),
        lax.psum_scatter(
            results[2].astype(jnp.bfloat16), "blk", scatter_dimension=0, tiled=True
        ).astype(jnp.float32),
    )
    low_q = d_query.reshape(row_count, width).astype(jnp.bfloat16)
    low_k = own_keys.astype(jnp.bfloat16)
    low_v = own_values.astype(jnp.bfloat16)
    d_projected = jnp.concatenate([low_q, low_k, low_v], axis=1)
    grad_wqkv = over_rows(low_in, d_projected)
    grad_qv = jnp.concatenate(
        [jnp.sum(low_q.astype(jnp.float32), axis=0), jnp.sum(low_v.astype(jnp.float32), axis=0)]
    )
    d_in = over_cols(d_projected, w_qkv)
    d_in_norm, grad_ln1_gain, grad_ln1_bias = ln1_back(d_in)
    grad_tokens = d_first + d_in_norm
    share_wqkv, share_wo, share_w1, share_w2 = (
        lax.psum_scatter(grad_wqkv, ("dp", "blk"), scatter_dimension=0, tiled=True),
        lax.psum_scatter(grad_wo, ("dp", "blk"), scatter_dimension=0, tiled=True),
        lax.psum_scatter(grad_w1, ("dp", "blk"), scatter_dimension=0, tiled=True),
        lax.psum_scatter(grad_w2, ("dp", "blk"), scatter_dimension=0, tiled=True),
    )
    summed = lax.psum(
        (
            grad_ln1_gain,
            grad_ln1_bias,
            grad_qv,
            grad_hs,
            grad_bo,
            grad_pa_gain,
            grad_pa_bias,
            grad_ln2_gain,
            grad_ln2_bias,
            grad_c1,
            grad_lnf_gain,
            grad_lnf_bias,
            grad_c2,
        ),
        ("dp", "blk"),
    )
    return (
        layer_out,
        grad_tokens,
        summed[0],
        summed[1],
        share_wqkv,
        summed[2],
        summed[3],
        share_wo,
        summed[4],
        summed[5],
        summed[6],
        summed[7],
        summed[8],
        share_w1,
        summed[9],
        summed[10],
        summed[11],
        share_w2,
        summed[12],
    )


def solution(mesh):
    in_specs = (
        P(("dp", "blk"), None),
        P("dp", None),
        P(),
        P(),
        P(),
        P(),
        P(),
        P(),
        P(),
        P(),
        P(),
        P(),
        P(),
        P(),
        P(),
        P(),
        P(),
        P(),
        P(),
        P(("dp", "blk"), None),
    )
    out_specs = (
        P(("dp", "blk"), None),
        P(("dp", "blk"), None),
        P(),
        P(),
        P(("dp", "blk"), None),
        P(),
        P(),
        P(("dp", "blk"), None),
        P(),
        P(),
        P(),
        P(),
        P(),
        P(("dp", "blk"), None),
        P(),
        P(),
        P(),
        P(("dp", "blk"), None),
        P(),
    )
    return jax.shard_map(shards, mesh=mesh, in_specs=in_specs, out_specs=out_specs, check_vma=False)
```

profile of v0, /device:TPU:0, one launch (start us, length us, event | category | flops | bytes accessed | tf_op | source)
XLA Modules:
  0.0 1057.6 jit_solution(10441434318306635688)
XLA Ops:
  9.9 4.9 fusion.45
  17.5 2.6 fusion.22
  21.3 21.6 %all-gather.5.cloned.1.call-done = bf16[1024,1024]{1,0:T(8,128)(2,1)} async-done(((bf16[256,1024]{1,0:T(8,128)(2,1)}), bf16[1024,1024]{1,0:T(8,128)(2,1)}) %all-gather.5.cloned.1.call-update) | async-done | bytes 2097168 | tf_op jit(solution)/shard_map/all_gather | solution.py:136
  42.9 4.5 copy.57
  47.3 4.5 select_reduce_fusion.1
  51.8 5.1 select_reduce_fusion
  57.7 9.9 all-gather.3.cloned.1.call-done
  67.6 4.0 copy.55
  71.6 9.1 fusion.29
  80.6 2.6 copy.58
  86.4 5.7 fusion.53
  92.1 7.7 multiply_reduce_fusion.1
  99.9 2.4 multiply_reduce_fusion
  102.2 4.0 convert_reduce_fusion
  106.3 7.4 multiply_reduce_fusion.3
  120.7 10.8 %convolution_convert_fusion = bf16[16,64,1024]{2,1,0:T(8,128)(2,1)} fusion(bf16[256,16,64]{0,2,1:T(8,128)(2,1)} %bitcast.65, f32[16,256,1024]{2,1,0:T(8,128)} %copy-done.2, f32[16,256]{1,0:T(8,128)S(1)} %log_add_fusion, pred[256,1024]{1,0:T(8,128)(4,1)S(1)} %fusion.24), kind=kOutput, calls=%fused_computation.20 | convolution fusion | flops 554696704 | bytes 19677184 | tf_op jit(solution)/shard_map/while/body/eval_jaxpr/hqk,qhd->khd/dot_general | solution.py:194
  131.6 9.3 fusion.14
  140.9 9.5 multiply_convert_fusion
  150.4 2.9 multiply_convert_fusion.1
  154.7 6.1 convert_reduce_fusion.5
  163.1 34.0 %reduce-scatter.7.cloned.1.call-done = bf16[256,1024]{0,1:T(8,128)(2,1)} async-done(((bf16[1024,1024]{0,1:T(8,128)(2,1)}), bf16[256,1024]{0,1:T(8,128)(2,1)}) %reduce-scatter.7.cloned.1.call-update) | async-done | bytes 524304 | tf_op jit(solution)/shard_map/reduce_scatter | solution.py:221
  197.1 5.8 fusion.50
  205.9 2.8 fusion.31
  209.8 6.5 fusion.25
  217.5 9.8 fusion.48
  228.4 10.6 fusion.49
  239.7 8.1 fusion.12
  249.2 107.1 %all-reduce.3.cloned.1.call-done = (f32[1024]{0:T(1024)}, f32[1024]{0:T(1024)}, f32[2048]{0:T(1024)}, f32[16]{0:T(128)}, f32[1024]{0:T(1024)}, /*index=5*/f32[10...) async-done(((f32[1024]{0:T(1024)}, f32[1024]{0:T(1024)}, ...) | async-done | bytes 90192 | tf_op jit(solution)/shard_map/psum | solution.py:245
  356.3 147.4 %reduce-scatter.13.cloned.1.call-done = f32[32,1024]{1,0:T(8,128)} async-done(((f32[1024,1024]{1,0:T(8,128)}), f32[32,1024]{1,0:T(8,128)}) %reduce-scatter.13.cloned.1.call-update) | async-done | bytes 131088 | tf_op jit(solution)/shard_map/reduce_scatter | solution.py:241
  503.7 157.9 %reduce-scatter.11.cloned.1.call-done = f32[32,3072]{1,0:T(8,128)} async-done(((f32[1024,3072]{1,0:T(8,128)}), f32[32,3072]{1,0:T(8,128)}) %reduce-scatter.11.cloned.1.call-update) | async-done | bytes 393232 | tf_op jit(solution)/shard_map/reduce_scatter | solution.py:240
  661.6 185.1 %reduce-scatter.15.cloned.1.call-done = f32[32,4096]{1,0:T(8,128)} async-done(((f32[1024,4096]{1,0:T(8,128)}), f32[32,4096]{1,0:T(8,128)}) %reduce-scatter.15.cloned.1.call-update) | async-done | bytes 524304 | tf_op jit(solution)/shard_map/reduce_scatter | solution.py:242
  846.7 187.6 %reduce-scatter.17.cloned.1.call-done = f32[128,1024]{1,0:T(8,128)} async-done(((f32[4096,1024]{1,0:T(8,128)}), f32[128,1024]{1,0:T(8,128)}) %reduce-scatter.17.cloned.1.call-update) | async-done | bytes 524304 | tf_op jit(solution)/shard_map/reduce_scatter | solution.py:243
  (156 shorter events, 45.7 us)
Async XLA Ops:
  7.2 76.1 %copy-start = (bf16[1024,1024]{1,0:T(8,128)(2,1)S(1)}, bf16[1024,1024]{1,0:T(8,128)(2,1)}, u32[]{:S(2)}) copy-start(bf16[1024,1024]{1,0:T(8,128)(2,1)} %param.27) | copy-start | bytes 6291460
  7.2 35.7 %all-gather.5.cloned.1.call-start = ((), (), s32[]{:S(2)}) async-start(), calls=%async_computation.7 | async-start | bytes 2621440 | tf_op jit(solution)/shard_map/all_gather | solution.py:136
  9.9 7.5 copy-start.33
  17.4 50.2 %all-gather.3.cloned.1.call-start = ((), (), s32[]{:S(2)}) async-start(), calls=%async_computation.6 | async-start | bytes 2621440 | tf_op jit(solution)/shard_map/all_gather | solution.py:137
  20.1 143.0 %reduce-scatter.9.cloned.1.call-start = ((), (), s32[]{:S(2)}) async-start(), calls=%async_computation.9 | async-start | bytes 2621440 | tf_op jit(solution)/shard_map/reduce_scatter | solution.py:224
  51.8 5.9 copy-start.2
  71.6 11.7 %copy-start.32 = (f32[1024]{0:T(1024)S(1)}, f32[1024]{0:T(1024)}, u32[]{:S(2)}) copy-start(f32[1024]{0:T(1024)} %param.28) | copy-start | bytes 12292
  80.6 5.0 copy-start.5
  80.6 5.0 copy-start.31
  80.6 5.0 copy-start.34
  86.0 27.6 %copy-start.7 = (f32[256,1024]{1,0:T(8,128)}, f32[256,1024]{1,0:T(8,128)S(1)}, u32[]{:S(2)}) copy-start(f32[256,1024]{1,0:T(8,128)S(1)} %get-tuple-element.161) | copy-start | bytes 3145732
  86.4 5.8 copy-start.21
  86.4 5.8 copy-start.26
  92.1 10.2 copy-start.4
  106.3 7.4 copy-start.13
  120.7 10.9 %copy-start.20 = (bf16[1024,1024]{0,1:T(8,128)(2,1)S(1)}, bf16[1024,1024]{0,1:T(8,128)(2,1)}, u32[]{:S(2)}) copy-start(bf16[1024,1024]{0,1:T(8,128)(2,1)} %copy.55) | copy-start | bytes 6291460
  131.5 65.6 %reduce-scatter.7.cloned.1.call-start = ((), (), s32[]{:S(2)}) async-start(), calls=%async_computation.8 | async-start | bytes 2621440 | tf_op jit(solution)/shard_map/reduce_scatter | solution.py:221
  131.6 9.3 copy-start.24
  150.4 4.2 copy-start.3
  150.4 4.3 copy-start.6
  154.6 42.5 %copy-start.25 = (f32[1024]{0:T(1024)S(1)}, f32[1024]{0:T(1024)}, u32[]{:S(2)}) copy-start(f32[1024]{0:T(1024)} %param.22) | copy-start | bytes 12292
  154.6 201.7 %all-reduce.3.cloned.1.call-start = ((), (), s32[]{:S(2)}) async-start(), calls=%async_computation.14 | async-start | bytes 181248 | tf_op jit(solution)/shard_map/psum | solution.py:245
  197.1 7.9 copy-start.19
  197.1 8.8 copy-start.10
  197.1 8.8 copy-start.15
  205.9 297.8 %reduce-scatter.13.cloned.1.call-start = ((), (), s32[]{:S(2)}) async-start(), calls=%async_computation.11 | async-start | bytes 4325376 | tf_op jit(solution)/shard_map/reduce_scatter | solution.py:241
  208.7 452.8 %reduce-scatter.11.cloned.1.call-start = ((), (), s32[]{:S(2)}) async-start(), calls=%async_computation.10 | async-start | bytes 12976128 | tf_op jit(solution)/shard_map/reduce_scatter | solution.py:240
  216.3 630.3 %reduce-scatter.15.cloned.1.call-start = ((), (), s32[]{:S(2)}) async-start(), calls=%async_computation.12 | async-start | bytes 17301504 | tf_op jit(solution)/shard_map/reduce_scatter | solution.py:242
  227.4 806.9 %reduce-scatter.17.cloned.1.call-start = ((), (), s32[]{:S(2)}) async-start(), calls=%async_computation.13 | async-start | bytes 17301504 | tf_op jit(solution)/shard_map/reduce_scatter | solution.py:243
  239.7 8.2 copy-start.12
  239.7 8.2 copy-start.17
  239.7 811.1 %copy-start.1 = (bf16[1024,1024]{1,0:T(8,128)(2,1)S(1)}, bf16[1024,1024]{1,0:T(8,128)(2,1)}, u32[]{:S(2)}) copy-start(bf16[1024,1024]{1,0:T(8,128)(2,1)} %param.27) | copy-start | bytes 6291460
  (16 other events, 33.3 us)
Sparse Core Ops, SparseCore 0:
  17.5 25.2 all-gather.4
  45.0 22.5 all-gather.2
  131.6 31.4 reduce-scatter.8
  165.7 31.3 reduce-scatter.6
  206.0 150.3 all-reduce.2
  361.2 142.4 reduce-scatter.12
  510.3 151.2 reduce-scatter.10
  664.5 182.0 reduce-scatter.14
  849.7 184.5 reduce-scatter.16
where the time goes:
time: 1060 us
  waiting for transfers between devices  852 us (80%)
  matrix products  125 us (12%)
  local copies, waits for them, and re-layouts  39.9 us (4%)
  other arithmetic  25.1 us (2%)
  between operations  14.6 us (1%)
    reduce_scatter x1, waiting for transfers between devices, shards(): lax.psum_scatter(grad_w2, ('dp', 'blk'), scatter_dimension=0, tiled=True)  188 us
    reduce_scatter x1, waiting for transfers between devices, shards(): lax.psum_scatter(grad_w1, ('dp', 'blk'), scatter_dimension=0, tiled=True)  185 us
    reduce_scatter x1, waiting for transfers between devices, shards(): lax.psum_scatter(grad_wqkv, ('dp', 'blk'), scatter_dimension=0, tiled=True)  158 us
    reduce_scatter x1, waiting for transfers between devices, shards(): lax.psum_scatter(grad_wo, ('dp', 'blk'), scatter_dimension=0, tiled=True)  147 us
    psum x1, waiting for transfers between devices, shards(): lax.psum((grad_ln1_gain, grad_ln1_bias, grad_qv, grad_hs, grad_bo, grad_p...  107 us
    reduce_scatter x1, waiting for transfers between devices, shards(): lax.psum_scatter(results[1].astype(jnp.bfloat16), 'blk', scatter_dimensio...  34 us
    dot_general x4, matrix products, over_rows(): lax.dot_general(left, right, (((0,), (0,)), ((), ())), preferred_element_...  29.7 us
    unnamed x91, local copies, waits for them, and re-layouts  25.4 us
  transfers between devices with their start and end apart: 9, of which 9 were waited for; matrix products, arithmetic and copies ran while one was open for 8% of the time, Pallas kernels for 0%

commit v1 on v0

--- a/solution.py
+++ b/solution.py
@@ -1,11 +1,21 @@
+import functools
 import math
 
 import jax
 import jax.numpy as jnp
 from jax import lax
+from jax.experimental import pallas as pl
+from jax.experimental.pallas import tpu as pltpu
 from jax.sharding import PartitionSpec as P
 
 HEADS = 16
+MESH = pl.DeviceIdType.MESH
+F32, BF16 = jnp.float32, jnp.bfloat16
+WX = 384
+WZ = 256
+WR = 2 * WX + WZ
+ROWS = 16
+SLOTS = 8
 
 
 def norm_rows(values_in, gain_vec, bias_vec):
@@ -29,6 +39,784 @@
     return lax.dot_general(
         left, right, (((1,), (1,)), ((), ())), preferred_element_type=jnp.float32
     )
+
+
+def dot32(left, right):
+    return jnp.dot(left, right, preferred_element_type=F32)
+
+
+def dot_nt(left, right):
+    return lax.dot_general(left, right, (((1,), (1,)), ((), ())), preferred_element_type=F32)
+
+
+def dot_tn(left, right):
+    return lax.dot_general(left, right, (((0,), (0,)), ((), ())), preferred_element_type=F32)
+
+
+def norm_in(rows, gain, bias):
+    mean = jnp.mean(rows, axis=-1, keepdims=True)
+    centered = rows - mean
+    variance = jnp.mean(centered * centered, axis=-1, keepdims=True)
+    return centered * lax.rsqrt(variance + 1e-05) * gain + bias
+
+
+def sequence_starts(lens, spots):
+    start = jnp.zeros_like(spots)
+    end = jnp.int32(0)
+    for j in range(lens.shape[1]):
+        end = end + lens[0, j]
+        start = jnp.where(spots >= end, jnp.maximum(start, end), start)
+    return start
+
+
+def attend_kernel(lens, tok, gain, bias, w_hbm, qv_bias, low_in, qw, kw, vw, att, lse,
+                  w, tok_y, low_y, mask, acc, w_sem, sends, recvs):
+    dp, blk = lax.axis_index("dp"), lax.axis_index("blk")
+    y, c = blk // 2, blk % 2
+    core_dev, y_dev = (dp, blk + 1 - 2 * c), (dp, blk + 2 - 4 * y)
+    rows, width = tok.shape
+    dim = width // HEADS
+    half = rows // 2
+
+    def remote(src, dst, i, dev):
+        return pltpu.make_async_remote_copy(src, dst, sends.at[i], recvs.at[i], device_id=dev, device_id_type=MESH)
+
+    n_w = 6
+    wc = 3 * width // n_w
+    loads = [pltpu.make_async_copy(w_hbm.at[:, pl.ds(i * wc, wc)], w.at[:, pl.ds(i * wc, wc)], w_sem.at[i]) for i in range(n_w)]
+    for cp in loads:
+        cp.start()
+    bar = pltpu.get_barrier_semaphore()
+    for dev in (core_dev, y_dev):
+        pl.semaphore_signal(bar, inc=1, device_id=dev, device_id_type=MESH)
+    pl.semaphore_wait(bar, 2)
+    cross = [remote(tok.at[pl.ds(i * half, half)], tok_y.at[pl.ds(i * half, half)], i, y_dev) for i in range(2)]
+    for cp in cross:
+        cp.start()
+
+    q_spots = blk * rows + lax.broadcasted_iota(jnp.int32, (1, rows), 1)
+    starts = sequence_starts(lens, q_spots)
+    k_spots = (blk - 2) * rows + lax.broadcasted_iota(jnp.int32, (3 * rows, 1), 0)
+    mask[...] = jnp.where((k_spots >= starts) & (k_spots <= q_spots), 0.0, -1e30)
+
+    low_in[...] = norm_in(tok[...].astype(F32), gain[...], bias[...]).astype(BF16)
+
+    def project(src, r0, n, part):
+        res = dot32(src[r0:r0 + n], w[:, part * width:(part + 1) * width])
+        if part == 0:
+            res = (res + qv_bias[:, 0:width]).astype(BF16).astype(F32) * (dim ** -0.5)
+        if part == 2:
+            res = res + qv_bias[:, width:]
+        return res.astype(BF16)
+
+    own_q = remote(qw.at[0], qw.at[1], 2, core_dev)
+    own_k = remote(kw.at[2], kw.at[1], 3, core_dev)
+    own_v = remote(vw.at[2], vw.at[1], 4, core_dev)
+    relay_q = remote(qw.at[2], qw.at[1], 5, core_dev)
+    relay_k = remote(kw.at[0], kw.at[1], 6, core_dev)
+    relay_v = remote(vw.at[0], vw.at[1], 7, core_dev)
+
+    for cp in loads[2:4]:
+        cp.wait()
+    kw[2] = project(low_in, 0, rows, 1)
+
+    @pl.when(c == 0)
+    def _():
+        own_k.start()
+
+    for cp in loads[4:6]:
+        cp.wait()
+    vw[2] = project(low_in, 0, rows, 2)
+
+    @pl.when(c == 0)
+    def _():
+        own_v.start()
+
+    for cp in loads[0:2]:
+        cp.wait()
+    qw[0] = project(low_in, 0, rows, 0)
+
+    @pl.when(c == 1)
+    def _():
+        own_q.start()
+
+    for i in range(2):
+        cross[i].wait_recv()
+        low_y[i * half:(i + 1) * half] = norm_in(tok_y[i * half:(i + 1) * half].astype(F32), gain[...], bias[...]).astype(BF16)
+
+        @pl.when(y == 1)
+        def _():
+            kw[0, i * half:(i + 1) * half] = project(low_y, i * half, half, 1)
+            vw[0, i * half:(i + 1) * half] = project(low_y, i * half, half, 2)
+
+        @pl.when(y == 0)
+        def _():
+            qw[2, i * half:(i + 1) * half] = project(low_y, i * half, half, 0)
+
+    @pl.when((y == 1) & (c == 1))
+    def _():
+        relay_k.start()
+        relay_v.start()
+
+    @pl.when((y == 0) & (c == 0))
+    def _():
+        relay_q.start()
+
+    @pl.when(c == 1)
+    def _():
+        own_k.wait_recv()
+        own_v.wait_recv()
+
+    @pl.when((y == 1) & (c == 0))
+    def _():
+        relay_k.wait_recv()
+        relay_v.wait_recv()
+
+    def heads(first):
+        def pair(i, carry):
+            cols = pl.ds(pl.multiple_of(i * 2 * dim, 2 * dim), 2 * dim)
+            q2 = qw[0, :, cols]
+            k2 = [kw[j, :, cols] for j in range(first, 3)]
+            v2 = [vw[j, :, cols] for j in range(first, 3)]
+            for sub in range(2):
+                part = slice(sub * dim, (sub + 1) * dim)
+                scores = [dot_nt(k[:, part], q2[:, part]) + mask[(first + n) * rows:(first + n + 1) * rows]
+                          for n, k in enumerate(k2)]
+                top = jnp.max(scores[0], axis=0, keepdims=True)
+                for s in scores[1:]:
+                    top = jnp.maximum(top, jnp.max(s, axis=0, keepdims=True))
+                total, out = None, None
+                for s, v in zip(scores, v2):
+                    p = jnp.exp(s - top)
+                    one = jnp.sum(p, axis=0, keepdims=True)
+                    term = dot_tn(v[:, part], p.astype(BF16))
+                    total = one if total is None else total + one
+                    out = term if out is None else out + term
+                acc[part] = out / total
+                lse[pl.ds(2 * i + sub, 1)] = top + jnp.log(total)
+            att[:, cols] = acc[...].T
+            return carry
+
+        lax.fori_loop(0, HEADS // 2, pair, 0)
+
+    @pl.when(blk == 0)
+    def _():
+        heads(2)
+
+    @pl.when(blk == 1)
+    def _():
+        heads(1)
+
+    @pl.when(blk >= 2)
+    def _():
+        heads(0)
+
+    for cp in cross:
+        cp.wait_send()
+
+    @pl.when(c == 0)
+    def _():
+        own_k.wait_send()
+        own_v.wait_send()
+        own_q.wait_recv()
+
+    @pl.when(c == 1)
+    def _():
+        own_q.wait_send()
+
+    @pl.when((y == 1) & (c == 1))
+    def _():
+        relay_k.wait_send()
+        relay_v.wait_send()
+
+    @pl.when((y == 0) & (c == 0))
+    def _():
+        relay_q.wait_send()
+
+    @pl.when((y == 0) & (c == 1))
+    def _():
+        relay_q.wait_recv()
+
+
+def attend(lengths, tokens, gain, bias, w_qkv, qv_bias):
+    rows, width = tokens.shape
+    vmem, hbm = pl.BlockSpec(memory_space=pltpu.VMEM), pl.BlockSpec(memory_space=pl.ANY)
+    window = jax.ShapeDtypeStruct((3, rows, width), BF16)
+    return pl.pallas_call(
+        attend_kernel,
+        out_shape=[jax.ShapeDtypeStruct((rows, width), BF16), window, window, window,
+                   jax.ShapeDtypeStruct((rows, width), F32), jax.ShapeDtypeStruct((HEADS, rows), F32)],
+        in_specs=[pl.BlockSpec(memory_space=pltpu.SMEM), vmem, vmem, vmem, hbm, vmem],
+        out_specs=[vmem] * 6,
+        scratch_shapes=[pltpu.VMEM((width, 3 * width), BF16), pltpu.VMEM((rows, width), BF16), pltpu.VMEM((rows, width), BF16),
+                        pltpu.VMEM((3 * rows, rows), F32), pltpu.VMEM((2 * width // HEADS, rows), F32),
+                        pltpu.SemaphoreType.DMA((6,)), pltpu.SemaphoreType.DMA((8,)), pltpu.SemaphoreType.DMA((8,))],
+        compiler_params=pltpu.CompilerParams(collective_id=1, has_side_effects=True, vmem_limit_bytes=56 << 20),
+        cost_estimate=pl.CostEstimate(flops=8 << 30, bytes_accessed=12 << 20, transcendentals=3 << 20),
+    )(lengths, tokens, gain[None], bias[None], w_qkv, qv_bias[None])
+
+
+RECV = 12
+PAIR0 = 4
+
+
+def back_kernel(tok, a2, a1, ao, aq, b2, b1, bo, lens, qw, kw, vw, d_att, stats, w_hbm, tokens, gain, d_first, vec_in,
+                out, vout, grad_tok,
+                am, ap, bm, bp, s1x, s1y, s2x, s2y, sr, sl, szr, szl, szx, szy, swx, swy,
+                r1x, r1y, r2x, r2y, rr, rl, rzr, rzl, rzx, rzy, rwx, rwy,
+                k2x, k2y, t3, kzx, kzy, kwx, kwy, vec, vown, vrecv,
+                w, dow, stw, mask, mask_q, dqa, dka, dva, d_in,
+                load_sem, peer_send, peer_recv, send, recv, vsend, vrecv_sem, w_sem, asend, arecv):
+    dp, blk = lax.axis_index("dp"), lax.axis_index("blk")
+    z, x = dp // 2, dp % 2
+    y, c = blk // 2, blk % 2
+    core_dev, x_dev, y_dev = (dp, blk + 1 - 2 * c), (dp + 1 - 2 * x, blk), (dp, blk + 2 - 4 * y)
+    up_dev, down_dev = (dp + 2, blk), (dp - 2, blk)
+    rounds = 24
+    rows, width = tokens.shape
+    dim = width // HEADS
+
+    w_load = pltpu.make_async_copy(w_hbm, w, w_sem.at[0])
+
+    bar = pltpu.get_barrier_semaphore()
+    z_devs = [((dp + 2 * k) % 8, blk) for k in range(1, 4)]
+    for dev in [core_dev, x_dev, y_dev] + z_devs:
+        pl.semaphore_signal(bar, inc=1, device_id=dev, device_id_type=MESH)
+    pl.semaphore_wait(bar, 6)
+
+    def remote(src, dst, ssem, rsem, dev):
+        return pltpu.make_async_remote_copy(src, dst, ssem, rsem, device_id=dev, device_id_type=MESH)
+
+    def window(kind):
+        src, dst, dev = {"cross": (0, 2, y_dev), "own": (0, 1, core_dev), "relay": (2, 1, core_dev)}[kind]
+        k = {"cross": 0, "own": 2, "relay": 4}[kind]
+        return [remote(d_att if src == 0 else dow.at[src], dow.at[dst], asend.at[k], arecv.at[k], dev),
+                remote(stats if src == 0 else stw.at[src], stw.at[dst], asend.at[k + 1], arecv.at[k + 1], dev)]
+
+    @pl.when(y == 1)
+    def _():
+        for cp in window("cross"):
+            cp.start()
+
+    @pl.when(c == 1)
+    def _():
+        for cp in window("own"):
+            cp.start()
+
+    a_src = [(a2, g) for g in range(8)] + [(a1, 0), (a1, 1), (ao, 0), (ao, 1), (aq, 0), (aq, 1)]
+    b_src = [(b2, 0)] + [(b1, i) for i in range(4)] + [(bo, 0)]
+    n_a = len(a_src)
+
+    def loads(kind, i, own):
+        k = i if kind == "a" else n_a + i
+        if kind == "a":
+            ref, g = a_src[i]
+            if own:
+                return pltpu.make_async_copy(ref.at[:, :, :, c, g], am.at[i], load_sem.at[k])
+            return remote(ref.at[:, :, :, 1 - c, g], ap.at[i], peer_send.at[k], peer_recv.at[k], core_dev)
+        ref, g = b_src[i]
+        part = ref.at[:, pl.ds(g * WR, WR)]
+        if own:
+            return pltpu.make_async_copy(part, bm.at[i], load_sem.at[k])
+        return remote(part, bp.at[i], peer_send.at[k], peer_recv.at[k], core_dev)
+
+    phases = [([("b", 0)] + [("a", g) for g in range(8)]),
+              ([("a", 8), ("a", 9)] + [("b", i) for i in range(1, 5)]),
+              ([("a", 10), ("a", 11), ("b", 5), ("a", 12), ("a", 13)])]
+    for phase in phases:
+        for item in phase:
+            loads(*item, True).start()
+            loads(*item, False).start()
+    w_load.start()
+
+    def peer_b(i):
+        k = n_a + i
+        return remote(bm.at[i], bp.at[i], peer_send.at[k], peer_recv.at[k], core_dev)
+
+    def arrive(phase):
+        for item in phase:
+            loads(*item, True).wait()
+            loads(*item, False).wait_recv()
+
+    vec[...] = vec_in[...]
+    q_spots = blk * rows + lax.broadcasted_iota(jnp.int32, (1, rows), 1)
+    k_spots = (blk - 2) * rows + lax.broadcasted_iota(jnp.int32, (3 * rows, 1), 0)
+    mask[...] = jnp.where((k_spots >= sequence_starts(lens, q_spots)) & (k_spots <= q_spots), 0.0, -1e30)
+    q_spots = (blk + 1) * rows + lax.broadcasted_iota(jnp.int32, (1, 2 * rows), 1)
+    k_spots = blk * rows + lax.broadcasted_iota(jnp.int32, (rows, 1), 0)
+    mask_q[...] = jnp.where(k_spots >= sequence_starts(lens, q_spots), 0.0, -1e30)
+
+    def place(r):
+        g = jnp.where(r < 8, r, jnp.where(r < 16, 8 + r % 2, jnp.where(r < 18, 10 + r % 2, 12 + r % 2)))
+        b = jnp.where(r < 8, 0, (r - 8) // 2 + 1)
+        return g, b
+
+    def product(r, zs, xs, ys, col, width):
+        g, b = place(r)
+        cols = pl.ds(col, width)
+        la, lp = am[g, zs, xs, ys], ap[g, zs, xs, ys]
+        lead = la.shape[:-1]
+        m = 1
+        for d in lead:
+            m *= d
+        res = dot32(la.reshape(m, tok), bm[b, :, cols]) + dot32(lp.reshape(m, tok), bp[b, :, cols])
+        return res.reshape(lead + (width,))
+
+    ALL = slice(None)
+    col_y, col_z = WX, 2 * WX
+    S1X, S1Y, S2X, S2Y, SR, SL, SZR, SZL, SZX, SZY, SWX, SWY = range(12)
+
+    def message(src, dst, kind, dev):
+        def make(r):
+            return remote(src.at[r % SLOTS], dst.at[r % RECV], send.at[kind, r % SLOTS], recv.at[kind, r % RECV], dev)
+        return make
+
+    step1x, step1y = message(s1x, r1x, S1X, x_dev), message(s1y, r1y, S1Y, y_dev)
+    step2x, step2y = message(s2x, r2x, S2X, y_dev), message(s2y, r2y, S2Y, x_dev)
+    stepzx, stepzy = message(szx, rzx, SZX, x_dev), message(szy, rzy, SZY, y_dev)
+    stepwx, stepwy = message(swx, rwx, SWX, y_dev), message(swy, rwy, SWY, x_dev)
+
+    def chain(src, dst, kind, r, lo, hi, dev):
+        return remote(src.at[r % SLOTS, lo:hi], dst.at[r % RECV, lo:hi], send.at[kind, r % SLOTS], recv.at[kind, r % RECV], dev)
+
+    def chain_hop(hop, r, src, dst, kind_r, kind_l, term):
+        slot, rslot = r % SLOTS, r % RECV
+
+        @pl.when(z == hop)
+        def _():
+            if hop > 0:
+                chain(src[0], dst[0], kind_r, r, hop - 1, 3, up_dev).wait_recv()
+            for d in range(hop + 1, 4):
+                value = term(r, d)
+                if hop > 0:
+                    value = value + dst[0][rslot, d - 1].astype(F32)
+                src[0][slot, d - 1] = value.astype(BF16)
+            chain(src[0], dst[0], kind_r, r, hop, 3, up_dev).start()
+
+        @pl.when(z == 3 - hop)
+        def _():
+            if hop > 0:
+                chain(src[1], dst[1], kind_l, r, 0, 4 - hop, down_dev).wait_recv()
+            for d in range(0, 3 - hop):
+                value = term(r, d)
+                if hop > 0:
+                    value = value + dst[1][rslot, d].astype(F32)
+                src[1][slot, d] = value.astype(BF16)
+            chain(src[1], dst[1], kind_l, r, 0, 3 - hop, down_dev).start()
+
+    def chain_last(r, src, dst, kind_r, kind_l, total_ref):
+        rslot = r % RECV
+        for at in range(4):
+            @pl.when(z == at)
+            def _():
+                if at == 3:
+                    chain(src[0], dst[0], kind_r, r, 2, 3, up_dev).wait_recv()
+                if at == 0:
+                    chain(src[1], dst[1], kind_l, r, 0, 1, down_dev).wait_recv()
+                value = None
+                if at > 0:
+                    value = dst[0][rslot, at - 1].astype(F32)
+                if at < 3:
+                    down = dst[1][rslot, at].astype(F32)
+                    value = down if value is None else value + down
+                total_ref[...] = value
+
+    def chain_drain(r, src, dst, kind_r, kind_l):
+        for hop in range(3):
+            @pl.when(z == hop)
+            def _():
+                chain(src[0], dst[0], kind_r, r, hop, 3, up_dev).wait_send()
+
+            @pl.when(z == 3 - hop)
+            def _():
+                chain(src[1], dst[1], kind_l, r, 0, 3 - hop, down_dev).wait_send()
+
+    def z_term(r, d):
+        return product(r, d, ALL, ALL, col_z, WZ)
+
+    def t_term(r, d):
+        return t3[r % SLOTS, d]
+
+    zsrc, zdst = (szr, szl), (rzr, rzl)
+    csrc, cdst = (sr, sl), (rr, rl)
+
+    def p0(r):
+        s1x[r % SLOTS] = product(r, ALL, 1 - x, ALL, 0, WX).astype(BF16)
+        step1x(r).start()
+        s1y[r % SLOTS] = product(r, ALL, ALL, 1 - y, col_y, WX).astype(BF16)
+        step1y(r).start()
+        chain_hop(0, r, zsrc, zdst, SZR, SZL, z_term)
+
+    def p1(r):
+        slot = r % SLOTS
+        step1x(r).wait_recv()
+        k2x[...] = product(r, ALL, x, ALL, 0, WX) + r1x[r % RECV].astype(F32)
+        s2x[slot] = k2x[:, 1 - y].astype(BF16)
+        step2x(r).start()
+        kwx[slot] = k2x[:, y]
+        step1y(r).wait_recv()
+        k2y[...] = product(r, ALL, ALL, y, col_y, WX) + r1y[r % RECV].astype(F32)
+        s2y[slot] = k2y[:, 1 - x].astype(BF16)
+        step2y(r).start()
+        kwy[slot] = k2y[:, x]
+        chain_hop(1, r, zsrc, zdst, SZR, SZL, z_term)
+
+    def p2(r):
+        slot = r % SLOTS
+        step2x(r).wait_recv()
+        t3[slot, :, :, 0:WX] = kwx[slot] + r2x[r % RECV].astype(F32)
+        step2y(r).wait_recv()
+        t3[slot, :, :, WX:2 * WX] = kwy[slot] + r2y[r % RECV].astype(F32)
+        chain_hop(0, r, csrc, cdst, SR, SL, t_term)
+        chain_hop(2, r, zsrc, zdst, SZR, SZL, z_term)
+
+    def p3(r):
+        slot = r % SLOTS
+        chain_hop(1, r, csrc, cdst, SR, SL, t_term)
+        chain_last(r, zsrc, zdst, SZR, SZL, kzx)
+        kzx[...] = kzx[...] + product(r, z, ALL, ALL, col_z, WZ)
+        szx[slot] = kzx[1 - x, :, :, 0:WZ // 2].astype(BF16)
+        stepzx(r).start()
+        szy[slot] = kzx[:, 1 - y, :, WZ // 2:WZ].astype(BF16)
+        stepzy(r).start()
+        kzy[slot, 0] = kzx[x, :, :, 0:WZ // 2]
+        kzy[slot, 1] = kzx[:, y, :, WZ // 2:WZ]
+
+    def p4(r):
+        slot = r % SLOTS
+        chain_hop(2, r, csrc, cdst, SR, SL, t_term)
+        stepzx(r).wait_recv()
+        kzy[slot, 0] = kzy[slot, 0] + rzx[r % RECV].astype(F32)
+        swx[slot] = kzy[slot, 0, 1 - y].astype(BF16)
+        stepwx(r).start()
+        stepzy(r).wait_recv()
+        kzy[slot, 1] = kzy[slot, 1] + rzy[r % RECV].astype(F32)
+        swy[slot] = kzy[slot, 1, 1 - x].astype(BF16)
+        stepwy(r).start()
+
+    def p5(r):
+        slot = r % SLOTS
+        chain_last(r, csrc, cdst, SR, SL, out.at[r, :, 0:2 * WX])
+        out[r, :, 0:2 * WX] = out[r, :, 0:2 * WX] + t3[slot, z]
+        stepwx(r).wait_recv()
+        out[r, :, 2 * WX:2 * WX + WZ // 2] = kzy[slot, 0, y] + rwx[r % RECV].astype(F32)
+        stepwy(r).wait_recv()
+        out[r, :, 2 * WX + WZ // 2:] = kzy[slot, 1, x] + rwy[r % RECV].astype(F32)
+
+    def drain(r):
+        for step in (step1x, step1y, step2x, step2y, stepzx, stepzy, stepwx, stepwy):
+            step(r).wait_send()
+        chain_drain(r, csrc, cdst, SR, SL)
+        chain_drain(r, zsrc, zdst, SZR, SZL)
+
+    v = vec.shape[0]
+    h1, h2, h3 = v // 2, v // 4, v // 8
+    o1 = c * h1
+    o2 = o1 + x * h2
+    o3 = o2 + y * h3
+    base = h1 + h2 + h3
+
+    def vstep(i):
+        if i == 0:
+            return [remote(vec.at[pl.ds((1 - c) * h1, h1)], vrecv.at[pl.ds(0, h1)], vsend.at[0], vrecv_sem.at[0], core_dev)]
+        if i == 1:
+            return [remote(vown.at[pl.ds(o1 + (1 - x) * h2, h2)], vrecv.at[pl.ds(h1, h2)], vsend.at[1], vrecv_sem.at[1], x_dev)]
+        if i == 2:
+            return [remote(vown.at[pl.ds(o2 + (1 - y) * h3, h3)], vrecv.at[pl.ds(h1 + h2, h3)], vsend.at[2], vrecv_sem.at[2], y_dev)]
+        if i == 3:
+            return [remote(vown.at[pl.ds(o3, h3)], vrecv.at[pl.ds(base + z * h3, h3)], vsend.at[3 + k], vrecv_sem.at[3 + k],
+                           z_devs[k - 1]) for k in range(1, 4)]
+        if i == 4:
+            return [remote(vout.at[pl.ds(o3, h3)], vout.at[pl.ds(o3, h3)], vsend.at[7], vrecv_sem.at[7], y_dev)]
+        if i == 5:
+            return [remote(vout.at[pl.ds(o2, h2)], vout.at[pl.ds(o2, h2)], vsend.at[8], vrecv_sem.at[8], x_dev)]
+        return [remote(vout.at[pl.ds(o1, h1)], vout.at[pl.ds(o1, h1)], vsend.at[9], vrecv_sem.at[9], core_dev)]
+
+    def vector_step(i):
+        if i > 0:
+            for cp in vstep(i - 1):
+                cp.wait_recv()
+        if i == 1:
+            vown[pl.ds(o1, h1)] = vec[pl.ds(o1, h1)] + vrecv[0:h1]
+        if i == 2:
+            vown[pl.ds(o2, h2)] = vown[pl.ds(o2, h2)] + vrecv[h1:h1 + h2]
+        if i == 3:
+            vown[pl.ds(o3, h3)] = vown[pl.ds(o3, h3)] + vrecv[h1 + h2:base]
+            vrecv[pl.ds(base + z * h3, h3)] = vown[pl.ds(o3, h3)]
+        if i == 4:
+            total = vrecv[base:base + h3]
+            for k in range(1, 4):
+                total = total + vrecv[base + k * h3:base + (k + 1) * h3]
+            vout[pl.ds(o3, h3)] = total
+        if i < 7:
+            for cp in vstep(i):
+                cp.start()
+
+    def windows_arrive():
+        dow[0] = d_att[...]
+        stw[0] = stats[...]
+
+        @pl.when(y == 0)
+        def _():
+            for cp in window("cross"):
+                cp.wait_recv()
+
+        @pl.when((y == 0) & (c == 0))
+        def _():
+            for cp in window("relay"):
+                cp.start()
+
+        @pl.when(c == 0)
+        def _():
+            for cp in window("own"):
+                cp.wait_recv()
+
+        @pl.when((y == 0) & (c == 1))
+        def _():
+            for cp in window("relay"):
+                cp.wait_recv()
+
+    def windows_drain():
+        @pl.when(y == 1)
+        def _():
+            for cp in window("cross"):
+                cp.wait_send()
+
+        @pl.when(c == 1)
+        def _():
+            for cp in window("own"):
+                cp.wait_send()
+
+        @pl.when((y == 0) & (c == 0))
+        def _():
+            for cp in window("relay"):
+                cp.wait_send()
+
+    def attend_back(i):
+        cols = pl.ds(pl.multiple_of(i * 2 * dim, 2 * dim), 2 * dim)
+
+        def pairs(kj, qj, bias, to_q, to_k, first):
+            k2, v2, q2, d2 = kw[kj, :, cols], vw[kj, :, cols], qw[qj, :, cols], dow[qj, :, cols]
+            for sub in range(2):
+                part = slice(sub * dim, (sub + 1) * dim)
+                k1, v1, q1, d1 = k2[:, part], v2[:, part], q2[:, part], d2[:, part]
+                log_total = stw[qj, pl.ds(2 * i + sub, 1)]
+                delta = stw[qj, pl.ds(HEADS + 2 * i + sub, 1)]
+                probs = jnp.exp(dot_nt(k1, q1) + bias[...] - log_total)
+                low_s = (probs * (dot_nt(v1, d1) - delta)).astype(BF16)
+                if to_q:
+                    term = dot_tn(k1, low_s)
+                    dqa[part] = term if first else dqa[part] + term
+                if to_k:
+                    term = dot32(low_s, q1)
+                    dka[sub] = term if first else dka[sub] + term
+                    term = dot32(probs.astype(BF16), d1)
+                    dva[sub] = term if first else dva[sub] + term
+
+        pairs(2, 0, mask.at[2 * rows:3 * rows], True, True, True)
+
+        @pl.when(blk >= 1)
+        def _():
+            pairs(1, 0, mask.at[rows:2 * rows], True, False, False)
+
+        @pl.when(blk >= 2)
+        def _():
+            pairs(0, 0, mask.at[0:rows], True, False, False)
+
+        @pl.when(blk <= 2)
+        def _():
+            pairs(2, 1, mask_q.at[:, 0:rows], False, True, False)
+
+        @pl.when(blk <= 1)
+        def _():
+            pairs(2, 2, mask_q.at[:, rows:2 * rows], False, True, False)
+
+        bm[6, :, cols] = (dqa[...].T * (dim ** -0.5)).astype(BF16)
+        bm[7, :, cols] = jnp.concatenate([dka[0], dka[1]], axis=1).astype(BF16)
+        bm[8, :, cols] = jnp.concatenate([dva[0], dva[1]], axis=1).astype(BF16)
+
+    def put_row(first, row):
+        for k in range(row.shape[1] // 128):
+            vec[first + k:first + k + 1, :] = row[:, k * 128:(k + 1) * 128]
+
+    def input_back():
+        for i in range(6, 9):
+            peer_b(i).start()
+        w_load.wait()
+        d_in[...] = dot_nt(bm[6], w[:, 0:width])
+        d_in[...] = d_in[...] + dot_nt(bm[7], w[:, width:2 * width])
+        grad = d_in[...] + dot_nt(bm[8], w[:, 2 * width:])
+        rows_in = tokens[...].astype(F32)
+        centered = rows_in - jnp.mean(rows_in, axis=-1, keepdims=True)
+        scale = lax.rsqrt(jnp.mean(centered * centered, axis=-1, keepdims=True) + 1e-05)
+        normed = centered * scale
+        put_row(0, jnp.sum(grad * normed, axis=0, keepdims=True))
+        put_row(width // 128, jnp.sum(grad, axis=0, keepdims=True))
+        put_row(2 * width // 128, jnp.sum(bm[6].astype(F32), axis=0, keepdims=True))
+        put_row(3 * width // 128, jnp.sum(bm[8].astype(F32), axis=0, keepdims=True))
+        grad = grad * gain[...]
+        grad = grad - jnp.mean(grad, axis=-1, keepdims=True) - normed * jnp.mean(grad * normed, axis=-1, keepdims=True)
+        grad_tok[...] = d_first[...] + scale * grad
+
+    phase_list = (p0, p1, p2, p3, p4, p5)
+    lags = (0, 2, 4, 5, 6, 7)
+    n_pairs = HEADS // 2
+    after = PAIR0 + n_pairs
+
+    def slot_step(s, carry):
+        for k in (5, 4, 3, 2, 1):
+            r = s - lags[k]
+
+            @pl.when((r >= 0) & (r < rounds))
+            def _():
+                phase_list[k](r)
+
+        for at, phase in ((0, 0), (7, 1), (15, 2)):
+            @pl.when(s == at)
+            def _():
+                arrive(phases[phase])
+
+        @pl.when(s == 17)
+        def _():
+            for i in range(6, 9):
+                peer_b(i).wait_recv()
+
+        @pl.when((s >= SLOTS) & (s < rounds))
+        def _():
+            drain(s - SLOTS)
+
+        @pl.when(s < rounds)
+        def _():
+            p0(s)
+
+        @pl.when(s == PAIR0)
+        def _():
+            windows_arrive()
+
+        @pl.when((s >= PAIR0) & (s < after))
+        def _():
+            attend_back(s - PAIR0)
+
+        @pl.when(s == after)
+        def _():
+            input_back()
+
+        for i in range(8):
+            @pl.when(s == after + i)
+            def _():
+                vector_step(i)
+
+        return carry
+
+    lax.fori_loop(0, rounds + lags[5], slot_step, 0)
+    lax.fori_loop(rounds - SLOTS, rounds, lambda r, carry: (drain(r), carry)[1], 0)
+    windows_drain()
+    for phase in phases:
+        for item in phase:
+            loads(*item, False).wait_send()
+    for i in range(6, 9):
+        peer_b(i).wait_send()
+    for i in range(7):
+        for cp in vstep(i):
+            cp.wait_send()
+
+
+def rows_first(act, rows_block):
+    tok = act.shape[0]
+    return act.T.reshape(4, 2, 2, 2, rows_block // ROWS, ROWS, tok)
+
+
+def backward(low_ffn, cot, low_mid, low_pre, scaled, low_attn, low_in, lengths, q_win, k_win, v_win, d_att, stats,
+             w_qkv, tokens, gain, d_first, vec):
+    tok, width = tokens.shape
+    rounds = 24
+    hbm, vmem = pl.BlockSpec(memory_space=pl.ANY), pl.BlockSpec(memory_space=pltpu.VMEM)
+    a_shape = (14, 4, 2, 2, ROWS, tok)
+    b_shape = (9, tok, WR)
+    msgs = [(4, 2, ROWS, WX), (4, 2, ROWS, WX), (4, ROWS, WX), (4, ROWS, WX), (3, ROWS, 2 * WX), (3, ROWS, 2 * WX),
+            (3, 2, 2, ROWS, WZ), (3, 2, 2, ROWS, WZ), (2, ROWS, WZ // 2), (2, ROWS, WZ // 2), (ROWS, WZ // 2), (ROWS, WZ // 2)]
+    v = vec.shape[0]
+    dma = pltpu.SemaphoreType.DMA
+    return pl.pallas_call(
+        functools.partial(back_kernel, tok),
+        out_shape=[jax.ShapeDtypeStruct((rounds, ROWS, WR), F32), jax.ShapeDtypeStruct(vec.shape, F32),
+                   jax.ShapeDtypeStruct(tokens.shape, F32)],
+        in_specs=[hbm] * 7 + [pl.BlockSpec(memory_space=pltpu.SMEM)] + [vmem] * 5 + [hbm] + [vmem] * 4,
+        out_specs=[vmem] * 3,
+        scratch_shapes=[pltpu.VMEM(a_shape, BF16), pltpu.VMEM(a_shape, BF16), pltpu.VMEM(b_shape, BF16), pltpu.VMEM(b_shape, BF16)]
+        + [pltpu.VMEM((SLOTS,) + m, BF16) for m in msgs]
+        + [pltpu.VMEM((RECV,) + m, BF16) for m in msgs]
+        + [pltpu.VMEM((4, 2, ROWS, WX), F32), pltpu.VMEM((4, 2, ROWS, WX), F32), pltpu.VMEM((SLOTS, 4, ROWS, 2 * WX), F32),
+           pltpu.VMEM((2, 2, ROWS, WZ), F32), pltpu.VMEM((SLOTS, 2, 2, ROWS, WZ // 2), F32),
+           pltpu.VMEM((SLOTS, 4, ROWS, WX), F32), pltpu.VMEM((SLOTS, 4, ROWS, WX), F32),
+           pltpu.VMEM((v, 128), F32), pltpu.VMEM((v, 128), F32), pltpu.VMEM((v // 2 + v // 4 + v // 8 * 5, 128), F32),
+           pltpu.VMEM((width, 3 * width), BF16), pltpu.VMEM((3, tok, width), BF16), pltpu.VMEM((3, 2 * HEADS, tok), F32),
+           pltpu.VMEM((3 * tok, tok), F32), pltpu.VMEM((tok, 2 * tok), F32),
+           pltpu.VMEM((2 * width // HEADS, tok), F32), pltpu.VMEM((2, tok, width // HEADS), F32),
+           pltpu.VMEM((2, tok, width // HEADS), F32), pltpu.VMEM((tok, width), F32),
+           dma((20,)), dma((23,)), dma((23,)), dma((12, SLOTS)), dma((12, RECV)), dma((10,)), dma((10,)), dma((1,)), dma((6,)), dma((6,))],
+        compiler_params=pltpu.CompilerParams(collective_id=0, has_side_effects=True, vmem_limit_bytes=62 << 20),
+        cost_estimate=pl.CostEstimate(flops=20 << 30, bytes_accessed=30 << 20, transcendentals=4 << 20),
+    )(rows_first(low_ffn, 128), rows_first(low_mid, 32), rows_first(scaled, 32), rows_first(low_in, 32),
+      cot, low_pre, low_attn, lengths, q_win, k_win, v_win, d_att, stats, w_qkv, tokens, gain[None], d_first, vec)
+
+
+def fast_shards(
+    tokens, lengths, ln1_gain, ln1_bias, w_qkv, qv_bias, head_scale, w_out, out_bias, lnpa_gain, lnpa_bias,
+    ln2_gain, ln2_bias, w_fc1, fc1_bias, lnf_gain, lnf_bias, w_fc2, fc2_bias, cotangent,
+):
+    row_count, width = tokens.shape
+    head_dim = width // HEADS
+    inputs = tokens.astype(F32)
+    low_in, q_win, k_win, v_win, attended, log_total = attend(lengths, tokens, ln1_gain, ln1_bias, w_qkv, qv_bias)
+    head_gain = jnp.repeat(head_scale, head_dim)
+    scaled = (attended * head_gain).astype(BF16)
+    attn_out = dot32(scaled, w_out) + out_bias
+    branch, pa_back = jax.vjp(norm_rows, attn_out, lnpa_gain, lnpa_bias)
+    first_sum = inputs + branch
+    normed_mid, ln2_back = jax.vjp(norm_rows, first_sum, ln2_gain, ln2_bias)
+    low_mid = normed_mid.astype(BF16)
+    pre_act = dot32(low_mid, w_fc1) + fc1_bias
+    activated, gelu_back = jax.vjp(gelu_exact, pre_act)
+    ffn_normed, lnf_back = jax.vjp(norm_rows, activated, lnf_gain, lnf_bias)
+    low_ffn = ffn_normed.astype(BF16)
+    layer_out = (first_sum + dot32(low_ffn, w_fc2) + fc2_bias).astype(BF16)
+    d_output = cotangent.astype(F32)
+    grad_c2 = jnp.sum(d_output, axis=0)
+    d_ffn = over_cols(cotangent, w_fc2)
+    d_active, grad_lnf_gain, grad_lnf_bias = lnf_back(d_ffn)
+    (d_pre,) = gelu_back(d_active)
+    low_pre = d_pre.astype(BF16)
+    grad_c1 = jnp.sum(low_pre.astype(F32), axis=0)
+    d_mid = over_cols(low_pre, w_fc1)
+    d_first_norm, grad_ln2_gain, grad_ln2_bias = ln2_back(d_mid)
+    d_first = d_output + d_first_norm
+    d_attn, grad_pa_gain, grad_pa_bias = pa_back(d_first)
+    low_attn = d_attn.astype(BF16)
+    grad_bo = jnp.sum(low_attn.astype(F32), axis=0)
+    d_scaled = over_cols(low_attn, w_out)
+    grad_hs = jnp.sum((d_scaled * attended).reshape(row_count, HEADS, head_dim), axis=(0, 2))
+    d_attended = (d_scaled * head_gain).astype(BF16)
+    delta = jnp.sum((d_attended.astype(F32) * attended).reshape(row_count, HEADS, head_dim), axis=-1).T
+    stats = jnp.concatenate([log_total, delta], axis=0)
+    vectors = (grad_bo, grad_pa_gain, grad_pa_bias, grad_ln2_gain, grad_ln2_bias, grad_c1, grad_lnf_gain, grad_lnf_bias,
+               grad_c2, grad_hs)
+    flat = jnp.concatenate((jnp.zeros((4 * width,), F32),) + vectors)
+    flat = jnp.pad(flat, (0, 192 * 128 - flat.shape[0])).reshape(192, 128)
+    out, flat, grad_tokens = backward(
+        low_ffn, cotangent, low_mid, low_pre, scaled, low_attn, low_in, lengths, q_win, k_win, v_win, d_attended, stats,
+        w_qkv, tokens, ln1_gain, d_first, flat)
+    share_w2 = out[:8].reshape(128, WR)
+    share_w1 = out[8:16].reshape(4, 32, WR).transpose(1, 0, 2).reshape(32, 4 * WR)
+    share_wo = out[16:18].reshape(32, WR)
+    share_wqkv = out[18:24].reshape(3, 32, WR).transpose(1, 0, 2).reshape(32, 3 * WR)
+    flat = flat.reshape(-1)
+    sizes = (width, width, 2 * width) + tuple(item.shape[0] for item in vectors)
+    starts = [sum(sizes[:i]) for i in range(len(sizes))]
+    ln1g, ln1b, qv, bo, pag, pab, ln2g, ln2b, c1, lnfg, lnfb, c2, hs = (
+        lax.slice(flat, (start,), (start + size,)) for start, size in zip(starts, sizes))
+    return (layer_out, grad_tokens, ln1g, ln1b, share_wqkv, qv, hs, share_wo, bo, pag, pab, ln2g, ln2b, share_w1, c1,
+            lnfg, lnfb, share_w2, c2)
 
 
 def shards(
@@ -327,4 +1115,5 @@
         P(("dp", "blk"), None),
         P(),
     )
-    return jax.shard_map(shards, mesh=mesh, in_specs=in_specs, out_specs=out_specs, check_vma=False)
+    body = fast_shards if dict(mesh.shape) == {"dp": 8, "blk": 4} else shards
+    return jax.shard_map(body, mesh=mesh, in_specs=in_specs, out_specs=out_specs, check_vma=False)

time: 1060 us -> 234 us (0.22)
  waiting for transfers between devices: 852 us -> 0 us
  Pallas kernels: 0 us -> 168 us
  matrix products: 125 us -> 28.2 us
  local copies, waits for them, and re-layouts: 39.9 us -> 23.2 us
  between operations: 14.6 us -> 1.09 us
  other arithmetic: 25.1 us -> 12.6 us
    reduce_scatter x6 -> x0, waiting for transfers between devices: 713 us -> none  [the longest x1 188 us: shards(): lax.psum_scatter(grad_w2, ('dp', 'blk'), scatter_dimension=0, tiled=True)]
    pallas_call x0 -> x2, Pallas kernels: none -> 168 us  [the longest x1 142 us: backward(): pl.pallas_call(functools.partial(back_kernel, tok), out_shape=[jax.ShapeD...]
    psum x1 -> x0, waiting for transfers between devices: 107 us -> none  [shards(): lax.psum((grad_ln1_gain, grad_ln1_bias, grad_qv, grad_hs, grad_bo, grad_p...]
    dot_general x15 -> x3, matrix products: 103 us -> 12.1 us  [dot32(): return jnp.dot(left, right, preferred_element_type=F32)]
    all_gather x2 -> x0, waiting for transfers between devices: 31.5 us -> none  [the longest x1 21.6 us: shards(): lax.all_gather(key_rows, 'blk', axis=0, tiled=True)]
    unnamed x91 -> x58, local copies, waits for them, and re-layouts: 25.4 us -> 2.91 us
    dot_general x4 -> x3, matrix products: 22.5 us -> 16.1 us  [over_cols(): lax.dot_general(left, right, (((1,), (1,)), ((), ())), preferred_element_...]
  transfers between devices with their start and end apart: 9 -> 0, of which waited for: 9 -> 0; matrix products, arithmetic and copies ran while one was open for 8% -> 0% of each run, Pallas kernels for 0% -> 0%
where the time goes in v1:
time: 234 us; the launch traced here: 233 us
  Pallas kernels  168 us (72%)
  matrix products  28.2 us (12%)
  local copies, waits for them, and re-layouts  23.2 us (10%)
  other arithmetic  12.6 us (5%)
    pallas_call x1, Pallas kernels, backward(): pl.pallas_call(functools.partial(back_kernel, tok), out_shape=[jax.ShapeD...  142 us
    pallas_call x1, Pallas kernels, attend(): pl.pallas_call(attend_kernel, out_shape=[jax.ShapeDtypeStruct((rows, widt...  26.6 us
    dot_general x3, matrix products, over_cols(): lax.dot_general(left, right, (((1,), (1,)), ((), ())), preferred_element_...  16.1 us
    dot_general x3, matrix products, dot32(): return jnp.dot(left, right, preferred_element_type=F32)  12.1 us
    transpose x3, local copies, waits for them, and re-layouts, rows_first(): return act.T.reshape(4, 2, 2, 2, rows_block // ROWS, ROWS, tok)  6.12 us

profile of v1, /device:TPU:0, one launch (start us, length us, event | category | flops | bytes accessed | tf_op | source)
XLA Modules:
  0.0 233.5 jit_solution(15791914804072301727)
XLA Ops:
  0.7 26.6 %shard_map.339 = (bf16[256,1024]{1,0:T(8,128)(2,1)}, bf16[3,256,1024]{2,1,0:T(8,128)(2,1)}, bf16[3,256,1024]{2,1,0:T(8,128)(2,1)}, bf16[3,256,1024]{2,1,0:T(8,12...) custom-call(s32[1,5]{1,0:T(1,128)} %lens.3, bf16[256,1024]{1,0:T(8,128)(2,1)} %tokens.1, f32[1,1024]{1,0:T(1,128)} %bitcast.80, ...), custom_call_target="tpu_custom_call" | custom-call | flops 8589934592 | bytes 12582912 | tf_op jit(solution)/shard_map/pallas_call | solution.py:245
  27.5 2.2 fusion.14
  30.0 1.7 fusion.12
  32.0 3.2 %fusion.11 = (f32[256]{0:T(256)S(1)}, f32[256,4096]{1,0:T(8,128)S(1)}, f32[256,4096]{1,0:T(8,128)S(1)}) fusion(f32[4096]{0:T(1024)S(1)} %copy-done.21, bf16[1024,4096]{1,0:T(8,128)(2,1)S(1)} %copy-done.20, f32[256,1024]{1,0:T(8,128)S(1)} %get-tuple-element.62, f32[1024]{0:T(1024)S(1)} %copy-done.17, f32[1024]{0:T(1024)S(1)} %copy-done.18, ...), kind=kOutput, calls=%fused_computation.79 | convolution fusion | flops 2155085568 | bytes 17853440 | tf_op jit(solution)/shard_map/dot_general | solution.py:45
  35.2 7.1 %multiply_reduce_fusion.1 = (f32[256]{0:T(256)S(1)}, f32[256]{0:T(256)S(1)}, f32[4096]{0:T(1024)S(1)}, f32[256,4096]{1,0:T(8,128)S(1)}) fusion(f32[256,4096]{1,0:T(8,128)S(1)} %get-tuple-element.60, f32[4096]{0:T(1024)S(1)} %copy-done.11, f32[256]{0:T(256)S(1)} %broadcast_multiply_fusion, bf16[256,1024]{1,0:T(8,128)(2,1)S(1)} %copy-done.9, ...), kind=kOutput, calls=%fused_computation.5 | convolution fusion | flops 2154819072 | bytes 17337344 | tf_op jit(solution)/shard_map/dot_general | solution.py:39
  42.4 1.8 multiply_reduce_fusion
  44.2 4.0 %convert_reduce_fusion = (f32[4096]{0:T(1024)S(1)}, bf16[256,4096]{1,0:T(8,128)(2,1)S(1)}, bf16[4096,256]{0,1:T(8,128)(2,1)S(1)}) fusion(f32[256,4096]{1,0:T(8,128)S(1)} %get-tuple-element.85, f32[256]{0:T(256)S(1)} %negate_multiply_fusion.2, f32[256]{0:T(256)S(1)} %get-tuple-element.81, f32[256,4096]{1,0:T(8,128)S(1)} %get-tuple-element.60, ...), kind=kLoop, calls=%fused_computation.3 | loop fusion | flops 27258880 | bytes 16830464 | tf_op jit(solution)/shard_map/reduce_sum | solution.py:790
  48.2 6.8 %multiply_reduce_fusion.4 = (f32[1024]{0:T(1024)S(1)}, f32[256]{0:T(256)S(1)}, f32[1024]{0:T(1024)S(1)}, f32[256,1024]{1,0:T(8,128)S(1)}) fusion(f32[256,1024]{1,0:T(8,128)S(1)} %get-tuple-element.62, f32[256]{0:T(256)S(1)} %fusion.5, f32[256]{0:T(256)S(1)} %broadcast_multiply_fusion.1, f32[1024]{0:T(1024)S(1)} %copy-done.18, ...), kind=kOutput, calls=%fused_computation.21 | convolution fusion | flops 2149578496 | bytes 12598272 | tf_op jit(solution)/shard_map/dot_general | solution.py:39
  55.0 1.2 fusion.10
  56.2 0.7 multiply_reduce_fusion.5
  58.0 0.5 copy-done.4
  58.5 2.2 convert_multiply_fusion
  60.8 0.6 pad_bitcast_fusion.vec_in
  61.5 2.6 %copy.56 = f32[256,1024]{0,1:T(8,128)} copy(f32[256,1024]{1,0:T(8,128)} %get-tuple-element.52) | data formatting | bytes 2097152 | tf_op jit(solution)/shard_map/mul | solution.py:800
  64.0 1.3 bitcast_reduce_fusion
  65.3 0.6 pad_maximum_fusion.stats
  66.0 2.0 copy.54
  68.0 2.0 copy.53
  70.0 2.5 %copy.52 = bf16[4096,256]{1,0:T(8,128)(2,1)} copy(bf16[4096,256]{0,1:T(8,128)(2,1)S(1)} %get-tuple-element.63) | data formatting | bytes 4194304 | tf_op jit(solution)/shard_map/convert_element_type | solution.py:782
  72.5 2.0 copy.55
  74.6 141.8 %shard_map.340 = (f32[24,16,1024]{2,1,0:T(8,128)}, f32[192,128]{1,0:T(8,128)}, f32[256,1024]{1,0:T(8,128)}) custom-call(bf16[4,2,2,2,8,16,256]{6,5,4,3,2,1,0:T(8,128)(2,1)} %bitcast.65, bf16[4,2,2,2,2,16,256]{6,5,4,3,2,1,0:T(8,128)(2,1)} %bitcast.71, bf16[4,2,2,2,2,16,256]{6,5,4,3,2,1,0:T(8,128)(2,1)} %bitcast.70, ...), custom_call_target="tpu_custom_call" | custom-call | flops 21474836480 | bytes 31457280 | tf_op jit(solution)/shard_map/pallas_call | solution.py:740
  216.4 2.3 fusion.13
  218.7 0.8 copy.59
  219.5 1.0 slice.91
  220.8 1.0 copy.60
  221.8 1.6 slice.95
  223.4 0.6 slice_bitcast_fusion
  224.0 0.6 slice_bitcast_fusion.4
  224.6 0.6 slice_bitcast_fusion.3
  225.2 0.5 slice.116
  225.7 6.8 %fusion.2 = bf16[256,1024]{1,0:T(8,128)(2,1)} fusion(f32[256,1024]{1,0:T(8,128)S(1)} %get-tuple-element.62, bf16[4096,1024]{1,0:T(8,128)(2,1)} %param.37, f32[1024]{0:T(1024)S(1)} %copy-done.22, f32[256,4096]{1,0:T(8,128)S(1)} %copy-done.1, f32[4096]{0:T(1024)S(1)} %copy-done.15, f32[4096]{0:T(1024)S(1)} %copy-done.11, f32[256]{0:T(256)S(1)} %get-tuple-element.82, ...), kind=kOutput, calls=%fused_computation.18 | convolution fusion | flops 2153512960 | bytes 14194688 | tf_op jit(solution)/shard_map/dot_general | solution.py:45
  232.5 1.0 copy.72
  (76 shorter events, 2.3 us)
Async XLA Ops:
  0.7 26.6 %copy-start.19 = (f32[16]{0:T(128)S(1)}, f32[16]{0:T(128)}, u32[]{:S(2)}) copy-start(f32[16]{0:T(128)} %param.26) | copy-start | bytes 196
  0.7 26.8 %copy-start.2 = (bf16[1024,1024]{1,0:T(8,128)(2,1)S(1)}, bf16[1024,1024]{1,0:T(8,128)(2,1)}, u32[]{:S(2)}) copy-start(bf16[1024,1024]{1,0:T(8,128)(2,1)} %param.27) | copy-start | bytes 6291460
  0.7 26.8 %copy-start.13 = (f32[1024]{0:T(1024)S(1)}, f32[1024]{0:T(1024)}, u32[]{:S(2)}) copy-start(f32[1024]{0:T(1024)} %param.28) | copy-start | bytes 12292
  27.3 2.7 %copy-start.12 = (f32[1024]{0:T(1024)S(1)}, f32[1024]{0:T(1024)}, u32[]{:S(2)}) copy-start(f32[1024]{0:T(1024)} %param.29) | copy-start | bytes 12292
  27.3 2.7 %copy-start.16 = (f32[1024]{0:T(1024)S(1)}, f32[1024]{0:T(1024)}, u32[]{:S(2)}) copy-start(f32[1024]{0:T(1024)} %param.30) | copy-start | bytes 12292
  27.5 4.5 %copy-start.17 = (f32[1024]{0:T(1024)S(1)}, f32[1024]{0:T(1024)}, u32[]{:S(2)}) copy-start(f32[1024]{0:T(1024)} %param.32) | copy-start | bytes 12292
  27.5 4.5 %copy-start.18 = (f32[1024]{0:T(1024)S(1)}, f32[1024]{0:T(1024)}, u32[]{:S(2)}) copy-start(f32[1024]{0:T(1024)} %param.31) | copy-start | bytes 12292
  27.5 4.5 %copy-start.20 = (bf16[1024,4096]{1,0:T(8,128)(2,1)S(1)}, bf16[1024,4096]{1,0:T(8,128)(2,1)}, u32[]{:S(2)}) copy-start(bf16[1024,4096]{1,0:T(8,128)(2,1)} %param.33) | copy-start | bytes 25165828
  27.5 4.5 %copy-start.21 = (f32[4096]{0:T(1024)S(1)}, f32[4096]{0:T(1024)}, u32[]{:S(2)}) copy-start(f32[4096]{0:T(1024)} %param.34) | copy-start | bytes 49156
  32.0 3.2 %copy-start.9 = (bf16[256,1024]{1,0:T(8,128)(2,1)S(1)}, bf16[256,1024]{1,0:T(8,128)(2,1)}, u32[]{:S(2)}) copy-start(bf16[256,1024]{1,0:T(8,128)(2,1)} %b2.1) | copy-start | bytes 1572868
  32.0 3.2 %copy-start.11 = (f32[4096]{0:T(1024)S(1)}, f32[4096]{0:T(1024)}, u32[]{:S(2)}) copy-start(f32[4096]{0:T(1024)} %param.35) | copy-start | bytes 49156
  35.2 9.0 %copy-start = (f32[256,4096]{1,0:T(8,128)}, f32[256,4096]{1,0:T(8,128)S(1)}, u32[]{:S(2)}) copy-start(f32[256,4096]{1,0:T(8,128)S(1)} %get-tuple-element.60) | copy-start | bytes 12582916
  42.4 1.8 copy-start.15
  48.2 6.8 %copy-start.7 = (bf16[256,4096]{1,0:T(8,128)(2,1)}, bf16[256,4096]{1,0:T(8,128)(2,1)S(1)}, u32[]{:S(2)}) copy-start(bf16[256,4096]{1,0:T(8,128)(2,1)S(1)} %get-tuple-element.49.b1) | copy-start | bytes 6291460
  56.2 1.8 copy-start.3
  56.2 2.2 copy-start.4
  56.9 1.0 copy-start.5
  57.9 2.7 %copy-start.6 = (bf16[256,1024]{1,0:T(8,128)(2,1)}, bf16[256,1024]{1,0:T(8,128)(2,1)S(1)}, u32[]{:S(2)}) copy-start(bf16[256,1024]{1,0:T(8,128)(2,1)S(1)} %get-tuple-element.51.bo) | copy-start | bytes 1572868
  58.5 6.9 %copy-start.14 = (f32[16,256]{1,0:T(8,128)S(1)}, f32[16,256]{1,0:T(8,128)}, u32[]{:S(2)}) copy-start(f32[16,256]{1,0:T(8,128)} %get-tuple-element.33) | copy-start | bytes 49156
  216.4 7.0 %copy-start.10 = (f32[192,128]{1,0:T(8,128)S(1)}, f32[192,128]{1,0:T(8,128)}, u32[]{:S(2)}) copy-start(f32[192,128]{1,0:T(8,128)} %get-tuple-element.35) | copy-start | bytes 294916
  216.4 9.3 %copy-start.1 = (f32[256,4096]{1,0:T(8,128)S(1)}, f32[256,4096]{1,0:T(8,128)}, u32[]{:S(2)}) copy-start(f32[256,4096]{1,0:T(8,128)} %copy-done) | copy-start | bytes 12582916
  216.4 9.3 %copy-start.22 = (f32[1024]{0:T(1024)S(1)}, f32[1024]{0:T(1024)}, u32[]{:S(2)}) copy-start(f32[1024]{0:T(1024)} %param.38) | copy-start | bytes 12292
  225.7 6.8 %copy-start.8 = (f32[256,1024]{1,0:T(8,128)S(1)}, f32[256,1024]{1,0:T(8,128)}, u32[]{:S(2)}) copy-start(f32[256,1024]{1,0:T(8,128)} %get-tuple-element.108) | copy-start | bytes 3145732

commit v2 on v1

--- a/solution.py
+++ b/solution.py
@@ -15,7 +15,6 @@
 WZ = 256
 WR = 2 * WX + WZ
 ROWS = 16
-SLOTS = 8
 
 
 def norm_rows(values_in, gain_vec, bias_vec):
@@ -69,14 +68,30 @@
     return start
 
 
-def attend_kernel(lens, tok, gain, bias, w_hbm, qv_bias, low_in, qw, kw, vw, att, lse,
-                  w, tok_y, low_y, mask, acc, w_sem, sends, recvs):
+def lane_sums(values):
+    total = values[:, 0:128]
+    for k in range(1, values.shape[1] // 128):
+        total = total + values[:, k * 128:(k + 1) * 128]
+    return total
+
+
+FC = 512
+
+
+def forward_kernel(lens, tok, gain, bias, w_hbm, qv_bias, head_gain, wo_hbm, out_bias, pa_gain, pa_bias, mid_gain, mid_bias,
+                   w1_hbm, fc1_bias, ffn_gain, ffn_bias,
+                   low_in_t, qw_out, kw_out, vw_out, att_out, lse, scaled_t, attn_out, first_out, low_mid_t, normed_out, slope_out,
+                   scale_out, low_ffn_out, low_ffn_t,
+                   w, wo, w1, tok_y, low_in, low_y, qw, kw, vw, mask, acc, att, attn, first, low_mid, act, part, turned, normed,
+                   slope, low_ffn, ffn_turned, w_sem, sends, recvs, out_sem):
     dp, blk = lax.axis_index("dp"), lax.axis_index("blk")
     y, c = blk // 2, blk % 2
     core_dev, y_dev = (dp, blk + 1 - 2 * c), (dp, blk + 2 - 4 * y)
     rows, width = tok.shape
     dim = width // HEADS
     half = rows // 2
+    ff = w1.shape[1]
+    n_ff = ff // FC
 
     def remote(src, dst, i, dev):
         return pltpu.make_async_remote_copy(src, dst, sends.at[i], recvs.at[i], device_id=dev, device_id_type=MESH)
@@ -84,8 +99,10 @@
     n_w = 6
     wc = 3 * width // n_w
     loads = [pltpu.make_async_copy(w_hbm.at[:, pl.ds(i * wc, wc)], w.at[:, pl.ds(i * wc, wc)], w_sem.at[i]) for i in range(n_w)]
-    for cp in loads:
-        cp.start()
+    loads.append(pltpu.make_async_copy(wo_hbm, wo, w_sem.at[6]))
+    loads.append(pltpu.make_async_copy(w1_hbm, w1, w_sem.at[7]))
+    for i in (2, 3, 4, 5, 0, 1, 6, 7):
+        loads[i].start()
     bar = pltpu.get_barrier_semaphore()
     for dev in (core_dev, y_dev):
         pl.semaphore_signal(bar, inc=1, device_id=dev, device_id_type=MESH)
@@ -94,6 +111,13 @@
     for cp in cross:
         cp.start()
 
+    outs = []
+
+    def emit(src, dst):
+        cp = pltpu.make_async_copy(src, dst, out_sem.at[len(outs)])
+        cp.start()
+        outs.append(cp)
+
     q_spots = blk * rows + lax.broadcasted_iota(jnp.int32, (1, rows), 1)
     starts = sequence_starts(lens, q_spots)
     k_spots = (blk - 2) * rows + lax.broadcasted_iota(jnp.int32, (3 * rows, 1), 0)
@@ -101,11 +125,11 @@
 
     low_in[...] = norm_in(tok[...].astype(F32), gain[...], bias[...]).astype(BF16)
 
-    def project(src, r0, n, part):
-        res = dot32(src[r0:r0 + n], w[:, part * width:(part + 1) * width])
-        if part == 0:
+    def project(src, r0, n, which):
+        res = dot32(src[r0:r0 + n], w[:, which * width:(which + 1) * width])
+        if which == 0:
             res = (res + qv_bias[:, 0:width]).astype(BF16).astype(F32) * (dim ** -0.5)
-        if part == 2:
+        if which == 2:
             res = res + qv_bias[:, width:]
         return res.astype(BF16)
 
@@ -140,6 +164,9 @@
     def _():
         own_q.start()
 
+    turned[0] = low_in[...].T
+    emit(turned.at[0], low_in_t)
+
     for i in range(2):
         cross[i].wait_recv()
         low_y[i * half:(i + 1) * half] = norm_in(tok_y[i * half:(i + 1) * half].astype(F32), gain[...], bias[...]).astype(BF16)
@@ -172,15 +199,18 @@
         relay_k.wait_recv()
         relay_v.wait_recv()
 
-    def heads(first):
+    emit(kw, kw_out)
+    emit(vw, vw_out)
+
+    def heads(lowest):
         def pair(i, carry):
             cols = pl.ds(pl.multiple_of(i * 2 * dim, 2 * dim), 2 * dim)
             q2 = qw[0, :, cols]
-            k2 = [kw[j, :, cols] for j in range(first, 3)]
-            v2 = [vw[j, :, cols] for j in range(first, 3)]
+            k2 = [kw[j, :, cols] for j in range(lowest, 3)]
+            v2 = [vw[j, :, cols] for j in range(lowest, 3)]
             for sub in range(2):
-                part = slice(sub * dim, (sub + 1) * dim)
-                scores = [dot_nt(k[:, part], q2[:, part]) + mask[(first + n) * rows:(first + n + 1) * rows]
+                one_head = slice(sub * dim, (sub + 1) * dim)
+                scores = [dot_nt(k[:, one_head], q2[:, one_head]) + mask[(lowest + n) * rows:(lowest + n + 1) * rows]
                           for n, k in enumerate(k2)]
                 top = jnp.max(scores[0], axis=0, keepdims=True)
                 for s in scores[1:]:
@@ -189,10 +219,10 @@
                 for s, v in zip(scores, v2):
                     p = jnp.exp(s - top)
                     one = jnp.sum(p, axis=0, keepdims=True)
-                    term = dot_tn(v[:, part], p.astype(BF16))
+                    term = dot_tn(v[:, one_head], p.astype(BF16))
                     total = one if total is None else total + one
                     out = term if out is None else out + term
-                acc[part] = out / total
+                acc[one_head] = out / total
                 lse[pl.ds(2 * i + sub, 1)] = top + jnp.log(total)
             att[:, cols] = acc[...].T
             return carry
@@ -211,6 +241,71 @@
     def _():
         heads(0)
 
+    @pl.when(c == 0)
+    def _():
+        own_q.wait_recv()
+
+    @pl.when((y == 0) & (c == 1))
+    def _():
+        relay_q.wait_recv()
+
+    emit(qw, qw_out)
+    emit(att, att_out)
+
+    scaled = (att[...] * head_gain[...]).astype(BF16)
+    loads[6].wait()
+    attn[...] = dot32(scaled, wo[...]) + out_bias[...]
+    emit(attn, attn_out)
+    first[...] = tok[...].astype(F32) + norm_in(attn[...], pa_gain[...], pa_bias[...])
+    emit(first, first_out)
+    low_mid[...] = norm_in(first[...], mid_gain[...], mid_bias[...]).astype(BF16)
+    loads[7].wait()
+    part[...] = jnp.zeros_like(part)
+
+    def ffn_cols(j):
+        return pl.ds(pl.multiple_of(j * FC, FC), FC)
+
+    def gelu_part(j, carry):
+        cols = ffn_cols(j)
+        pre = dot32(low_mid[...], w1[:, cols]) + fc1_bias[:, cols]
+        gate = 0.5 * (1.0 + lax.erf(pre * 0.7071067811865476))
+        out = pre * gate
+        act[:, cols] = out
+        slope[:, cols] = (gate + pre * (jnp.exp(-0.5 * (pre * pre)) * 0.3989422804014327)).astype(BF16)
+        part[0] = part[0] + lane_sums(out)
+        return carry
+
+    lax.fori_loop(0, n_ff, gelu_part, 0)
+    emit(slope, slope_out)
+    mean = jnp.sum(part[0], axis=-1, keepdims=True) * (1.0 / ff)
+
+    def spread_part(j, carry):
+        centered = act[:, ffn_cols(j)] - mean
+        part[1] = part[1] + lane_sums(centered * centered)
+        return carry
+
+    lax.fori_loop(0, n_ff, spread_part, 0)
+    scale = lax.rsqrt(jnp.sum(part[1], axis=-1, keepdims=True) * (1.0 / ff) + 1e-05)
+    scale_out[...] = jnp.broadcast_to(scale, scale_out.shape)
+
+    def norm_part(j, carry):
+        cols = ffn_cols(j)
+        unit = (act[:, cols] - mean) * scale
+        normed[:, cols] = unit.astype(BF16)
+        low = (unit * ffn_gain[:, cols] + ffn_bias[:, cols]).astype(BF16)
+        low_ffn[:, cols] = low
+        ffn_turned[cols] = low.T
+        return carry
+
+    lax.fori_loop(0, n_ff, norm_part, 0)
+    emit(normed, normed_out)
+    emit(low_ffn, low_ffn_out)
+    emit(ffn_turned, low_ffn_t)
+    turned[1] = scaled.T
+    emit(turned.at[1], scaled_t)
+    turned[2] = low_mid[...].T
+    emit(turned.at[2], low_mid_t)
+
     for cp in cross:
         cp.wait_send()
 
@@ -218,7 +313,6 @@
     def _():
         own_k.wait_send()
         own_v.wait_send()
-        own_q.wait_recv()
 
     @pl.when(c == 1)
     def _():
@@ -233,40 +327,59 @@
     def _():
         relay_q.wait_send()
 
-    @pl.when((y == 0) & (c == 1))
-    def _():
-        relay_q.wait_recv()
-
-
-def attend(lengths, tokens, gain, bias, w_qkv, qv_bias):
+    for cp in outs:
+        cp.wait()
+
+
+def forward(lengths, tokens, ln1_gain, ln1_bias, w_qkv, qv_bias, head_gain, w_out, out_bias, pa_gain, pa_bias, mid_gain, mid_bias,
+            w_fc1, fc1_bias, ffn_gain, ffn_bias):
     rows, width = tokens.shape
+    ff = w_fc1.shape[1]
     vmem, hbm = pl.BlockSpec(memory_space=pltpu.VMEM), pl.BlockSpec(memory_space=pl.ANY)
-    window = jax.ShapeDtypeStruct((3, rows, width), BF16)
+    shape = jax.ShapeDtypeStruct
+    window, wide, tall = (3, rows, width), (rows, ff), (ff, rows)
+    dma = pltpu.SemaphoreType.DMA
     return pl.pallas_call(
-        attend_kernel,
-        out_shape=[jax.ShapeDtypeStruct((rows, width), BF16), window, window, window,
-                   jax.ShapeDtypeStruct((rows, width), F32), jax.ShapeDtypeStruct((HEADS, rows), F32)],
-        in_specs=[pl.BlockSpec(memory_space=pltpu.SMEM), vmem, vmem, vmem, hbm, vmem],
-        out_specs=[vmem] * 6,
-        scratch_shapes=[pltpu.VMEM((width, 3 * width), BF16), pltpu.VMEM((rows, width), BF16), pltpu.VMEM((rows, width), BF16),
+        forward_kernel,
+        out_shape=[shape((width, rows), BF16), shape(window, BF16), shape(window, BF16), shape(window, BF16),
+                   shape((rows, width), F32), shape((HEADS, rows), F32), shape((width, rows), BF16), shape((rows, width), F32),
+                   shape((rows, width), F32), shape((width, rows), BF16), shape(wide, BF16), shape(wide, BF16),
+                   shape((rows, 128), F32), shape(wide, BF16), shape(tall, BF16)],
+        in_specs=[pl.BlockSpec(memory_space=pltpu.SMEM), vmem, vmem, vmem, hbm, vmem, vmem, hbm] + [vmem] * 5 + [hbm] + [vmem] * 3,
+        out_specs=[hbm] * 5 + [vmem] + [hbm] * 6 + [vmem] + [hbm] * 2,
+        scratch_shapes=[pltpu.VMEM((width, 3 * width), BF16), pltpu.VMEM((width, width), BF16), pltpu.VMEM((width, ff), BF16),
+                        pltpu.VMEM((rows, width), BF16), pltpu.VMEM((rows, width), BF16), pltpu.VMEM((rows, width), BF16),
+                        pltpu.VMEM(window, BF16), pltpu.VMEM(window, BF16), pltpu.VMEM(window, BF16),
                         pltpu.VMEM((3 * rows, rows), F32), pltpu.VMEM((2 * width // HEADS, rows), F32),
-                        pltpu.SemaphoreType.DMA((6,)), pltpu.SemaphoreType.DMA((8,)), pltpu.SemaphoreType.DMA((8,))],
-        compiler_params=pltpu.CompilerParams(collective_id=1, has_side_effects=True, vmem_limit_bytes=56 << 20),
-        cost_estimate=pl.CostEstimate(flops=8 << 30, bytes_accessed=12 << 20, transcendentals=3 << 20),
-    )(lengths, tokens, gain[None], bias[None], w_qkv, qv_bias[None])
-
-
-RECV = 12
-PAIR0 = 4
-
-
-def back_kernel(tok, a2, a1, ao, aq, b2, b1, bo, lens, qw, kw, vw, d_att, stats, w_hbm, tokens, gain, d_first, vec_in,
-                out, vout, grad_tok,
+                        pltpu.VMEM((rows, width), F32), pltpu.VMEM((rows, width), F32), pltpu.VMEM((rows, width), F32),
+                        pltpu.VMEM((rows, width), BF16), pltpu.VMEM(wide, F32), pltpu.VMEM((2, rows, 128), F32),
+                        pltpu.VMEM((3, width, rows), BF16), pltpu.VMEM(wide, BF16), pltpu.VMEM(wide, BF16), pltpu.VMEM(wide, BF16),
+                        pltpu.VMEM(tall, BF16), dma((8,)), dma((8,)), dma((8,)), dma((13,))],
+        compiler_params=pltpu.CompilerParams(collective_id=1, has_side_effects=True, vmem_limit_bytes=60 << 20),
+        cost_estimate=pl.CostEstimate(flops=12 << 30, bytes_accessed=40 << 20, transcendentals=5 << 20),
+    )(lengths, tokens, ln1_gain[None], ln1_bias[None], w_qkv, qv_bias[None], head_gain[None], w_out, out_bias[None],
+      pa_gain[None], pa_bias[None], mid_gain[None], mid_bias[None], w_fc1, fc1_bias[None], ffn_gain[None], ffn_bias[None])
+
+
+SEND = 4
+RECV = 8
+KEEP = 8
+LAG_XY = (0, 2, 4, 6, 8, 10)
+LAG_Z = (0, 2, 4, 6, 8, 10)
+PAIR0 = 9
+PIECES = 3
+
+
+def back_kernel(tok, a2, a1, ao, aq, cot, lens, qw_in, kw_in, vw_in, lse, att, attn, first, scale_ffn, tokens,
+                gain, pa_gain, mid_gain, ffn_gain, head_gain, fc2_bias, normed_in, slope_in, low_ffn_in, w2_in, w1_in, wo_in, wq_in,
+                out2, out1, outo, outq, vout, grad_tok, layer_out,
                 am, ap, bm, bp, s1x, s1y, s2x, s2y, sr, sl, szr, szl, szx, szy, swx, swy,
                 r1x, r1y, r2x, r2y, rr, rl, rzr, rzl, rzx, rzy, rwx, rwy,
-                k2x, k2y, t3, kzx, kzy, kwx, kwy, vec, vown, vrecv,
-                w, dow, stw, mask, mask_q, dqa, dka, dva, d_in,
-                load_sem, peer_send, peer_recv, send, recv, vsend, vrecv_sem, w_sem, asend, arecv):
+                k2x, k2y, t3, kzx, kzy, kwx, kwy, out, vec, vown, vrecv,
+                qw, kw, vw, dow, stw, mask, mask_q, dqa, dka, dva, total, d_first, d_ffn, parts,
+                normed, w2b, colb, lowb, slopeb,
+                load_sem, peer_send, peer_recv, send, recv, vsend, vrecv_sem, asend, arecv, in_sem, w2_sem, col_sem, low_sem, slope_sem,
+                out_sem):
     dp, blk = lax.axis_index("dp"), lax.axis_index("blk")
     z, x = dp // 2, dp % 2
     y, c = blk // 2, blk % 2
@@ -276,7 +389,36 @@
     rows, width = tokens.shape
     dim = width // HEADS
 
-    w_load = pltpu.make_async_copy(w_hbm, w, w_sem.at[0])
+    ff = normed.shape[1]
+    n_ff = ff // FC
+    n_o, n_q = width // FC, 3 * width // FC
+
+    def piece2(j):
+        return [pltpu.make_async_copy(w2_in.at[pl.ds(j * FC, FC)], w2b.at[j % PIECES], w2_sem.at[j % PIECES]),
+                pltpu.make_async_copy(low_ffn_in.at[:, pl.ds(j * FC, FC)], lowb.at[j % PIECES], low_sem.at[j % PIECES])]
+
+    def piece_slope(j):
+        return pltpu.make_async_copy(slope_in.at[:, pl.ds(j * FC, FC)], slopeb.at[j % PIECES], slope_sem.at[j % PIECES])
+
+    def piece_col(q, ref, j):
+        return pltpu.make_async_copy(ref.at[:, pl.ds(j * FC, FC)], colb.at[q % PIECES], col_sem.at[q % PIECES])
+
+    def start_col(q):
+        def go(ref, low, high):
+            def start():
+                piece_col(q, ref, q - low).start()
+            if isinstance(q, int):
+                if low <= q < high:
+                    start()
+            else:
+                pl.when((q >= low) & (q < high))(start)
+        go(w1_in, 0, n_ff)
+        go(wo_in, n_ff, n_ff + n_o)
+        go(wq_in, n_ff + n_o, n_ff + n_o + n_q)
+
+    early = [pltpu.make_async_copy(qw_in, qw, in_sem.at[0]), pltpu.make_async_copy(kw_in, kw, in_sem.at[1]),
+             pltpu.make_async_copy(vw_in, vw, in_sem.at[2])]
+    normed_load = pltpu.make_async_copy(normed_in, normed, in_sem.at[3])
 
     bar = pltpu.get_barrier_semaphore()
     z_devs = [((dp + 2 * k) % 8, blk) for k in range(1, 4)]
@@ -290,21 +432,11 @@
     def window(kind):
         src, dst, dev = {"cross": (0, 2, y_dev), "own": (0, 1, core_dev), "relay": (2, 1, core_dev)}[kind]
         k = {"cross": 0, "own": 2, "relay": 4}[kind]
-        return [remote(d_att if src == 0 else dow.at[src], dow.at[dst], asend.at[k], arecv.at[k], dev),
-                remote(stats if src == 0 else stw.at[src], stw.at[dst], asend.at[k + 1], arecv.at[k + 1], dev)]
-
-    @pl.when(y == 1)
-    def _():
-        for cp in window("cross"):
-            cp.start()
-
-    @pl.when(c == 1)
-    def _():
-        for cp in window("own"):
-            cp.start()
+        return [remote(dow.at[src], dow.at[dst], asend.at[k], arecv.at[k], dev),
+                remote(stw.at[src], stw.at[dst], asend.at[k + 1], arecv.at[k + 1], dev)]
 
     a_src = [(a2, g) for g in range(8)] + [(a1, 0), (a1, 1), (ao, 0), (ao, 1), (aq, 0), (aq, 1)]
-    b_src = [(b2, 0)] + [(b1, i) for i in range(4)] + [(bo, 0)]
+    b_src = [(cot, 0)]
     n_a = len(a_src)
 
     def loads(kind, i, own):
@@ -320,14 +452,23 @@
             return pltpu.make_async_copy(part, bm.at[i], load_sem.at[k])
         return remote(part, bp.at[i], peer_send.at[k], peer_recv.at[k], core_dev)
 
-    phases = [([("b", 0)] + [("a", g) for g in range(8)]),
-              ([("a", 8), ("a", 9)] + [("b", i) for i in range(1, 5)]),
-              ([("a", 10), ("a", 11), ("b", 5), ("a", 12), ("a", 13)])]
-    for phase in phases:
+    phases = [([("b", 0)] + [("a", g) for g in range(8)]), [("a", 8), ("a", 9)], [("a", 10), ("a", 11), ("a", 12), ("a", 13)]]
+    for item in phases[0]:
+        loads(*item, True).start()
+        loads(*item, False).start()
+    normed_load.start()
+    for j in range(PIECES):
+        for cp in piece2(j):
+            cp.start()
+    for phase in phases[1:]:
         for item in phase:
             loads(*item, True).start()
             loads(*item, False).start()
-    w_load.start()
+    for j in range(PIECES):
+        start_col(j)
+        piece_slope(j).start()
+    for cp in early:
+        cp.start()
 
     def peer_b(i):
         k = n_a + i
@@ -338,7 +479,9 @@
             loads(*item, True).wait()
             loads(*item, False).wait_recv()
 
-    vec[...] = vec_in[...]
+    vec[...] = jnp.zeros_like(vec)
+    total[...] = jnp.zeros_like(total)
+    parts[...] = jnp.zeros_like(parts)
     q_spots = blk * rows + lax.broadcasted_iota(jnp.int32, (1, rows), 1)
     k_spots = (blk - 2) * rows + lax.broadcasted_iota(jnp.int32, (3 * rows, 1), 0)
     mask[...] = jnp.where((k_spots >= sequence_starts(lens, q_spots)) & (k_spots <= q_spots), 0.0, -1e30)
@@ -368,24 +511,38 @@
 
     def message(src, dst, kind, dev):
         def make(r):
-            return remote(src.at[r % SLOTS], dst.at[r % RECV], send.at[kind, r % SLOTS], recv.at[kind, r % RECV], dev)
+            return remote(src.at[r % SEND], dst.at[r % RECV], send.at[kind, r % SEND], recv.at[kind, r % RECV], dev)
         return make
 
     step1x, step1y = message(s1x, r1x, S1X, x_dev), message(s1y, r1y, S1Y, y_dev)
     step2x, step2y = message(s2x, r2x, S2X, y_dev), message(s2y, r2y, S2Y, x_dev)
     stepzx, stepzy = message(szx, rzx, SZX, x_dev), message(szy, rzy, SZY, y_dev)
     stepwx, stepwy = message(swx, rwx, SWX, y_dev), message(swy, rwy, SWY, x_dev)
+    steps = (step1x, step1y, step2x, step2y, stepzx, stepzy, stepwx, stepwy)
+
+    def put(step, ref, r, value):
+        @pl.when(r >= SEND)
+        def _():
+            step(r - SEND).wait_send()
+
+        ref[r % SEND] = value.astype(BF16)
+        step(r).start()
 
     def chain(src, dst, kind, r, lo, hi, dev):
-        return remote(src.at[r % SLOTS, lo:hi], dst.at[r % RECV, lo:hi], send.at[kind, r % SLOTS], recv.at[kind, r % RECV], dev)
+        return remote(src.at[r % SEND, lo:hi], dst.at[r % RECV, lo:hi], send.at[kind, r % SEND], recv.at[kind, r % RECV], dev)
 
     def chain_hop(hop, r, src, dst, kind_r, kind_l, term):
-        slot, rslot = r % SLOTS, r % RECV
+        slot, rslot = r % SEND, r % RECV
 
         @pl.when(z == hop)
         def _():
             if hop > 0:
                 chain(src[0], dst[0], kind_r, r, hop - 1, 3, up_dev).wait_recv()
+
+            @pl.when(r >= SEND)
+            def _():
+                chain(src[0], dst[0], kind_r, r - SEND, hop, 3, up_dev).wait_send()
+
             for d in range(hop + 1, 4):
                 value = term(r, d)
                 if hop > 0:
@@ -397,6 +554,11 @@
         def _():
             if hop > 0:
                 chain(src[1], dst[1], kind_l, r, 0, 4 - hop, down_dev).wait_recv()
+
+            @pl.when(r >= SEND)
+            def _():
+                chain(src[1], dst[1], kind_l, r - SEND, 0, 3 - hop, down_dev).wait_send()
+
             for d in range(0, 3 - hop):
                 value = term(r, d)
                 if hop > 0:
@@ -435,76 +597,80 @@
         return product(r, d, ALL, ALL, col_z, WZ)
 
     def t_term(r, d):
-        return t3[r % SLOTS, d]
+        return t3[r % KEEP, d]
 
     zsrc, zdst = (szr, szl), (rzr, rzl)
     csrc, cdst = (sr, sl), (rr, rl)
 
-    def p0(r):
-        s1x[r % SLOTS] = product(r, ALL, 1 - x, ALL, 0, WX).astype(BF16)
-        step1x(r).start()
-        s1y[r % SLOTS] = product(r, ALL, ALL, 1 - y, col_y, WX).astype(BF16)
-        step1y(r).start()
-        chain_hop(0, r, zsrc, zdst, SZR, SZL, z_term)
-
-    def p1(r):
-        slot = r % SLOTS
+    def xy0(r):
+        put(step1x, s1x, r, product(r, ALL, 1 - x, ALL, 0, WX))
+        put(step1y, s1y, r, product(r, ALL, ALL, 1 - y, col_y, WX))
+
+    def xy1(r):
+        slot = r % KEEP
         step1x(r).wait_recv()
         k2x[...] = product(r, ALL, x, ALL, 0, WX) + r1x[r % RECV].astype(F32)
-        s2x[slot] = k2x[:, 1 - y].astype(BF16)
-        step2x(r).start()
+        put(step2x, s2x, r, k2x[:, 1 - y])
         kwx[slot] = k2x[:, y]
         step1y(r).wait_recv()
         k2y[...] = product(r, ALL, ALL, y, col_y, WX) + r1y[r % RECV].astype(F32)
-        s2y[slot] = k2y[:, 1 - x].astype(BF16)
-        step2y(r).start()
+        put(step2y, s2y, r, k2y[:, 1 - x])
         kwy[slot] = k2y[:, x]
-        chain_hop(1, r, zsrc, zdst, SZR, SZL, z_term)
-
-    def p2(r):
-        slot = r % SLOTS
+
+    def xy2(r):
+        slot = r % KEEP
         step2x(r).wait_recv()
         t3[slot, :, :, 0:WX] = kwx[slot] + r2x[r % RECV].astype(F32)
         step2y(r).wait_recv()
         t3[slot, :, :, WX:2 * WX] = kwy[slot] + r2y[r % RECV].astype(F32)
         chain_hop(0, r, csrc, cdst, SR, SL, t_term)
+
+    def xy3(r):
+        chain_hop(1, r, csrc, cdst, SR, SL, t_term)
+
+    def xy4(r):
+        chain_hop(2, r, csrc, cdst, SR, SL, t_term)
+
+    def xy5(r):
+        chain_last(r, csrc, cdst, SR, SL, out.at[r, :, 0:2 * WX])
+        out[r, :, 0:2 * WX] = out[r, :, 0:2 * WX] + t3[r % KEEP, z]
+
+    def z0(r):
+        chain_hop(0, r, zsrc, zdst, SZR, SZL, z_term)
+
+    def z1(r):
+        chain_hop(1, r, zsrc, zdst, SZR, SZL, z_term)
+
+    def z2(r):
         chain_hop(2, r, zsrc, zdst, SZR, SZL, z_term)
 
-    def p3(r):
-        slot = r % SLOTS
-        chain_hop(1, r, csrc, cdst, SR, SL, t_term)
+    def z3(r):
+        slot = r % KEEP
         chain_last(r, zsrc, zdst, SZR, SZL, kzx)
         kzx[...] = kzx[...] + product(r, z, ALL, ALL, col_z, WZ)
-        szx[slot] = kzx[1 - x, :, :, 0:WZ // 2].astype(BF16)
-        stepzx(r).start()
-        szy[slot] = kzx[:, 1 - y, :, WZ // 2:WZ].astype(BF16)
-        stepzy(r).start()
+        put(stepzx, szx, r, kzx[1 - x, :, :, 0:WZ // 2])
+        put(stepzy, szy, r, kzx[:, 1 - y, :, WZ // 2:WZ])
         kzy[slot, 0] = kzx[x, :, :, 0:WZ // 2]
         kzy[slot, 1] = kzx[:, y, :, WZ // 2:WZ]
 
-    def p4(r):
-        slot = r % SLOTS
-        chain_hop(2, r, csrc, cdst, SR, SL, t_term)
+    def z4(r):
+        slot = r % KEEP
         stepzx(r).wait_recv()
         kzy[slot, 0] = kzy[slot, 0] + rzx[r % RECV].astype(F32)
-        swx[slot] = kzy[slot, 0, 1 - y].astype(BF16)
-        stepwx(r).start()
+        put(stepwx, swx, r, kzy[slot, 0, 1 - y])
         stepzy(r).wait_recv()
         kzy[slot, 1] = kzy[slot, 1] + rzy[r % RECV].astype(F32)
-        swy[slot] = kzy[slot, 1, 1 - x].astype(BF16)
-        stepwy(r).start()
-
-    def p5(r):
-        slot = r % SLOTS
-        chain_last(r, csrc, cdst, SR, SL, out.at[r, :, 0:2 * WX])
-        out[r, :, 0:2 * WX] = out[r, :, 0:2 * WX] + t3[slot, z]
+        put(stepwy, swy, r, kzy[slot, 1, 1 - x])
+
+    def z5(r):
+        slot = r % KEEP
         stepwx(r).wait_recv()
         out[r, :, 2 * WX:2 * WX + WZ // 2] = kzy[slot, 0, y] + rwx[r % RECV].astype(F32)
         stepwy(r).wait_recv()
         out[r, :, 2 * WX + WZ // 2:] = kzy[slot, 1, x] + rwy[r % RECV].astype(F32)
 
     def drain(r):
-        for step in (step1x, step1y, step2x, step2y, stepzx, stepzy, stepwx, stepwy):
+        for step in steps:
             step(r).wait_send()
         chain_drain(r, csrc, cdst, SR, SL)
         chain_drain(r, zsrc, zdst, SZR, SZL)
@@ -553,8 +719,8 @@
                 cp.start()
 
     def windows_arrive():
-        dow[0] = d_att[...]
-        stw[0] = stats[...]
+        for cp in early:
+            cp.wait()
 
         @pl.when(y == 0)
         def _():
@@ -635,72 +801,203 @@
         bm[7, :, cols] = jnp.concatenate([dka[0], dka[1]], axis=1).astype(BF16)
         bm[8, :, cols] = jnp.concatenate([dva[0], dva[1]], axis=1).astype(BF16)
 
-    def put_row(first, row):
+    V_IN_GAIN, V_IN_BIAS, V_QV, V_OUT, V_PA_GAIN, V_PA_BIAS, V_MID_GAIN, V_MID_BIAS, V_FC2, V_HEADS = (
+        k * (width // 128) for k in (0, 1, 2, 4, 5, 6, 7, 8, 9, 10))
+    V_FC1 = 11 * (width // 128)
+    V_FFN_GAIN = V_FC1 + ff // 128
+    V_FFN_BIAS = V_FFN_GAIN + ff // 128
+
+    def put_row(first_row, row):
         for k in range(row.shape[1] // 128):
-            vec[first + k:first + k + 1, :] = row[:, k * 128:(k + 1) * 128]
-
-    def input_back():
+            vec[first_row + k:first_row + k + 1, :] = row[:, k * 128:(k + 1) * 128]
+
+    def put_row_at(first_row, j, row):
+        for k in range(FC // 128):
+            vec[pl.ds(first_row + j * (FC // 128) + k, 1), :] = row[:, k * 128:(k + 1) * 128]
+
+    def chunk_cols(j):
+        return pl.ds(pl.multiple_of(j * FC, FC), FC)
+
+    def ffn_first(j):
+        cols = chunk_cols(j)
+        for cp in piece2(j):
+            cp.wait()
+        weights = w2b[j % PIECES]
+        total[...] = total[...] + dot32(lowb[j % PIECES], weights)
+        grad = dot_nt(bm[0], weights)
+        unit = normed[:, cols].astype(F32)
+        d_ffn[:, cols] = grad
+        put_row_at(V_FFN_GAIN, j, jnp.sum(grad * unit, axis=0, keepdims=True))
+        put_row_at(V_FFN_BIAS, j, jnp.sum(grad, axis=0, keepdims=True))
+        grad = grad * ffn_gain[:, cols]
+        parts[0] = parts[0] + lane_sums(grad)
+        parts[1] = parts[1] + lane_sums(grad * unit)
+
+        @pl.when(j + PIECES < n_ff)
+        def _():
+            for cp in piece2(j + PIECES):
+                cp.start()
+
+    def ffn_between():
+        layer_out[...] = (first[...] + total[...] + fc2_bias[...]).astype(BF16)
+        total[...] = jnp.zeros_like(total)
+        parts[2] = jnp.broadcast_to(jnp.sum(parts[0], axis=-1, keepdims=True) * (1.0 / ff), parts.shape[1:])
+        parts[3] = jnp.broadcast_to(jnp.sum(parts[1], axis=-1, keepdims=True) * (1.0 / ff), parts.shape[1:])
+
+    def ffn_second(j):
+        cols = chunk_cols(j)
+        piece_col(j, w1_in, j).wait()
+        piece_slope(j).wait()
+        grad = d_ffn[:, cols] * ffn_gain[:, cols]
+        grad = scale_ffn[:, 0:1] * (grad - parts[2][:, 0:1] - normed[:, cols].astype(F32) * parts[3][:, 0:1])
+        low = (grad * slopeb[j % PIECES].astype(F32)).astype(BF16)
+        bm[1 + j // 2, :, pl.ds(pl.multiple_of((j % 2) * FC, FC), FC)] = low
+        put_row_at(V_FC1, j, jnp.sum(low.astype(F32), axis=0, keepdims=True))
+        total[...] = total[...] + dot_nt(low, colb[j % PIECES])
+
+        @pl.when(j % 2 == 1)
+        def _():
+            peer_b(1 + j // 2).start()
+
+        @pl.when(j + PIECES < n_ff)
+        def _():
+            piece_slope(j + PIECES).start()
+
+        start_col(j + PIECES)
+
+    def unit_rows(values):
+        centered = values - jnp.mean(values, axis=-1, keepdims=True)
+        scale = lax.rsqrt(jnp.mean(centered * centered, axis=-1, keepdims=True) + 1e-05)
+        return centered * scale, scale
+
+    def norm_back(grad, values, gain_row, gain_at, bias_at):
+        unit, scale = unit_rows(values)
+        put_row(gain_at, jnp.sum(grad * unit, axis=0, keepdims=True))
+        put_row(bias_at, jnp.sum(grad, axis=0, keepdims=True))
+        grad = grad * gain_row
+        return scale * (grad - jnp.mean(grad, axis=-1, keepdims=True) - unit * jnp.mean(grad * unit, axis=-1, keepdims=True))
+
+    def middle_first():
+        d_out = bm[0].astype(F32)
+        put_row(V_FC2, jnp.sum(d_out, axis=0, keepdims=True))
+        d_first[...] = d_out + norm_back(total[...], first[...], mid_gain[...], V_MID_GAIN, V_MID_BIAS)
+        low = norm_back(d_first[...], attn[...], pa_gain[...], V_PA_GAIN, V_PA_BIAS).astype(BF16)
+        bm[5] = low
+        peer_b(5).start()
+        put_row(V_OUT, jnp.sum(low.astype(F32), axis=0, keepdims=True))
+
+    def middle_second():
+        for k in range(n_o):
+            piece_col(n_ff + k, wo_in, k).wait()
+        total[...] = dot_nt(bm[5, :, 0:FC], colb[n_ff % PIECES])
+        for k in range(1, n_o):
+            total[...] = total[...] + dot_nt(bm[5, :, k * FC:(k + 1) * FC], colb[(n_ff + k) % PIECES])
+        for k in range(n_o):
+            start_col(n_ff + k + PIECES)
+        attended = att[...]
+        put_row(V_HEADS, jnp.sum(total[...] * attended, axis=0, keepdims=True))
+        low = (total[...] * head_gain[...]).astype(BF16)
+        dow[0] = low
+        both = low.astype(F32) * attended
+        high = both.astype(BF16)
+        rest = (both - high.astype(F32)).astype(BF16)
+        head_of = lax.broadcasted_iota(jnp.int32, (HEADS, width), 1) // dim
+        pick = jnp.where(head_of == lax.broadcasted_iota(jnp.int32, (HEADS, width), 0), 1.0, 0.0).astype(BF16)
+        stw[0, 0:HEADS] = lse[...]
+        stw[0, HEADS:2 * HEADS] = dot_nt(pick, high) + dot_nt(pick, rest)
+
+        @pl.when(y == 1)
+        def _():
+            for cp in window("cross"):
+                cp.start()
+
+        @pl.when(c == 1)
+        def _():
+            for cp in window("own"):
+                cp.start()
+
+    def input_first():
         for i in range(6, 9):
             peer_b(i).start()
-        w_load.wait()
-        d_in[...] = dot_nt(bm[6], w[:, 0:width])
-        d_in[...] = d_in[...] + dot_nt(bm[7], w[:, width:2 * width])
-        grad = d_in[...] + dot_nt(bm[8], w[:, 2 * width:])
-        rows_in = tokens[...].astype(F32)
-        centered = rows_in - jnp.mean(rows_in, axis=-1, keepdims=True)
-        scale = lax.rsqrt(jnp.mean(centered * centered, axis=-1, keepdims=True) + 1e-05)
-        normed = centered * scale
-        put_row(0, jnp.sum(grad * normed, axis=0, keepdims=True))
-        put_row(width // 128, jnp.sum(grad, axis=0, keepdims=True))
-        put_row(2 * width // 128, jnp.sum(bm[6].astype(F32), axis=0, keepdims=True))
-        put_row(3 * width // 128, jnp.sum(bm[8].astype(F32), axis=0, keepdims=True))
-        grad = grad * gain[...]
-        grad = grad - jnp.mean(grad, axis=-1, keepdims=True) - normed * jnp.mean(grad * normed, axis=-1, keepdims=True)
-        grad_tok[...] = d_first[...] + scale * grad
-
-    phase_list = (p0, p1, p2, p3, p4, p5)
-    lags = (0, 2, 4, 5, 6, 7)
+        base_q = n_ff + n_o
+        for k in range(n_q):
+            piece_col(base_q + k, wq_in, k).wait()
+            at = k * FC
+            term = dot_nt(bm[6 + at // width, :, at % width:at % width + FC], colb[(base_q + k) % PIECES])
+            total[...] = term if k == 0 else total[...] + term
+            start_col(base_q + k + PIECES)
+
+    def input_second():
+        grad = norm_back(total[...], tokens[...].astype(F32), gain[...], V_IN_GAIN, V_IN_BIAS)
+        grad_tok[...] = d_first[...] + grad
+        put_row(V_QV, jnp.sum(bm[6].astype(F32), axis=0, keepdims=True))
+        put_row(V_QV + width // 128, jnp.sum(bm[8].astype(F32), axis=0, keepdims=True))
+
+    def share(r):
+        half = pl.ds((r % 2) * ROWS, ROWS)
+        return [((r >= 0) & (r < 8), pltpu.make_async_copy(out.at[r], out2.at[pl.ds(r * ROWS, ROWS)], out_sem.at[0])),
+                ((r >= 8) & (r < 16), pltpu.make_async_copy(out.at[r], out1.at[half, pl.ds((r - 8) // 2 * WR, WR)], out_sem.at[0])),
+                ((r >= 16) & (r < 18), pltpu.make_async_copy(out.at[r], outo.at[half], out_sem.at[0])),
+                ((r >= 18) & (r < rounds), pltpu.make_async_copy(out.at[r], outq.at[half, pl.ds((r - 18) // 2 * WR, WR)], out_sem.at[0]))]
+
     n_pairs = HEADS // 2
     after = PAIR0 + n_pairs
+    plan = sorted(list(zip(LAG_XY, (xy0, xy1, xy2, xy3, xy4, xy5))) + list(zip(LAG_Z, (z0, z1, z2, z3, z4, z5))),
+                  key=lambda item: -item[0])
+    last = max(LAG_XY + LAG_Z)
+
+    def at_slot(s, number, work):
+        @pl.when(s == number)
+        def _():
+            work()
 
     def slot_step(s, carry):
-        for k in (5, 4, 3, 2, 1):
-            r = s - lags[k]
+        at_slot(s, 0, lambda: arrive(phases[0]))
+        at_slot(s, 7, lambda: arrive(phases[1]))
+        at_slot(s, 15, lambda: arrive(phases[2]))
+
+        @pl.when((s >= 8) & (s < 16) & (s % 2 == 0))
+        def _():
+            peer_b(1 + (s - 8) // 2).wait_recv()
+
+        at_slot(s, 16, lambda: peer_b(5).wait_recv())
+        at_slot(s, 18, lambda: [peer_b(i).wait_recv() for i in range(6, 9)])
+
+        for lag, work in plan:
+            r = s - lag
 
             @pl.when((r >= 0) & (r < rounds))
             def _():
-                phase_list[k](r)
-
-        for at, phase in ((0, 0), (7, 1), (15, 2)):
-            @pl.when(s == at)
+                work(r)
+
+        r = s - last
+
+        @pl.when(r >= 0)
+        def _():
+            for here, cp in share(r):
+                pl.when(here)(cp.start)
+
+        at_slot(s, 0, normed_load.wait)
+        for u in range(2):
+            @pl.when(s < 4)
             def _():
-                arrive(phases[phase])
-
-        @pl.when(s == 17)
-        def _():
-            for i in range(6, 9):
-                peer_b(i).wait_recv()
-
-        @pl.when((s >= SLOTS) & (s < rounds))
-        def _():
-            drain(s - SLOTS)
-
-        @pl.when(s < rounds)
-        def _():
-            p0(s)
-
-        @pl.when(s == PAIR0)
-        def _():
-            windows_arrive()
+                ffn_first(2 * s + u)
+
+            @pl.when((s >= 4) & (s < 8))
+            def _():
+                ffn_second(2 * (s - 4) + u)
+
+        at_slot(s, 3, ffn_between)
+        at_slot(s, 8, middle_first)
+        at_slot(s, 8, middle_second)
+        at_slot(s, PAIR0, windows_arrive)
 
         @pl.when((s >= PAIR0) & (s < after))
         def _():
             attend_back(s - PAIR0)
 
-        @pl.when(s == after)
-        def _():
-            input_back()
-
+        at_slot(s, after - 1, input_first)
+        at_slot(s, after, input_second)
         for i in range(8):
             @pl.when(s == after + i)
             def _():
@@ -708,115 +1005,79 @@
 
         return carry
 
-    lax.fori_loop(0, rounds + lags[5], slot_step, 0)
-    lax.fori_loop(rounds - SLOTS, rounds, lambda r, carry: (drain(r), carry)[1], 0)
+    lax.fori_loop(0, rounds + last, slot_step, 0)
+    lax.fori_loop(rounds - SEND, rounds, lambda r, carry: (drain(r), carry)[1], 0)
     windows_drain()
     for phase in phases:
         for item in phase:
             loads(*item, False).wait_send()
-    for i in range(6, 9):
+    for i in range(1, 9):
         peer_b(i).wait_send()
     for i in range(7):
         for cp in vstep(i):
             cp.wait_send()
 
-
-def rows_first(act, rows_block):
-    tok = act.shape[0]
-    return act.T.reshape(4, 2, 2, 2, rows_block // ROWS, ROWS, tok)
-
-
-def backward(low_ffn, cot, low_mid, low_pre, scaled, low_attn, low_in, lengths, q_win, k_win, v_win, d_att, stats,
-             w_qkv, tokens, gain, d_first, vec):
+    def share_wait(r, carry):
+        share(jnp.int32(0))[0][1].wait()
+        return carry
+
+    lax.fori_loop(0, rounds, share_wait, 0)
+
+
+def blocks_first(turned):
+    return turned.reshape(4, 2, 2, 2, turned.shape[0] // 32 // ROWS, ROWS, turned.shape[1])
+
+
+def fast_shards(
+    tokens, lengths, ln1_gain, ln1_bias, w_qkv, qv_bias, head_scale, w_out, out_bias, lnpa_gain, lnpa_bias,
+    ln2_gain, ln2_bias, w_fc1, fc1_bias, lnf_gain, lnf_bias, w_fc2, fc2_bias, cotangent,
+):
     tok, width = tokens.shape
+    ff = w_fc1.shape[1]
+    head_gain = jnp.repeat(head_scale, width // HEADS)
+    (low_in_t, q_win, k_win, v_win, att, lse, scaled_t, attn, first, low_mid_t, normed, slope, scale_ffn, low_ffn, low_ffn_t) = forward(
+        lengths, tokens, ln1_gain, ln1_bias, w_qkv, qv_bias, head_gain, w_out, out_bias, lnpa_gain, lnpa_bias, ln2_gain, ln2_bias,
+        w_fc1, fc1_bias, lnf_gain, lnf_bias)
     rounds = 24
     hbm, vmem = pl.BlockSpec(memory_space=pl.ANY), pl.BlockSpec(memory_space=pltpu.VMEM)
     a_shape = (14, 4, 2, 2, ROWS, tok)
     b_shape = (9, tok, WR)
     msgs = [(4, 2, ROWS, WX), (4, 2, ROWS, WX), (4, ROWS, WX), (4, ROWS, WX), (3, ROWS, 2 * WX), (3, ROWS, 2 * WX),
             (3, 2, 2, ROWS, WZ), (3, 2, 2, ROWS, WZ), (2, ROWS, WZ // 2), (2, ROWS, WZ // 2), (ROWS, WZ // 2), (ROWS, WZ // 2)]
-    v = vec.shape[0]
-    dma = pltpu.SemaphoreType.DMA
-    return pl.pallas_call(
+    sizes = (width, width, 2 * width) + (width,) * 7 + (ff, ff, ff)
+    v = -(-sum(sizes) // 8192) * 64
+    dma, shape = pltpu.SemaphoreType.DMA, jax.ShapeDtypeStruct
+    f32s = [(4, 2, ROWS, WX), (4, 2, ROWS, WX), (KEEP, 4, ROWS, 2 * WX), (2, 2, ROWS, WZ), (KEEP, 2, 2, ROWS, WZ // 2),
+            (KEEP, 4, ROWS, WX), (KEEP, 4, ROWS, WX), (rounds, ROWS, WR), (v, 128), (v, 128), (v // 2 + v // 4 + v // 8 * 5, 128)]
+    windows = [pltpu.VMEM((3, tok, width), BF16)] * 4 + [pltpu.VMEM((3, 2 * HEADS, tok), F32)]
+    more = [(3 * tok, tok), (tok, 2 * tok), (2 * width // HEADS, tok), (2, tok, width // HEADS), (2, tok, width // HEADS),
+            (tok, width), (tok, width), (tok, ff), (4, tok, 128)]
+    out2, out1, outo, outq, flat, grad_tokens, layer_out = pl.pallas_call(
         functools.partial(back_kernel, tok),
-        out_shape=[jax.ShapeDtypeStruct((rounds, ROWS, WR), F32), jax.ShapeDtypeStruct(vec.shape, F32),
-                   jax.ShapeDtypeStruct(tokens.shape, F32)],
-        in_specs=[hbm] * 7 + [pl.BlockSpec(memory_space=pltpu.SMEM)] + [vmem] * 5 + [hbm] + [vmem] * 4,
-        out_specs=[vmem] * 3,
+        out_shape=[shape((ff // 32, width), F32), shape((width // 32, ff), F32), shape((width // 32, width), F32),
+                   shape((width // 32, 3 * width), F32), shape((v, 128), F32), shape((tok, width), F32), shape((tok, width), BF16)],
+        in_specs=[hbm] * 5 + [pl.BlockSpec(memory_space=pltpu.SMEM)] + [hbm] * 3 + [vmem] * 12 + [hbm] * 7,
+        out_specs=[hbm] * 4 + [vmem] * 3,
         scratch_shapes=[pltpu.VMEM(a_shape, BF16), pltpu.VMEM(a_shape, BF16), pltpu.VMEM(b_shape, BF16), pltpu.VMEM(b_shape, BF16)]
-        + [pltpu.VMEM((SLOTS,) + m, BF16) for m in msgs]
+        + [pltpu.VMEM((SEND,) + m, BF16) for m in msgs]
         + [pltpu.VMEM((RECV,) + m, BF16) for m in msgs]
-        + [pltpu.VMEM((4, 2, ROWS, WX), F32), pltpu.VMEM((4, 2, ROWS, WX), F32), pltpu.VMEM((SLOTS, 4, ROWS, 2 * WX), F32),
-           pltpu.VMEM((2, 2, ROWS, WZ), F32), pltpu.VMEM((SLOTS, 2, 2, ROWS, WZ // 2), F32),
-           pltpu.VMEM((SLOTS, 4, ROWS, WX), F32), pltpu.VMEM((SLOTS, 4, ROWS, WX), F32),
-           pltpu.VMEM((v, 128), F32), pltpu.VMEM((v, 128), F32), pltpu.VMEM((v // 2 + v // 4 + v // 8 * 5, 128), F32),
-           pltpu.VMEM((width, 3 * width), BF16), pltpu.VMEM((3, tok, width), BF16), pltpu.VMEM((3, 2 * HEADS, tok), F32),
-           pltpu.VMEM((3 * tok, tok), F32), pltpu.VMEM((tok, 2 * tok), F32),
-           pltpu.VMEM((2 * width // HEADS, tok), F32), pltpu.VMEM((2, tok, width // HEADS), F32),
-           pltpu.VMEM((2, tok, width // HEADS), F32), pltpu.VMEM((tok, width), F32),
-           dma((20,)), dma((23,)), dma((23,)), dma((12, SLOTS)), dma((12, RECV)), dma((10,)), dma((10,)), dma((1,)), dma((6,)), dma((6,))],
-        compiler_params=pltpu.CompilerParams(collective_id=0, has_side_effects=True, vmem_limit_bytes=62 << 20),
-        cost_estimate=pl.CostEstimate(flops=20 << 30, bytes_accessed=30 << 20, transcendentals=4 << 20),
-    )(rows_first(low_ffn, 128), rows_first(low_mid, 32), rows_first(scaled, 32), rows_first(low_in, 32),
-      cot, low_pre, low_attn, lengths, q_win, k_win, v_win, d_att, stats, w_qkv, tokens, gain[None], d_first, vec)
-
-
-def fast_shards(
-    tokens, lengths, ln1_gain, ln1_bias, w_qkv, qv_bias, head_scale, w_out, out_bias, lnpa_gain, lnpa_bias,
-    ln2_gain, ln2_bias, w_fc1, fc1_bias, lnf_gain, lnf_bias, w_fc2, fc2_bias, cotangent,
-):
-    row_count, width = tokens.shape
-    head_dim = width // HEADS
-    inputs = tokens.astype(F32)
-    low_in, q_win, k_win, v_win, attended, log_total = attend(lengths, tokens, ln1_gain, ln1_bias, w_qkv, qv_bias)
-    head_gain = jnp.repeat(head_scale, head_dim)
-    scaled = (attended * head_gain).astype(BF16)
-    attn_out = dot32(scaled, w_out) + out_bias
-    branch, pa_back = jax.vjp(norm_rows, attn_out, lnpa_gain, lnpa_bias)
-    first_sum = inputs + branch
-    normed_mid, ln2_back = jax.vjp(norm_rows, first_sum, ln2_gain, ln2_bias)
-    low_mid = normed_mid.astype(BF16)
-    pre_act = dot32(low_mid, w_fc1) + fc1_bias
-    activated, gelu_back = jax.vjp(gelu_exact, pre_act)
-    ffn_normed, lnf_back = jax.vjp(norm_rows, activated, lnf_gain, lnf_bias)
-    low_ffn = ffn_normed.astype(BF16)
-    layer_out = (first_sum + dot32(low_ffn, w_fc2) + fc2_bias).astype(BF16)
-    d_output = cotangent.astype(F32)
-    grad_c2 = jnp.sum(d_output, axis=0)
-    d_ffn = over_cols(cotangent, w_fc2)
-    d_active, grad_lnf_gain, grad_lnf_bias = lnf_back(d_ffn)
-    (d_pre,) = gelu_back(d_active)
-    low_pre = d_pre.astype(BF16)
-    grad_c1 = jnp.sum(low_pre.astype(F32), axis=0)
-    d_mid = over_cols(low_pre, w_fc1)
-    d_first_norm, grad_ln2_gain, grad_ln2_bias = ln2_back(d_mid)
-    d_first = d_output + d_first_norm
-    d_attn, grad_pa_gain, grad_pa_bias = pa_back(d_first)
-    low_attn = d_attn.astype(BF16)
-    grad_bo = jnp.sum(low_attn.astype(F32), axis=0)
-    d_scaled = over_cols(low_attn, w_out)
-    grad_hs = jnp.sum((d_scaled * attended).reshape(row_count, HEADS, head_dim), axis=(0, 2))
-    d_attended = (d_scaled * head_gain).astype(BF16)
-    delta = jnp.sum((d_attended.astype(F32) * attended).reshape(row_count, HEADS, head_dim), axis=-1).T
-    stats = jnp.concatenate([log_total, delta], axis=0)
-    vectors = (grad_bo, grad_pa_gain, grad_pa_bias, grad_ln2_gain, grad_ln2_bias, grad_c1, grad_lnf_gain, grad_lnf_bias,
-               grad_c2, grad_hs)
-    flat = jnp.concatenate((jnp.zeros((4 * width,), F32),) + vectors)
-    flat = jnp.pad(flat, (0, 192 * 128 - flat.shape[0])).reshape(192, 128)
-    out, flat, grad_tokens = backward(
-        low_ffn, cotangent, low_mid, low_pre, scaled, low_attn, low_in, lengths, q_win, k_win, v_win, d_attended, stats,
-        w_qkv, tokens, ln1_gain, d_first, flat)
-    share_w2 = out[:8].reshape(128, WR)
-    share_w1 = out[8:16].reshape(4, 32, WR).transpose(1, 0, 2).reshape(32, 4 * WR)
-    share_wo = out[16:18].reshape(32, WR)
-    share_wqkv = out[18:24].reshape(3, 32, WR).transpose(1, 0, 2).reshape(32, 3 * WR)
+        + [pltpu.VMEM(m, F32) for m in f32s] + windows + [pltpu.VMEM(m, F32) for m in more]
+        + [pltpu.VMEM((tok, ff), BF16), pltpu.VMEM((PIECES, FC, width), BF16), pltpu.VMEM((PIECES, width, FC), BF16),
+           pltpu.VMEM((PIECES, tok, FC), BF16), pltpu.VMEM((PIECES, tok, FC), BF16),
+           dma((15,)), dma((23,)), dma((23,)), dma((12, SEND)), dma((12, RECV)), dma((10,)), dma((10,)), dma((6,)), dma((6,)),
+           dma((4,)), dma((PIECES,)), dma((PIECES,)), dma((PIECES,)), dma((PIECES,)), dma((1,))],
+        compiler_params=pltpu.CompilerParams(collective_id=0, has_side_effects=True, vmem_limit_bytes=63 << 20),
+        cost_estimate=pl.CostEstimate(flops=30 << 30, bytes_accessed=50 << 20, transcendentals=4 << 20),
+    )(blocks_first(low_ffn_t), blocks_first(low_mid_t), blocks_first(scaled_t), blocks_first(low_in_t),
+      cotangent, lengths, q_win, k_win, v_win, lse, att, attn, first, scale_ffn, tokens,
+      ln1_gain[None], lnpa_gain[None], ln2_gain[None], lnf_gain[None], head_gain[None], fc2_bias[None],
+      normed, slope, low_ffn, w_fc2, w_fc1, w_out, w_qkv)
     flat = flat.reshape(-1)
-    sizes = (width, width, 2 * width) + tuple(item.shape[0] for item in vectors)
     starts = [sum(sizes[:i]) for i in range(len(sizes))]
-    ln1g, ln1b, qv, bo, pag, pab, ln2g, ln2b, c1, lnfg, lnfb, c2, hs = (
+    ln1g, ln1b, qv, bo, pag, pab, ln2g, ln2b, c2, hs, c1, lnfg, lnfb = (
         lax.slice(flat, (start,), (start + size,)) for start, size in zip(starts, sizes))
-    return (layer_out, grad_tokens, ln1g, ln1b, share_wqkv, qv, hs, share_wo, bo, pag, pab, ln2g, ln2b, share_w1, c1,
-            lnfg, lnfb, share_w2, c2)
+    hs = jnp.sum(hs.reshape(HEADS, width // HEADS), axis=1)
+    return (layer_out, grad_tokens, ln1g, ln1b, outq, qv, hs, outo, bo, pag, pab, ln2g, ln2b, out1, c1, lnfg, lnfb, out2, c2)
 
 
 def shards(

time: 234 us -> 191 us (0.82)
  matrix products: 28.2 us -> 0 us
  other arithmetic: 12.6 us -> 0.63 us
  local copies, waits for them, and re-layouts: 23.2 us -> 12.8 us
  Pallas kernels: 168 us -> 177 us
    dot_general x6 -> x0, matrix products: 28.2 us -> none  [the longest x3 16.1 us: over_cols(): lax.dot_general(left, right, (((1,), (1,)), ((), ())), preferred_element_...]
    reduce_sum x11 -> x1, other arithmetic: 11.9 us -> 0.63 us  [fast_shards(): hs = jnp.sum(hs.reshape(HEADS, width // HEADS), axis=1)]
    pallas_call x2, Pallas kernels: 168 us -> 177 us  [the longest x1 140 us: fast_shards(): pl.pallas_call(functools.partial(back_kernel, tok), out_shape=[shape((ff...]
    transpose x3 -> x0, local copies, waits for them, and re-layouts: 6.12 us -> none  [rows_first(): return act.T.reshape(4, 2, 2, 2, rows_block // ROWS, ROWS, tok)]
    slice x3 -> x0, local copies, waits for them, and re-layouts: 4.84 us -> none  [the longest x1 2.26 us: fast_shards(): share_w2 = out[:8].reshape(128, WR)]
    unnamed x58 -> x14, local copies, waits for them, and re-layouts: 2.91 us -> 7.29 us
    mul x2 -> x0, local copies, waits for them, and re-layouts: 2.63 us -> none  [the longest x1 2.55 us: fast_shards(): d_attended.astype(F32) * attended]
    convert_element_type x1 -> x0, local copies, waits for them, and re-layouts: 2.46 us -> none  [fast_shards(): low_ffn = ffn_normed.astype(BF16)]
where the time goes in v2:
time: 191 us
  Pallas kernels  177 us (93%)
  local copies, waits for them, and re-layouts  12.8 us (7%)
    pallas_call x1, Pallas kernels, fast_shards(): pl.pallas_call(functools.partial(back_kernel, tok), out_shape=[shape((ff...  140 us
    pallas_call x1, Pallas kernels, forward(): pl.pallas_call(forward_kernel, out_shape=[shape((width, rows), BF16), sha...  36.4 us
    unnamed x14, local copies, waits for them, and re-layouts  7.29 us
    slice x3, local copies, waits for them, and re-layouts, fast_shards(): lax.slice(flat, (start,), (start + size,))  4.07 us

profile of v2, /device:TPU:0, one launch (start us, length us, event | category | flops | bytes accessed | tf_op | source)
XLA Modules:
  0.0 190.9 jit_solution(6100680090128771151)
XLA Ops:
  0.7 0.7 broadcast_in_dim.46
  1.4 0.7 broadcast_in_dim_reshape.4.head_gain
  2.1 36.4 %shard_map.339 = (bf16[1024,256]{1,0:T(8,128)(2,1)}, bf16[3,256,1024]{2,1,0:T(8,128)(2,1)}, bf16[3,256,1024]{2,1,0:T(8,128)(2,1)}, bf16[3,256,1024]{2,1,0:T(8,12...) custom-call(s32[1,5]{1,0:T(1,128)} %lens.3, ...), custom_call_target="tpu_custom_call" | custom-call | flops 12884901888 | bytes 41943040 | tf_op jit(solution)/shard_map/pallas_call | solution.py:342
  38.4 140.3 %shard_map.340 = (f32[128,1024]{1,0:T(8,128)}, f32[32,4096]{1,0:T(8,128)}, f32[32,1024]{1,0:T(8,128)}, f32[32,3072]{1,0:T(8,128)}, f32[192,128]{1,0:T(8,128)}, /...) custom-call(bf16[4,2,2,2,8,16,256]{6,5,4,3,2,1,0:T(8,128)(2,1)} %bitcast.56, bf16[4,2,2,2,2,16,256]{6,5,4,3,2,1,0:T(8,128)(2,1)} %bitcast.59, ...), custom_call_target="tpu_custom_call" | custom-call | flops 32212254720 | bytes 52428800 | tf_op jit(solution)/shard_map/pallas_call | solution.py:1055
  178.8 0.0 copy-start.2
  178.8 0.0 copy-start.3
  178.8 1.4 slice_bitcast_fusion.3
  180.1 1.3 slice_bitcast_fusion.4
  181.5 1.4 slice_bitcast_fusion
  182.9 0.1 reshape.72
  182.9 0.6 reduce_sum.9
  183.6 0.0 copy-start.1
  183.6 1.9 %copy.45 = bf16[256,1024]{1,0:T(8,128)(2,1)} copy(bf16[256,1024]{1,0:T(8,128)(2,1)} %get-tuple-element.94) | data formatting | bytes 1048576
  185.5 0.0 copy-start
  185.5 2.4 %copy.46 = f32[256,1024]{1,0:T(8,128)} copy(f32[256,1024]{1,0:T(8,128)} %get-tuple-element.95) | data formatting | bytes 2097152
  187.9 0.0 copy-done.2
  187.9 0.7 copy.47
  188.6 0.0 copy-done.3
  188.6 0.7 copy.48
  189.3 0.0 copy-done.1
  189.3 0.8 copy.49
  190.1 0.0 copy-done
  190.1 0.8 copy.50
Async XLA Ops:
  178.8 9.1 %copy-start.2 = (f32[32,3072]{1,0:T(8,128)S(1)}, f32[32,3072]{1,0:T(8,128)}, u32[]{:S(2)}) copy-start(f32[32,3072]{1,0:T(8,128)} %get-tuple-element.98) | copy-start | bytes 1179652
  178.8 9.8 %copy-start.3 = (f32[32,1024]{1,0:T(8,128)S(1)}, f32[32,1024]{1,0:T(8,128)}, u32[]{:S(2)}) copy-start(f32[32,1024]{1,0:T(8,128)} %get-tuple-element.101) | copy-start | bytes 393220
  183.6 5.7 %copy-start.1 = (f32[32,4096]{1,0:T(8,128)S(1)}, f32[32,4096]{1,0:T(8,128)}, u32[]{:S(2)}) copy-start(f32[32,4096]{1,0:T(8,128)} %get-tuple-element.107) | copy-start | bytes 1572868
  185.5 4.6 %copy-start = (f32[128,1024]{1,0:T(8,128)S(1)}, f32[128,1024]{1,0:T(8,128)}, u32[]{:S(2)}) copy-start(f32[128,1024]{1,0:T(8,128)} %get-tuple-element.111) | copy-start | bytes 1572868

commit v3 on v2

--- a/solution.py
+++ b/solution.py
@@ -75,10 +75,18 @@
     return total
 
 
+def head_row(scales, width):
+    head_of = lax.broadcasted_iota(jnp.int32, (1, width), 1) // (width // HEADS)
+    row = jnp.full((1, width), scales[0, 0], F32)
+    for h in range(1, HEADS):
+        row = jnp.where(head_of == h, scales[0, h], row)
+    return row
+
+
 FC = 512
 
 
-def forward_kernel(lens, tok, gain, bias, w_hbm, qv_bias, head_gain, wo_hbm, out_bias, pa_gain, pa_bias, mid_gain, mid_bias,
+def forward_kernel(lens, tok, gain, bias, w_hbm, qv_bias, head_scale, wo_hbm, out_bias, pa_gain, pa_bias, mid_gain, mid_bias,
                    w1_hbm, fc1_bias, ffn_gain, ffn_bias,
                    low_in_t, qw_out, kw_out, vw_out, att_out, lse, scaled_t, attn_out, first_out, low_mid_t, normed_out, slope_out,
                    scale_out, low_ffn_out, low_ffn_t,
@@ -252,7 +260,7 @@
     emit(qw, qw_out)
     emit(att, att_out)
 
-    scaled = (att[...] * head_gain[...]).astype(BF16)
+    scaled = (att[...] * head_row(head_scale, width)).astype(BF16)
     loads[6].wait()
     attn[...] = dot32(scaled, wo[...]) + out_bias[...]
     emit(attn, attn_out)
@@ -331,11 +339,11 @@
         cp.wait()
 
 
-def forward(lengths, tokens, ln1_gain, ln1_bias, w_qkv, qv_bias, head_gain, w_out, out_bias, pa_gain, pa_bias, mid_gain, mid_bias,
+def forward(lengths, tokens, ln1_gain, ln1_bias, w_qkv, qv_bias, head_scale, w_out, out_bias, pa_gain, pa_bias, mid_gain, mid_bias,
             w_fc1, fc1_bias, ffn_gain, ffn_bias):
     rows, width = tokens.shape
     ff = w_fc1.shape[1]
-    vmem, hbm = pl.BlockSpec(memory_space=pltpu.VMEM), pl.BlockSpec(memory_space=pl.ANY)
+    hbm, vmem, smem = (pl.BlockSpec(memory_space=space) for space in (pl.ANY, pltpu.VMEM, pltpu.SMEM))
     shape = jax.ShapeDtypeStruct
     window, wide, tall = (3, rows, width), (rows, ff), (ff, rows)
     dma = pltpu.SemaphoreType.DMA
@@ -345,7 +353,7 @@
                    shape((rows, width), F32), shape((HEADS, rows), F32), shape((width, rows), BF16), shape((rows, width), F32),
                    shape((rows, width), F32), shape((width, rows), BF16), shape(wide, BF16), shape(wide, BF16),
                    shape((rows, 128), F32), shape(wide, BF16), shape(tall, BF16)],
-        in_specs=[pl.BlockSpec(memory_space=pltpu.SMEM), vmem, vmem, vmem, hbm, vmem, vmem, hbm] + [vmem] * 5 + [hbm] + [vmem] * 3,
+        in_specs=[smem, vmem, vmem, vmem, hbm, vmem, smem, hbm] + [vmem] * 5 + [hbm] + [vmem] * 3,
         out_specs=[hbm] * 5 + [vmem] + [hbm] * 6 + [vmem] + [hbm] * 2,
         scratch_shapes=[pltpu.VMEM((width, 3 * width), BF16), pltpu.VMEM((width, width), BF16), pltpu.VMEM((width, ff), BF16),
                         pltpu.VMEM((rows, width), BF16), pltpu.VMEM((rows, width), BF16), pltpu.VMEM((rows, width), BF16),
@@ -357,7 +365,7 @@
                         pltpu.VMEM(tall, BF16), dma((8,)), dma((8,)), dma((8,)), dma((13,))],
         compiler_params=pltpu.CompilerParams(collective_id=1, has_side_effects=True, vmem_limit_bytes=60 << 20),
         cost_estimate=pl.CostEstimate(flops=12 << 30, bytes_accessed=40 << 20, transcendentals=5 << 20),
-    )(lengths, tokens, ln1_gain[None], ln1_bias[None], w_qkv, qv_bias[None], head_gain[None], w_out, out_bias[None],
+    )(lengths, tokens, ln1_gain[None], ln1_bias[None], w_qkv, qv_bias[None], head_scale[None], w_out, out_bias[None],
       pa_gain[None], pa_bias[None], mid_gain[None], mid_bias[None], w_fc1, fc1_bias[None], ffn_gain[None], ffn_bias[None])
 
 
@@ -366,12 +374,12 @@
 KEEP = 8
 LAG_XY = (0, 2, 4, 6, 8, 10)
 LAG_Z = (0, 2, 4, 6, 8, 10)
-PAIR0 = 9
+MIDDLE = 6
 PIECES = 3
 
 
 def back_kernel(tok, a2, a1, ao, aq, cot, lens, qw_in, kw_in, vw_in, lse, att, attn, first, scale_ffn, tokens,
-                gain, pa_gain, mid_gain, ffn_gain, head_gain, fc2_bias, normed_in, slope_in, low_ffn_in, w2_in, w1_in, wo_in, wq_in,
+                gain, pa_gain, mid_gain, ffn_gain, head_scale, fc2_bias, normed_in, slope_in, low_ffn_in, w2_in, w1_in, wo_in, wq_in,
                 out2, out1, outo, outq, vout, grad_tok, layer_out,
                 am, ap, bm, bp, s1x, s1y, s2x, s2y, sr, sl, szr, szl, szx, szy, swx, swy,
                 r1x, r1y, r2x, r2y, rr, rl, rzr, rzl, rzx, rzy, rwx, rwy,
@@ -424,16 +432,20 @@
     z_devs = [((dp + 2 * k) % 8, blk) for k in range(1, 4)]
     for dev in [core_dev, x_dev, y_dev] + z_devs:
         pl.semaphore_signal(bar, inc=1, device_id=dev, device_id_type=MESH)
-    pl.semaphore_wait(bar, 6)
-
     def remote(src, dst, ssem, rsem, dev):
         return pltpu.make_async_remote_copy(src, dst, ssem, rsem, device_id=dev, device_id_type=MESH)
 
-    def window(kind):
-        src, dst, dev = {"cross": (0, 2, y_dev), "own": (0, 1, core_dev), "relay": (2, 1, core_dev)}[kind]
-        k = {"cross": 0, "own": 2, "relay": 4}[kind]
-        return [remote(dow.at[src], dow.at[dst], asend.at[k], arecv.at[k], dev),
-                remote(stw.at[src], stw.at[dst], asend.at[k + 1], arecv.at[k + 1], dev)]
+    def window_rows(kind):
+        src, dst, dev, k = {"cross": (0, 2, y_dev, 0), "own": (0, 1, core_dev, 1), "relay": (2, 1, core_dev, 2)}[kind]
+        copies = [remote(stw.at[src], stw.at[dst], asend.at[k], arecv.at[k], dev)]
+        if kind == "own":
+            copies.append(remote(dow.at[src], dow.at[dst], asend.at[3], arecv.at[3], dev))
+        return copies
+
+    def window_piece(kind, i):
+        src, dst, dev, k = {"cross": (0, 2, y_dev, 4), "relay": (2, 1, core_dev, 4 + HEADS // 2)}[kind]
+        cols = pl.ds(pl.multiple_of(i * 2 * dim, 2 * dim), 2 * dim)
+        return remote(dow.at[src, :, cols], dow.at[dst, :, cols], asend.at[k + i], arecv.at[k + i], dev)
 
     a_src = [(a2, g) for g in range(8)] + [(a1, 0), (a1, 1), (ao, 0), (ao, 1), (aq, 0), (aq, 1)]
     b_src = [(cot, 0)]
@@ -455,7 +467,6 @@
     phases = [([("b", 0)] + [("a", g) for g in range(8)]), [("a", 8), ("a", 9)], [("a", 10), ("a", 11), ("a", 12), ("a", 13)]]
     for item in phases[0]:
         loads(*item, True).start()
-        loads(*item, False).start()
     normed_load.start()
     for j in range(PIECES):
         for cp in piece2(j):
@@ -463,7 +474,6 @@
     for phase in phases[1:]:
         for item in phase:
             loads(*item, True).start()
-            loads(*item, False).start()
     for j in range(PIECES):
         start_col(j)
         piece_slope(j).start()
@@ -488,6 +498,11 @@
     q_spots = (blk + 1) * rows + lax.broadcasted_iota(jnp.int32, (1, 2 * rows), 1)
     k_spots = blk * rows + lax.broadcasted_iota(jnp.int32, (rows, 1), 0)
     mask_q[...] = jnp.where(k_spots >= sequence_starts(lens, q_spots), 0.0, -1e30)
+
+    pl.semaphore_wait(bar, 6)
+    for phase in phases:
+        for item in phase:
+            loads(*item, False).start()
 
     def place(r):
         g = jnp.where(r < 8, r, jnp.where(r < 16, 8 + r % 2, jnp.where(r < 18, 10 + r % 2, 12 + r % 2)))
@@ -718,94 +733,132 @@
             for cp in vstep(i):
                 cp.start()
 
-    def windows_arrive():
+    def rows_arrive():
         for cp in early:
             cp.wait()
 
+    def cross_arrive():
         @pl.when(y == 0)
         def _():
-            for cp in window("cross"):
+            for cp in window_rows("cross"):
                 cp.wait_recv()
 
         @pl.when((y == 0) & (c == 0))
         def _():
-            for cp in window("relay"):
+            for cp in window_rows("relay"):
                 cp.start()
 
         @pl.when(c == 0)
         def _():
-            for cp in window("own"):
+            for cp in window_rows("own"):
                 cp.wait_recv()
 
         @pl.when((y == 0) & (c == 1))
         def _():
-            for cp in window("relay"):
+            for cp in window_rows("relay"):
                 cp.wait_recv()
+
+    def cross_send(i):
+        @pl.when(y == 1)
+        def _():
+            window_piece("cross", i).start()
+
+    def cross_relay(i):
+        @pl.when(y == 0)
+        def _():
+            window_piece("cross", i).wait_recv()
+
+        @pl.when((y == 0) & (c == 0))
+        def _():
+            window_piece("relay", i).start()
 
     def windows_drain():
         @pl.when(y == 1)
         def _():
-            for cp in window("cross"):
+            for cp in window_rows("cross"):
                 cp.wait_send()
+            for i in range(HEADS // 2):
+                window_piece("cross", i).wait_send()
 
         @pl.when(c == 1)
         def _():
-            for cp in window("own"):
+            for cp in window_rows("own"):
                 cp.wait_send()
 
         @pl.when((y == 0) & (c == 0))
         def _():
-            for cp in window("relay"):
+            for cp in window_rows("relay"):
                 cp.wait_send()
-
-    def attend_back(i):
+            for i in range(HEADS // 2):
+                window_piece("relay", i).wait_send()
+
+    def attend_pairs(i, kj, qj, bias, to_q, to_k, first):
         cols = pl.ds(pl.multiple_of(i * 2 * dim, 2 * dim), 2 * dim)
-
-        def pairs(kj, qj, bias, to_q, to_k, first):
-            k2, v2, q2, d2 = kw[kj, :, cols], vw[kj, :, cols], qw[qj, :, cols], dow[qj, :, cols]
-            for sub in range(2):
-                part = slice(sub * dim, (sub + 1) * dim)
-                k1, v1, q1, d1 = k2[:, part], v2[:, part], q2[:, part], d2[:, part]
-                log_total = stw[qj, pl.ds(2 * i + sub, 1)]
-                delta = stw[qj, pl.ds(HEADS + 2 * i + sub, 1)]
-                probs = jnp.exp(dot_nt(k1, q1) + bias[...] - log_total)
-                low_s = (probs * (dot_nt(v1, d1) - delta)).astype(BF16)
-                if to_q:
-                    term = dot_tn(k1, low_s)
-                    dqa[part] = term if first else dqa[part] + term
-                if to_k:
-                    term = dot32(low_s, q1)
-                    dka[sub] = term if first else dka[sub] + term
-                    term = dot32(probs.astype(BF16), d1)
-                    dva[sub] = term if first else dva[sub] + term
-
-        pairs(2, 0, mask.at[2 * rows:3 * rows], True, True, True)
+        k2, v2, q2, d2 = kw[kj, :, cols], vw[kj, :, cols], qw[qj, :, cols], dow[qj, :, cols]
+        for sub in range(2):
+            part = slice(sub * dim, (sub + 1) * dim)
+            k1, v1, q1, d1 = k2[:, part], v2[:, part], q2[:, part], d2[:, part]
+            log_total = stw[qj, pl.ds(2 * i + sub, 1)]
+            delta = stw[qj, pl.ds(HEADS + 2 * i + sub, 1)]
+            probs = jnp.exp(dot_nt(k1, q1) + bias[...] - log_total)
+            low_s = (probs * (dot_nt(v1, d1) - delta)).astype(BF16)
+            if to_q:
+                term = dot_tn(k1, low_s)
+                dqa[part] = term if first else dqa[part] + term
+            if to_k:
+                term = dot32(low_s, q1)
+                dka[sub] = term if first else dka[sub] + term
+                term = dot32(probs.astype(BF16), d1)
+                dva[sub] = term if first else dva[sub] + term
+
+    def attend_near(i):
+        cols = pl.ds(pl.multiple_of(i * 2 * dim, 2 * dim), 2 * dim)
+        attend_pairs(i, 2, 0, mask.at[2 * rows:3 * rows], True, True, True)
 
         @pl.when(blk >= 1)
         def _():
-            pairs(1, 0, mask.at[rows:2 * rows], True, False, False)
+            attend_pairs(i, 1, 0, mask.at[rows:2 * rows], True, False, False)
 
         @pl.when(blk >= 2)
         def _():
-            pairs(0, 0, mask.at[0:rows], True, False, False)
+            attend_pairs(i, 0, 0, mask.at[0:rows], True, False, False)
+
+        bm[6, :, cols] = (dqa[...].T * (dim ** -0.5)).astype(BF16)
+        d_ffn[:, cols] = jnp.concatenate([dka[0], dka[1]], axis=1)
+        d_ffn[:, pl.ds(pl.multiple_of(width + i * 2 * dim, 2 * dim), 2 * dim)] = jnp.concatenate([dva[0], dva[1]], axis=1)
+
+    def attend_far(i):
+        cols = pl.ds(pl.multiple_of(i * 2 * dim, 2 * dim), 2 * dim)
+        dk_sum, dv_sum = d_ffn[:, cols], d_ffn[:, pl.ds(pl.multiple_of(width + i * 2 * dim, 2 * dim), 2 * dim)]
+
+        @pl.when(blk == 3)
+        def _():
+            bm[7, :, cols] = dk_sum.astype(BF16)
+            bm[8, :, cols] = dv_sum.astype(BF16)
+
+        @pl.when((y == 0) & (c == 1))
+        def _():
+            window_piece("relay", i).wait_recv()
 
         @pl.when(blk <= 2)
         def _():
-            pairs(2, 1, mask_q.at[:, 0:rows], False, True, False)
+            attend_pairs(i, 2, 1, mask_q.at[:, 0:rows], False, True, True)
 
         @pl.when(blk <= 1)
         def _():
-            pairs(2, 2, mask_q.at[:, rows:2 * rows], False, True, False)
-
-        bm[6, :, cols] = (dqa[...].T * (dim ** -0.5)).astype(BF16)
-        bm[7, :, cols] = jnp.concatenate([dka[0], dka[1]], axis=1).astype(BF16)
-        bm[8, :, cols] = jnp.concatenate([dva[0], dva[1]], axis=1).astype(BF16)
-
-    V_IN_GAIN, V_IN_BIAS, V_QV, V_OUT, V_PA_GAIN, V_PA_BIAS, V_MID_GAIN, V_MID_BIAS, V_FC2, V_HEADS = (
-        k * (width // 128) for k in (0, 1, 2, 4, 5, 6, 7, 8, 9, 10))
-    V_FC1 = 11 * (width // 128)
+            attend_pairs(i, 2, 2, mask_q.at[:, rows:2 * rows], False, True, False)
+
+        @pl.when(blk <= 2)
+        def _():
+            bm[7, :, cols] = (dk_sum + jnp.concatenate([dka[0], dka[1]], axis=1)).astype(BF16)
+            bm[8, :, cols] = (dv_sum + jnp.concatenate([dva[0], dva[1]], axis=1)).astype(BF16)
+
+    V_IN_GAIN, V_IN_BIAS, V_QV, V_OUT, V_PA_GAIN, V_PA_BIAS, V_MID_GAIN, V_MID_BIAS, V_FC2 = (
+        k * (width // 128) for k in (0, 1, 2, 4, 5, 6, 7, 8, 9))
+    V_FC1 = 10 * (width // 128)
     V_FFN_GAIN = V_FC1 + ff // 128
     V_FFN_BIAS = V_FFN_GAIN + ff // 128
+    V_HEADS = V_FFN_BIAS + ff // 128
 
     def put_row(first_row, row):
         for k in range(row.shape[1] // 128):
@@ -895,25 +948,29 @@
         for k in range(n_o):
             start_col(n_ff + k + PIECES)
         attended = att[...]
-        put_row(V_HEADS, jnp.sum(total[...] * attended, axis=0, keepdims=True))
-        low = (total[...] * head_gain[...]).astype(BF16)
+        low = (total[...] * head_row(head_scale, width)).astype(BF16)
         dow[0] = low
         both = low.astype(F32) * attended
         high = both.astype(BF16)
         rest = (both - high.astype(F32)).astype(BF16)
         head_of = lax.broadcasted_iota(jnp.int32, (HEADS, width), 1) // dim
         pick = jnp.where(head_of == lax.broadcasted_iota(jnp.int32, (HEADS, width), 0), 1.0, 0.0).astype(BF16)
+        by_column = jnp.broadcast_to(jnp.sum(total[...] * attended, axis=0, keepdims=True), (8, width))
+        high_sum = by_column.astype(BF16)
+        rest_sum = (by_column - high_sum.astype(F32)).astype(BF16)
+        by_head = dot_nt(high_sum, pick) + dot_nt(rest_sum, pick)
+        vec[V_HEADS:V_HEADS + 1, 0:HEADS] = by_head[0:1]
         stw[0, 0:HEADS] = lse[...]
         stw[0, HEADS:2 * HEADS] = dot_nt(pick, high) + dot_nt(pick, rest)
 
         @pl.when(y == 1)
         def _():
-            for cp in window("cross"):
+            for cp in window_rows("cross"):
                 cp.start()
 
         @pl.when(c == 1)
         def _():
-            for cp in window("own"):
+            for cp in window_rows("own"):
                 cp.start()
 
     def input_first():
@@ -941,7 +998,7 @@
                 ((r >= 18) & (r < rounds), pltpu.make_async_copy(out.at[r], outq.at[half, pl.ds((r - 18) // 2 * WR, WR)], out_sem.at[0]))]
 
     n_pairs = HEADS // 2
-    after = PAIR0 + n_pairs
+    after = MIDDLE + n_pairs + 3
     plan = sorted(list(zip(LAG_XY, (xy0, xy1, xy2, xy3, xy4, xy5))) + list(zip(LAG_Z, (z0, z1, z2, z3, z4, z5))),
                   key=lambda item: -item[0])
     last = max(LAG_XY + LAG_Z)
@@ -978,23 +1035,42 @@
                 pl.when(here)(cp.start)
 
         at_slot(s, 0, normed_load.wait)
-        for u in range(2):
-            @pl.when(s < 4)
+        for u in range(3):
+            j = 3 * s + u
+
+            @pl.when(j < n_ff)
             def _():
-                ffn_first(2 * s + u)
-
-            @pl.when((s >= 4) & (s < 8))
+                ffn_first(j)
+
+        at_slot(s, 2, ffn_between)
+        for u in range(3):
+            j = 3 * (s - 3) + u
+
+            @pl.when((j >= 0) & (j < n_ff))
             def _():
-                ffn_second(2 * (s - 4) + u)
-
-        at_slot(s, 3, ffn_between)
-        at_slot(s, 8, middle_first)
-        at_slot(s, 8, middle_second)
-        at_slot(s, PAIR0, windows_arrive)
-
-        @pl.when((s >= PAIR0) & (s < after))
-        def _():
-            attend_back(s - PAIR0)
+                ffn_second(j)
+
+        at_slot(s, MIDDLE, middle_first)
+        at_slot(s, MIDDLE, middle_second)
+        at_slot(s, MIDDLE, rows_arrive)
+        at_slot(s, MIDDLE + 2, cross_arrive)
+        i = s - MIDDLE
+
+        @pl.when((i >= 0) & (i < n_pairs))
+        def _():
+            cross_send(i)
+
+        @pl.when((i >= 1) & (i < n_pairs + 1))
+        def _():
+            attend_near(i - 1)
+
+        @pl.when((i >= 2) & (i < n_pairs + 2))
+        def _():
+            cross_relay(i - 2)
+
+        @pl.when((i >= 3) & (i < n_pairs + 3))
+        def _():
+            attend_far(i - 3)
 
         at_slot(s, after - 1, input_first)
         at_slot(s, after, input_second)
@@ -1028,24 +1104,69 @@
     return turned.reshape(4, 2, 2, 2, turned.shape[0] // 32 // ROWS, ROWS, turned.shape[1])
 
 
+def finish_kernel(n_big, rows_of, *refs):
+    n_vec = len(rows_of)
+    n_in = n_big + 1
+    big = refs[:n_in]
+    out_big, out_vec = refs[n_in:n_in + n_big], refs[n_in + n_big:n_in + n_big + n_vec]
+    out_heads = refs[n_in + n_big + n_vec]
+    held, in_sem, out_sem = refs[n_in + n_big + n_vec + 1:-2], refs[-2], refs[-1]
+    loads = [pltpu.make_async_copy(src, dst, in_sem.at[k]) for k, (src, dst) in enumerate(zip(big, held))]
+    for cp in loads:
+        cp.start()
+    stores = [[pltpu.make_async_copy(src, dst, out_sem.at[k])] for k, (src, dst) in enumerate(zip(held, out_big))]
+    stores.append([pltpu.make_async_copy(held[-1].at[pl.ds(first, count)], dst, out_sem.at[n_big + k])
+                   for k, ((first, count), dst) in enumerate(zip(rows_of, out_vec))])
+    for load, group in zip(loads, stores):
+        load.wait()
+        for cp in group:
+            cp.start()
+    at = sum(rows_of[-1])
+    out_heads[...] = held[-1][at:at + 1, 0:HEADS]
+    for group in stores:
+        for cp in group:
+            cp.wait()
+
+
+def finish(layer_out, grad_tokens, out2, out1, outo, outq, flat, sizes):
+    big = (layer_out, grad_tokens, out2, out1, outo, outq)
+    rows_of, at = [], 0
+    for size in sizes:
+        rows_of.append((at, size // 128))
+        at += size // 128
+    hbm, vmem = pl.BlockSpec(memory_space=pl.ANY), pl.BlockSpec(memory_space=pltpu.VMEM)
+    res = pl.pallas_call(
+        functools.partial(finish_kernel, len(big), tuple(rows_of)),
+        out_shape=[jax.ShapeDtypeStruct(item.shape, item.dtype) for item in big]
+        + [jax.ShapeDtypeStruct((count, 128), F32) for _, count in rows_of] + [jax.ShapeDtypeStruct((1, HEADS), F32)],
+        in_specs=[hbm] * (len(big) + 1),
+        out_specs=[hbm] * (len(big) + len(rows_of)) + [vmem],
+        scratch_shapes=[pltpu.VMEM(item.shape, item.dtype) for item in big + (flat,)]
+        + [pltpu.SemaphoreType.DMA((len(big) + 1,)), pltpu.SemaphoreType.DMA((len(big) + len(rows_of),))],
+    )(*big, flat)
+    layer_out, grad_tokens, out2, out1, outo, outq = res[:6]
+    ln1g, ln1b, qv, bo, pag, pab, ln2g, ln2b, c2, c1, lnfg, lnfb = (item.reshape(-1) for item in res[6:-1])
+    return (layer_out, grad_tokens, ln1g, ln1b, outq, qv, res[-1].reshape(-1), outo, bo, pag, pab, ln2g, ln2b, out1, c1, lnfg, lnfb,
+            out2, c2)
+
+
 def fast_shards(
     tokens, lengths, ln1_gain, ln1_bias, w_qkv, qv_bias, head_scale, w_out, out_bias, lnpa_gain, lnpa_bias,
     ln2_gain, ln2_bias, w_fc1, fc1_bias, lnf_gain, lnf_bias, w_fc2, fc2_bias, cotangent,
 ):
     tok, width = tokens.shape
     ff = w_fc1.shape[1]
-    head_gain = jnp.repeat(head_scale, width // HEADS)
     (low_in_t, q_win, k_win, v_win, att, lse, scaled_t, attn, first, low_mid_t, normed, slope, scale_ffn, low_ffn, low_ffn_t) = forward(
-        lengths, tokens, ln1_gain, ln1_bias, w_qkv, qv_bias, head_gain, w_out, out_bias, lnpa_gain, lnpa_bias, ln2_gain, ln2_bias,
+        lengths, tokens, ln1_gain, ln1_bias, w_qkv, qv_bias, head_scale, w_out, out_bias, lnpa_gain, lnpa_bias, ln2_gain, ln2_bias,
         w_fc1, fc1_bias, lnf_gain, lnf_bias)
     rounds = 24
-    hbm, vmem = pl.BlockSpec(memory_space=pl.ANY), pl.BlockSpec(memory_space=pltpu.VMEM)
+    hbm, vmem, smem = (pl.BlockSpec(memory_space=space) for space in (pl.ANY, pltpu.VMEM, pltpu.SMEM))
     a_shape = (14, 4, 2, 2, ROWS, tok)
     b_shape = (9, tok, WR)
     msgs = [(4, 2, ROWS, WX), (4, 2, ROWS, WX), (4, ROWS, WX), (4, ROWS, WX), (3, ROWS, 2 * WX), (3, ROWS, 2 * WX),
             (3, 2, 2, ROWS, WZ), (3, 2, 2, ROWS, WZ), (2, ROWS, WZ // 2), (2, ROWS, WZ // 2), (ROWS, WZ // 2), (ROWS, WZ // 2)]
-    sizes = (width, width, 2 * width) + (width,) * 7 + (ff, ff, ff)
-    v = -(-sum(sizes) // 8192) * 64
+    sizes = (width, width, 2 * width) + (width,) * 6 + (ff, ff, ff)
+    v = -(-(sum(sizes) + 128) // 8192) * 64
     dma, shape = pltpu.SemaphoreType.DMA, jax.ShapeDtypeStruct
     f32s = [(4, 2, ROWS, WX), (4, 2, ROWS, WX), (KEEP, 4, ROWS, 2 * WX), (2, 2, ROWS, WZ), (KEEP, 2, 2, ROWS, WZ // 2),
             (KEEP, 4, ROWS, WX), (KEEP, 4, ROWS, WX), (rounds, ROWS, WR), (v, 128), (v, 128), (v // 2 + v // 4 + v // 8 * 5, 128)]
@@ -1056,7 +1177,7 @@
         functools.partial(back_kernel, tok),
         out_shape=[shape((ff // 32, width), F32), shape((width // 32, ff), F32), shape((width // 32, width), F32),
                    shape((width // 32, 3 * width), F32), shape((v, 128), F32), shape((tok, width), F32), shape((tok, width), BF16)],
-        in_specs=[hbm] * 5 + [pl.BlockSpec(memory_space=pltpu.SMEM)] + [hbm] * 3 + [vmem] * 12 + [hbm] * 7,
+        in_specs=[hbm] * 5 + [smem] + [hbm] * 3 + [vmem] * 10 + [smem, vmem] + [hbm] * 7,
         out_specs=[hbm] * 4 + [vmem] * 3,
         scratch_shapes=[pltpu.VMEM(a_shape, BF16), pltpu.VMEM(a_shape, BF16), pltpu.VMEM(b_shape, BF16), pltpu.VMEM(b_shape, BF16)]
         + [pltpu.VMEM((SEND,) + m, BF16) for m in msgs]
@@ -1064,20 +1185,15 @@
         + [pltpu.VMEM(m, F32) for m in f32s] + windows + [pltpu.VMEM(m, F32) for m in more]
         + [pltpu.VMEM((tok, ff), BF16), pltpu.VMEM((PIECES, FC, width), BF16), pltpu.VMEM((PIECES, width, FC), BF16),
            pltpu.VMEM((PIECES, tok, FC), BF16), pltpu.VMEM((PIECES, tok, FC), BF16),
-           dma((15,)), dma((23,)), dma((23,)), dma((12, SEND)), dma((12, RECV)), dma((10,)), dma((10,)), dma((6,)), dma((6,)),
+           dma((15,)), dma((23,)), dma((23,)), dma((12, SEND)), dma((12, RECV)), dma((10,)), dma((10,)), dma((4 + HEADS,)), dma((4 + HEADS,)),
            dma((4,)), dma((PIECES,)), dma((PIECES,)), dma((PIECES,)), dma((PIECES,)), dma((1,))],
         compiler_params=pltpu.CompilerParams(collective_id=0, has_side_effects=True, vmem_limit_bytes=63 << 20),
         cost_estimate=pl.CostEstimate(flops=30 << 30, bytes_accessed=50 << 20, transcendentals=4 << 20),
     )(blocks_first(low_ffn_t), blocks_first(low_mid_t), blocks_first(scaled_t), blocks_first(low_in_t),
       cotangent, lengths, q_win, k_win, v_win, lse, att, attn, first, scale_ffn, tokens,
-      ln1_gain[None], lnpa_gain[None], ln2_gain[None], lnf_gain[None], head_gain[None], fc2_bias[None],
+      ln1_gain[None], lnpa_gain[None], ln2_gain[None], lnf_gain[None], head_scale[None], fc2_bias[None],
       normed, slope, low_ffn, w_fc2, w_fc1, w_out, w_qkv)
-    flat = flat.reshape(-1)
-    starts = [sum(sizes[:i]) for i in range(len(sizes))]
-    ln1g, ln1b, qv, bo, pag, pab, ln2g, ln2b, c2, hs, c1, lnfg, lnfb = (
-        lax.slice(flat, (start,), (start + size,)) for start, size in zip(starts, sizes))
-    hs = jnp.sum(hs.reshape(HEADS, width // HEADS), axis=1)
-    return (layer_out, grad_tokens, ln1g, ln1b, outq, qv, hs, outo, bo, pag, pab, ln2g, ln2b, out1, c1, lnfg, lnfb, out2, c2)
+    return finish(layer_out, grad_tokens, out2, out1, outo, outq, flat, sizes)
 
 
 def shards(

time: 191 us -> 172 us (0.901)
  local copies, waits for them, and re-layouts: 12.8 us -> 0 us
  Pallas kernels: 177 us -> 171 us
    pallas_call x1, Pallas kernels: 140 us -> 130 us  [fast_shards(): pl.pallas_call(functools.partial(back_kernel, tok), out_shape=[shape((ff...]
    unnamed x14 -> x0, local copies, waits for them, and re-layouts: 7.29 us -> none
    slice x3 -> x0, local copies, waits for them, and re-layouts: 4.07 us -> none  [fast_shards(): lax.slice(flat, (start,), (start + size,))]
    pallas_call x0 -> x1, Pallas kernels: none -> 3.65 us  [finish(): pl.pallas_call(functools.partial(finish_kernel, len(big), tuple(rows_of))...]
where the time goes in v3:
time: 172 us; the launch traced here: 171 us
  Pallas kernels  171 us (99%)
    pallas_call x1, Pallas kernels, fast_shards(): pl.pallas_call(functools.partial(back_kernel, tok), out_shape=[shape((ff...  130 us
    pallas_call x1, Pallas kernels, forward(): pl.pallas_call(forward_kernel, out_shape=[shape((width, rows), BF16), sha...  36.5 us
    pallas_call x1, Pallas kernels, finish(): pl.pallas_call(functools.partial(finish_kernel, len(big), tuple(rows_of))...  3.65 us

profile of v3, /device:TPU:0, one launch (start us, length us, event | category | flops | bytes accessed | tf_op | source)
XLA Modules:
  0.0 171.4 jit_solution(16311028107835846272)
XLA Ops:
  0.7 36.5 %shard_map.339 = (bf16[1024,256]{1,0:T(8,128)(2,1)}, bf16[3,256,1024]{2,1,0:T(8,128)(2,1)}, bf16[3,256,1024]{2,1,0:T(8,128)(2,1)}, bf16[3,256,1024]{2,1,0:T(8,12...) custom-call(s32[1,5]{1,0:T(1,128)} %lens.3, ...), custom_call_target="tpu_custom_call" | custom-call | flops 12884901888 | bytes 41943040 | tf_op jit(solution)/shard_map/pallas_call | solution.py:350
  37.1 130.4 %shard_map.340 = (f32[128,1024]{1,0:T(8,128)}, f32[32,4096]{1,0:T(8,128)}, f32[32,1024]{1,0:T(8,128)}, f32[32,3072]{1,0:T(8,128)}, f32[192,128]{1,0:T(8,128)}, /...) custom-call(bf16[4,2,2,2,8,16,256]{6,5,4,3,2,1,0:T(8,128)(2,1)} %bitcast.61, bf16[4,2,2,2,2,16,256]{6,5,4,3,2,1,0:T(8,128)(2,1)} %bitcast.64, ...), custom_call_target="tpu_custom_call" | custom-call | flops 32212254720 | bytes 52428800 | tf_op jit(solution)/shard_map/pallas_call | solution.py:1176
  167.5 3.6 %shard_map.341 = (bf16[256,1024]{1,0:T(8,128)(2,1)}, f32[256,1024]{1,0:T(8,128)}, f32[128,1024]{1,0:T(8,128)}, f32[32,4096]{1,0:T(8,128)}, f32[32,1024]{1,0:T(8,...) custom-call(bf16[256,1024]{1,0:T(8,128)(2,1)} %get-tuple-element.75., ...), custom_call_target="tpu_custom_call" | custom-call | tf_op jit(solution)/shard_map/pallas_call | solution.py:1138

commit v4 on v3

--- a/solution.py
+++ b/solution.py
@@ -11,10 +11,6 @@
 HEADS = 16
 MESH = pl.DeviceIdType.MESH
 F32, BF16 = jnp.float32, jnp.bfloat16
-WX = 384
-WZ = 256
-WR = 2 * WX + WZ
-ROWS = 16
 
 
 def norm_rows(values_in, gain_vec, bias_vec):
@@ -87,14 +83,14 @@
 
 
 def forward_kernel(lens, tok, gain, bias, w_hbm, qv_bias, head_scale, wo_hbm, out_bias, pa_gain, pa_bias, mid_gain, mid_bias,
-                   w1_hbm, fc1_bias, ffn_gain, ffn_bias,
+                   w1_hbm, fc1_bias, ffn_gain, ffn_bias, cot,
                    low_in_t, qw_out, kw_out, vw_out, att_out, lse, scaled_t, attn_out, first_out, low_mid_t, normed_out, slope_out,
-                   scale_out, low_ffn_out, low_ffn_t,
+                   scale_out, low_ffn_out, low_ffn_t, cot_x, low_in_x, low_mid_x, scaled_y,
                    w, wo, w1, tok_y, low_in, low_y, qw, kw, vw, mask, acc, att, attn, first, low_mid, act, part, turned, normed,
                    slope, low_ffn, ffn_turned, w_sem, sends, recvs, out_sem):
     dp, blk = lax.axis_index("dp"), lax.axis_index("blk")
-    y, c = blk // 2, blk % 2
-    core_dev, y_dev = (dp, blk + 1 - 2 * c), (dp, blk + 2 - 4 * y)
+    x, y, c = dp % 2, blk // 2, blk % 2
+    core_dev, x_dev, y_dev = (dp, blk + 1 - 2 * c), (dp + 1 - 2 * x, blk), (dp, blk + 2 - 4 * y)
     rows, width = tok.shape
     dim = width // HEADS
     half = rows // 2
@@ -112,13 +108,16 @@
     for i in (2, 3, 4, 5, 0, 1, 6, 7):
         loads[i].start()
     bar = pltpu.get_barrier_semaphore()
-    for dev in (core_dev, y_dev):
+    for dev in (core_dev, x_dev, y_dev):
         pl.semaphore_signal(bar, inc=1, device_id=dev, device_id_type=MESH)
-    pl.semaphore_wait(bar, 2)
+    pl.semaphore_wait(bar, 3)
     cross = [remote(tok.at[pl.ds(i * half, half)], tok_y.at[pl.ds(i * half, half)], i, y_dev) for i in range(2)]
     for cp in cross:
         cp.start()
 
+    ahead = [remote(cot, cot_x, 8, x_dev), remote(turned.at[0], low_in_x, 9, x_dev), remote(turned.at[2], low_mid_x, 10, x_dev),
+             remote(turned.at[1], scaled_y, 11, y_dev)]
+    ahead[0].start()
     outs = []
 
     def emit(src, dst):
@@ -173,6 +172,7 @@
         own_q.start()
 
     turned[0] = low_in[...].T
+    ahead[1].start()
     emit(turned.at[0], low_in_t)
 
     for i in range(2):
@@ -261,12 +261,18 @@
     emit(att, att_out)
 
     scaled = (att[...] * head_row(head_scale, width)).astype(BF16)
+    turned[1] = scaled.T
+    ahead[3].start()
+    emit(turned.at[1], scaled_t)
     loads[6].wait()
     attn[...] = dot32(scaled, wo[...]) + out_bias[...]
     emit(attn, attn_out)
     first[...] = tok[...].astype(F32) + norm_in(attn[...], pa_gain[...], pa_bias[...])
     emit(first, first_out)
     low_mid[...] = norm_in(first[...], mid_gain[...], mid_bias[...]).astype(BF16)
+    turned[2] = low_mid[...].T
+    ahead[2].start()
+    emit(turned.at[2], low_mid_t)
     loads[7].wait()
     part[...] = jnp.zeros_like(part)
 
@@ -309,13 +315,10 @@
     emit(normed, normed_out)
     emit(low_ffn, low_ffn_out)
     emit(ffn_turned, low_ffn_t)
-    turned[1] = scaled.T
-    emit(turned.at[1], scaled_t)
-    turned[2] = low_mid[...].T
-    emit(turned.at[2], low_mid_t)
-
     for cp in cross:
         cp.wait_send()
+    for cp in ahead:
+        cp.wait()
 
     @pl.when(c == 0)
     def _():
@@ -340,7 +343,7 @@
 
 
 def forward(lengths, tokens, ln1_gain, ln1_bias, w_qkv, qv_bias, head_scale, w_out, out_bias, pa_gain, pa_bias, mid_gain, mid_bias,
-            w_fc1, fc1_bias, ffn_gain, ffn_bias):
+            w_fc1, fc1_bias, ffn_gain, ffn_bias, cotangent):
     rows, width = tokens.shape
     ff = w_fc1.shape[1]
     hbm, vmem, smem = (pl.BlockSpec(memory_space=space) for space in (pl.ANY, pltpu.VMEM, pltpu.SMEM))
@@ -352,9 +355,10 @@
         out_shape=[shape((width, rows), BF16), shape(window, BF16), shape(window, BF16), shape(window, BF16),
                    shape((rows, width), F32), shape((HEADS, rows), F32), shape((width, rows), BF16), shape((rows, width), F32),
                    shape((rows, width), F32), shape((width, rows), BF16), shape(wide, BF16), shape(wide, BF16),
-                   shape((rows, 128), F32), shape(wide, BF16), shape(tall, BF16)],
-        in_specs=[smem, vmem, vmem, vmem, hbm, vmem, smem, hbm] + [vmem] * 5 + [hbm] + [vmem] * 3,
-        out_specs=[hbm] * 5 + [vmem] + [hbm] * 6 + [vmem] + [hbm] * 2,
+                   shape((rows, 128), F32), shape(wide, BF16), shape(tall, BF16), shape((rows, width), BF16), shape((width, rows), BF16),
+                   shape((width, rows), BF16), shape((width, rows), BF16)],
+        in_specs=[smem, vmem, vmem, vmem, hbm, vmem, smem, hbm] + [vmem] * 5 + [hbm] + [vmem] * 3 + [hbm],
+        out_specs=[hbm] * 5 + [vmem] + [hbm] * 6 + [vmem] + [hbm] * 6,
         scratch_shapes=[pltpu.VMEM((width, 3 * width), BF16), pltpu.VMEM((width, width), BF16), pltpu.VMEM((width, ff), BF16),
                         pltpu.VMEM((rows, width), BF16), pltpu.VMEM((rows, width), BF16), pltpu.VMEM((rows, width), BF16),
                         pltpu.VMEM(window, BF16), pltpu.VMEM(window, BF16), pltpu.VMEM(window, BF16),
@@ -362,40 +366,48 @@
                         pltpu.VMEM((rows, width), F32), pltpu.VMEM((rows, width), F32), pltpu.VMEM((rows, width), F32),
                         pltpu.VMEM((rows, width), BF16), pltpu.VMEM(wide, F32), pltpu.VMEM((2, rows, 128), F32),
                         pltpu.VMEM((3, width, rows), BF16), pltpu.VMEM(wide, BF16), pltpu.VMEM(wide, BF16), pltpu.VMEM(wide, BF16),
-                        pltpu.VMEM(tall, BF16), dma((8,)), dma((8,)), dma((8,)), dma((13,))],
+                        pltpu.VMEM(tall, BF16), dma((8,)), dma((12,)), dma((12,)), dma((13,))],
         compiler_params=pltpu.CompilerParams(collective_id=1, has_side_effects=True, vmem_limit_bytes=60 << 20),
         cost_estimate=pl.CostEstimate(flops=12 << 30, bytes_accessed=40 << 20, transcendentals=5 << 20),
     )(lengths, tokens, ln1_gain[None], ln1_bias[None], w_qkv, qv_bias[None], head_scale[None], w_out, out_bias[None],
-      pa_gain[None], pa_bias[None], mid_gain[None], mid_bias[None], w_fc1, fc1_bias[None], ffn_gain[None], ffn_bias[None])
+      pa_gain[None], pa_bias[None], mid_gain[None], mid_bias[None], w_fc1, fc1_bias[None], ffn_gain[None], ffn_bias[None], cotangent)
 
 
 SEND = 4
 RECV = 8
 KEEP = 8
-LAG_XY = (0, 2, 4, 6, 8, 10)
-LAG_Z = (0, 2, 4, 6, 8, 10)
+WY = 384
+WZ = 128
+WR = WY + WZ
+ROWS = 32
+FIRST = 2
+LAG_Y = (0, 2, 4, 6, 8)
+LAG_Z = (0, 2, 4, 6, 8)
+LAG_SWAP = (9, 11)
 MIDDLE = 6
+FAR = 3
 PIECES = 3
 
 
-def back_kernel(tok, a2, a1, ao, aq, cot, lens, qw_in, kw_in, vw_in, lse, att, attn, first, scale_ffn, tokens,
+def back_kernel(tok, a2, a1, a1x, ao, aoy, aq, aqx, cot, cot_x, lens, qw_in, kw_in, vw_in, lse, att_in, attn_in, first_in, scale_ffn, tokens,
                 gain, pa_gain, mid_gain, ffn_gain, head_scale, fc2_bias, normed_in, slope_in, low_ffn_in, w2_in, w1_in, wo_in, wq_in,
                 out2, out1, outo, outq, vout, grad_tok, layer_out,
-                am, ap, bm, bp, s1x, s1y, s2x, s2y, sr, sl, szr, szl, szx, szy, swx, swy,
-                r1x, r1y, r2x, r2y, rr, rl, rzr, rzl, rzx, rzy, rwx, rwy,
-                k2x, k2y, t3, kzx, kzy, kwx, kwy, out, vec, vown, vrecv,
-                qw, kw, vw, dow, stw, mask, mask_q, dqa, dka, dva, total, d_first, d_ffn, parts,
+                am, bm, pre_other, attn_other, dpj, s1, sr, sl, szr, szl, szy, sswap, r1, rr, rl, rzr, rzl, rzy, rswap,
+                prod, kz, kzy, out, swapped, vec, vown, vrecv,
+                qw, kw, vw, dow, stw, mask, mask_q, total, d_first, d_ffn, parts, att, attn, first, layer_held,
                 normed, w2b, colb, lowb, slopeb,
-                load_sem, peer_send, peer_recv, send, recv, vsend, vrecv_sem, asend, arecv, in_sem, w2_sem, col_sem, low_sem, slope_sem,
-                out_sem):
+                a_send, a_recv, b_send, b_recv, send, recv, vsend, vrecv_sem, asend, arecv, in_sem, w2_sem, col_sem, low_sem, slope_sem,
+                swap_sems, attn_sems, out_sem):
     dp, blk = lax.axis_index("dp"), lax.axis_index("blk")
     z, x = dp // 2, dp % 2
     y, c = blk // 2, blk % 2
     core_dev, x_dev, y_dev = (dp, blk + 1 - 2 * c), (dp + 1 - 2 * x, blk), (dp, blk + 2 - 4 * y)
+    cross_dev = (dp + 1 - 2 * x, blk + 1 - 2 * c)
     up_dev, down_dev = (dp + 2, blk), (dp - 2, blk)
     rounds = 24
     rows, width = tokens.shape
     dim = width // HEADS
+    n_attn = WR // (2 * dim)
 
     ff = normed.shape[1]
     n_ff = ff // FC
@@ -405,32 +417,41 @@
         return [pltpu.make_async_copy(w2_in.at[pl.ds(j * FC, FC)], w2b.at[j % PIECES], w2_sem.at[j % PIECES]),
                 pltpu.make_async_copy(low_ffn_in.at[:, pl.ds(j * FC, FC)], lowb.at[j % PIECES], low_sem.at[j % PIECES])]
 
-    def piece_slope(j):
-        return pltpu.make_async_copy(slope_in.at[:, pl.ds(j * FC, FC)], slopeb.at[j % PIECES], slope_sem.at[j % PIECES])
+    def pre_place(q):
+        half = n_ff // 2
+        return ((q + 1) % 2 + x * (2 * (q % 2) - 1)) * half + q // 2
+
+    def piece_slope(q):
+        return pltpu.make_async_copy(slope_in.at[:, pl.ds(pre_place(q) * FC, FC)], slopeb.at[q % PIECES], slope_sem.at[q % PIECES])
 
     def piece_col(q, ref, j):
         return pltpu.make_async_copy(ref.at[:, pl.ds(j * FC, FC)], colb.at[q % PIECES], col_sem.at[q % PIECES])
 
     def start_col(q):
-        def go(ref, low, high):
+        def go(ref, low, high, where=None):
             def start():
-                piece_col(q, ref, q - low).start()
+                piece_col(q, ref, q - low if where is None else where(q)).start()
             if isinstance(q, int):
                 if low <= q < high:
                     start()
             else:
                 pl.when((q >= low) & (q < high))(start)
-        go(w1_in, 0, n_ff)
+        go(w1_in, 0, n_ff, pre_place)
         go(wo_in, n_ff, n_ff + n_o)
         go(wq_in, n_ff + n_o, n_ff + n_o + n_q)
 
     early = [pltpu.make_async_copy(qw_in, qw, in_sem.at[0]), pltpu.make_async_copy(kw_in, kw, in_sem.at[1]),
              pltpu.make_async_copy(vw_in, vw, in_sem.at[2])]
     normed_load = pltpu.make_async_copy(normed_in, normed, in_sem.at[3])
+    layer_copy = pltpu.make_async_copy(layer_held, layer_out, in_sem.at[4])
+    grad_copy = pltpu.make_async_copy(d_first, grad_tok, in_sem.at[5])
+    first_load = pltpu.make_async_copy(first_in, first, in_sem.at[6])
+    attn_load = pltpu.make_async_copy(attn_in, attn, in_sem.at[7])
+    att_load = pltpu.make_async_copy(att_in, att, in_sem.at[8])
 
     bar = pltpu.get_barrier_semaphore()
     z_devs = [((dp + 2 * k) % 8, blk) for k in range(1, 4)]
-    for dev in [core_dev, x_dev, y_dev] + z_devs:
+    for dev in [core_dev, x_dev, y_dev, cross_dev] + z_devs:
         pl.semaphore_signal(bar, inc=1, device_id=dev, device_id_type=MESH)
     def remote(src, dst, ssem, rsem, dev):
         return pltpu.make_async_remote_copy(src, dst, ssem, rsem, device_id=dev, device_id_type=MESH)
@@ -447,47 +468,81 @@
         cols = pl.ds(pl.multiple_of(i * 2 * dim, 2 * dim), 2 * dim)
         return remote(dow.at[src, :, cols], dow.at[dst, :, cols], asend.at[k + i], arecv.at[k + i], dev)
 
-    a_src = [(a2, g) for g in range(8)] + [(a1, 0), (a1, 1), (ao, 0), (ao, 1), (aq, 0), (aq, 1)]
-    b_src = [(cot, 0)]
-    n_a = len(a_src)
-
-    def loads(kind, i, own):
-        k = i if kind == "a" else n_a + i
-        if kind == "a":
-            ref, g = a_src[i]
-            if own:
-                return pltpu.make_async_copy(ref.at[:, :, :, c, g], am.at[i], load_sem.at[k])
-            return remote(ref.at[:, :, :, 1 - c, g], ap.at[i], peer_send.at[k], peer_recv.at[k], core_dev)
-        ref, g = b_src[i]
-        part = ref.at[:, pl.ds(g * WR, WR)]
-        if own:
-            return pltpu.make_async_copy(part, bm.at[i], load_sem.at[k])
-        return remote(part, bp.at[i], peer_send.at[k], peer_recv.at[k], core_dev)
-
-    phases = [([("b", 0)] + [("a", g) for g in range(8)]), [("a", 8), ("a", 9)], [("a", 10), ("a", 11), ("a", 12), ("a", 13)]]
-    for item in phases[0]:
-        loads(*item, True).start()
+    def rows_of(ref, g, who, core):
+        if g < 4:
+            return ref.at[:, who, :, core, g]
+        if g in (6, 7):
+            return ref.at[:, :, g % 2, core, 0]
+        return ref.at[:, g % 2, :, core, 0]
+
+    a_own = [a2] * 4 + [a1] * 2 + [ao] * 2 + [aq] * 2
+    a_far = [None] * 4 + [a1x] * 2 + [aoy] * 2 + [aqx] * 2
+
+    def a_load(g, t):
+        sems = (a_send.at[g, t], a_recv.at[g, t])
+        if t == 0:
+            return pltpu.make_async_copy(rows_of(a_own[g], g, x, c), am.at[g, 0], a_recv.at[g, 0])
+        if t == 1:
+            return remote(rows_of(a_own[g], g, x, 1 - c), am.at[g, 1], *sems, core_dev)
+        if g < 4:
+            return remote(rows_of(a2, g, 1 - x, c if t == 2 else 1 - c), am.at[g, t], *sems, x_dev if t == 2 else cross_dev)
+        if t == 2:
+            return pltpu.make_async_copy(rows_of(a_far[g], g, x, c), am.at[g, 2], a_recv.at[g, 2])
+        return remote(rows_of(a_far[g], g, x, 1 - c), am.at[g, 3], *sems, core_dev)
+
+    def cot_load(b, t):
+        part = (cot if t < 2 else cot_x).at[:, pl.ds(b * WR, WR)]
+        if t % 2 == 0:
+            return pltpu.make_async_copy(part, bm.at[b, t], b_recv.at[b, t])
+        return remote(part, bm.at[b, t], b_send.at[b, t], b_recv.at[b, t], core_dev)
+
+    def local(g, t):
+        return t == 0 or (t == 2 and g >= 4)
+
+    def a_arrive(g):
+        for t in range(4):
+            if local(g, t):
+                a_load(g, t).wait()
+            else:
+                a_load(g, t).wait_recv()
+
+    def b_to_core(b, t):
+        return remote(bm.at[b, t], bm.at[b, t + 1], b_send.at[b, t + 1], b_recv.at[b, t + 1], core_dev)
+
+    def b_far(b, src, dev):
+        return remote(src, bm.at[b, 2], b_send.at[b, 2], b_recv.at[b, 2], dev)
+
+    def pre_far(k):
+        return b_far(2 + k, pre_other.at[k], x_dev)
+
+    def attn_far(k):
+        cols = pl.ds(k * 2 * dim, 2 * dim)
+        return remote(attn_other.at[:, cols], bm.at[6, 2, :, cols], attn_sems.at[0, k], attn_sems.at[1, k], y_dev)
+
+    def proj_block(who, k):
+        return jnp.where(who == 0, k, jnp.where(k == 0, 4, jnp.where(k == 1, 3, 5)))
+
+    def proj_far(k):
+        return b_far(7 + k, dpj.at[proj_block(1 - x, k)], x_dev)
+
+    for b in range(2):
+        cot_load(b, 0).start()
+    for g in range(4):
+        a_load(g, 0).start()
     normed_load.start()
     for j in range(PIECES):
         for cp in piece2(j):
             cp.start()
-    for phase in phases[1:]:
-        for item in phase:
-            loads(*item, True).start()
+    for b in range(2):
+        cot_load(b, 2).start()
     for j in range(PIECES):
         start_col(j)
         piece_slope(j).start()
-    for cp in early:
+    for g in range(4, 10):
+        a_load(g, 0).start()
+        a_load(g, 2).start()
+    for cp in early + [first_load, attn_load, att_load]:
         cp.start()
-
-    def peer_b(i):
-        k = n_a + i
-        return remote(bm.at[i], bp.at[i], peer_send.at[k], peer_recv.at[k], core_dev)
-
-    def arrive(phase):
-        for item in phase:
-            loads(*item, True).wait()
-            loads(*item, False).wait_recv()
 
     vec[...] = jnp.zeros_like(vec)
     total[...] = jnp.zeros_like(total)
@@ -499,41 +554,56 @@
     k_spots = blk * rows + lax.broadcasted_iota(jnp.int32, (rows, 1), 0)
     mask_q[...] = jnp.where(k_spots >= sequence_starts(lens, q_spots), 0.0, -1e30)
 
-    pl.semaphore_wait(bar, 6)
-    for phase in phases:
-        for item in phase:
-            loads(*item, False).start()
+    pl.semaphore_wait(bar, 7)
+    for g in range(4):
+        for t in (2, 3, 1):
+            a_load(g, t).start()
+        if g < 2:
+            cot_load(g, 1).start()
+            cot_load(g, 3).start()
+    for g in range(4, 10):
+        a_load(g, 1).start()
+        a_load(g, 3).start()
+
+    def is_out(r):
+        return (r >= 18) & (r < 20)
+
+    def proj_turn(r):
+        return jnp.where(r < 18, 0, (r - 18) // 2)
 
     def place(r):
-        g = jnp.where(r < 8, r, jnp.where(r < 16, 8 + r % 2, jnp.where(r < 18, 10 + r % 2, 12 + r % 2)))
-        b = jnp.where(r < 8, 0, (r - 8) // 2 + 1)
+        q = r % 2
+        g = jnp.where(r < 8, r // 2, jnp.where(r < 16, 4 + q, jnp.where(is_out(r), 6 + q, 8 + q)))
+        b = jnp.where(r < 8, q, jnp.where(r < 16, 2 + (r - 8) // 2, jnp.where(is_out(r), 6, 7 + proj_turn(r))))
         return g, b
 
-    def product(r, zs, xs, ys, col, width):
+    def turned_axes(r):
+        is_o = is_out(r)
+        here = jnp.where(is_o, x, y)
+        sum_dev = (jnp.where(is_o, x_dev[0], y_dev[0]), jnp.where(is_o, x_dev[1], y_dev[1]))
+        swap_dev = (jnp.where(is_o, y_dev[0], x_dev[0]), jnp.where(is_o, y_dev[1], x_dev[1]))
+        return here, sum_dev, swap_dev
+
+    def multiply(r):
         g, b = place(r)
-        cols = pl.ds(col, width)
-        la, lp = am[g, zs, xs, ys], ap[g, zs, xs, ys]
-        lead = la.shape[:-1]
-        m = 1
-        for d in lead:
-            m *= d
-        res = dot32(la.reshape(m, tok), bm[b, :, cols]) + dot32(lp.reshape(m, tok), bp[b, :, cols])
-        return res.reshape(lead + (width,))
-
-    ALL = slice(None)
-    col_y, col_z = WX, 2 * WX
-    S1X, S1Y, S2X, S2Y, SR, SL, SZR, SZL, SZX, SZY, SWX, SWY = range(12)
-
-    def message(src, dst, kind, dev):
+        res = None
+        for t in range(4):
+            term = dot32(am[g, t].reshape(8 * ROWS, tok), bm[b, t])
+            res = term if res is None else res + term
+        prod[r % KEEP] = res.reshape(4, 2, ROWS, WR)
+
+    S1, SR, SL, SZR, SZL, SZY = range(6)
+
+    def from_slot(r):
+        return jnp.where(is_out(r), RECV + r % 2, r % RECV)
+
+    def message(src, dst, kind, which):
         def make(r):
-            return remote(src.at[r % SEND], dst.at[r % RECV], send.at[kind, r % SEND], recv.at[kind, r % RECV], dev)
+            slot = from_slot(r)
+            return remote(src.at[r % SEND], dst.at[slot], send.at[kind, r % SEND], recv.at[kind, slot], turned_axes(r)[which])
         return make
 
-    step1x, step1y = message(s1x, r1x, S1X, x_dev), message(s1y, r1y, S1Y, y_dev)
-    step2x, step2y = message(s2x, r2x, S2X, y_dev), message(s2y, r2y, S2Y, x_dev)
-    stepzx, stepzy = message(szx, rzx, SZX, x_dev), message(szy, rzy, SZY, y_dev)
-    stepwx, stepwy = message(swx, rwx, SWX, y_dev), message(swy, rwy, SWY, x_dev)
-    steps = (step1x, step1y, step2x, step2y, stepzx, stepzy, stepwx, stepwy)
+    step1, stepz = message(s1, r1, S1, 1), message(szy, rzy, SZY, 1)
 
     def put(step, ref, r, value):
         @pl.when(r >= SEND)
@@ -609,46 +679,33 @@
                 chain(src[1], dst[1], kind_l, r, 0, 3 - hop, down_dev).wait_send()
 
     def z_term(r, d):
-        return product(r, d, ALL, ALL, col_z, WZ)
+        return prod[r % KEEP, d, :, :, WY:WR]
 
     def t_term(r, d):
-        return t3[r % KEEP, d]
+        return prod[r % KEEP, d, turned_axes(r)[0], :, 0:WY]
 
     zsrc, zdst = (szr, szl), (rzr, rzl)
     csrc, cdst = (sr, sl), (rr, rl)
 
-    def xy0(r):
-        put(step1x, s1x, r, product(r, ALL, 1 - x, ALL, 0, WX))
-        put(step1y, s1y, r, product(r, ALL, ALL, 1 - y, col_y, WX))
-
-    def xy1(r):
-        slot = r % KEEP
-        step1x(r).wait_recv()
-        k2x[...] = product(r, ALL, x, ALL, 0, WX) + r1x[r % RECV].astype(F32)
-        put(step2x, s2x, r, k2x[:, 1 - y])
-        kwx[slot] = k2x[:, y]
-        step1y(r).wait_recv()
-        k2y[...] = product(r, ALL, ALL, y, col_y, WX) + r1y[r % RECV].astype(F32)
-        put(step2y, s2y, r, k2y[:, 1 - x])
-        kwy[slot] = k2y[:, x]
-
-    def xy2(r):
-        slot = r % KEEP
-        step2x(r).wait_recv()
-        t3[slot, :, :, 0:WX] = kwx[slot] + r2x[r % RECV].astype(F32)
-        step2y(r).wait_recv()
-        t3[slot, :, :, WX:2 * WX] = kwy[slot] + r2y[r % RECV].astype(F32)
+    def y0(r):
+        multiply(r)
+        put(step1, s1, r, prod[r % KEEP, :, 1 - turned_axes(r)[0], :, 0:WY])
+
+    def y1(r):
+        step1(r).wait_recv()
+        here = turned_axes(r)[0]
+        prod[r % KEEP, :, here, :, 0:WY] = prod[r % KEEP, :, here, :, 0:WY] + r1[from_slot(r)].astype(F32)
         chain_hop(0, r, csrc, cdst, SR, SL, t_term)
 
-    def xy3(r):
+    def y2(r):
         chain_hop(1, r, csrc, cdst, SR, SL, t_term)
 
-    def xy4(r):
+    def y3(r):
         chain_hop(2, r, csrc, cdst, SR, SL, t_term)
 
-    def xy5(r):
-        chain_last(r, csrc, cdst, SR, SL, out.at[r, :, 0:2 * WX])
-        out[r, :, 0:2 * WX] = out[r, :, 0:2 * WX] + t3[r % KEEP, z]
+    def y4(r):
+        chain_last(r, csrc, cdst, SR, SL, out.at[r, :, 0:WY])
+        out[r, :, 0:WY] = out[r, :, 0:WY] + prod[r % KEEP, z, turned_axes(r)[0], :, 0:WY]
 
     def z0(r):
         chain_hop(0, r, zsrc, zdst, SZR, SZL, z_term)
@@ -660,33 +717,75 @@
         chain_hop(2, r, zsrc, zdst, SZR, SZL, z_term)
 
     def z3(r):
-        slot = r % KEEP
-        chain_last(r, zsrc, zdst, SZR, SZL, kzx)
-        kzx[...] = kzx[...] + product(r, z, ALL, ALL, col_z, WZ)
-        put(stepzx, szx, r, kzx[1 - x, :, :, 0:WZ // 2])
-        put(stepzy, szy, r, kzx[:, 1 - y, :, WZ // 2:WZ])
-        kzy[slot, 0] = kzx[x, :, :, 0:WZ // 2]
-        kzy[slot, 1] = kzx[:, y, :, WZ // 2:WZ]
+        here = turned_axes(r)[0]
+        chain_last(r, zsrc, zdst, SZR, SZL, kz)
+        kz[...] = kz[...] + prod[r % KEEP, z, :, :, WY:WR]
+        put(stepz, szy, r, kz[1 - here])
+        kzy[r % KEEP] = kz[here]
 
     def z4(r):
-        slot = r % KEEP
-        stepzx(r).wait_recv()
-        kzy[slot, 0] = kzy[slot, 0] + rzx[r % RECV].astype(F32)
-        put(stepwx, swx, r, kzy[slot, 0, 1 - y])
-        stepzy(r).wait_recv()
-        kzy[slot, 1] = kzy[slot, 1] + rzy[r % RECV].astype(F32)
-        put(stepwy, swy, r, kzy[slot, 1, 1 - x])
-
-    def z5(r):
-        slot = r % KEEP
-        stepwx(r).wait_recv()
-        out[r, :, 2 * WX:2 * WX + WZ // 2] = kzy[slot, 0, y] + rwx[r % RECV].astype(F32)
-        stepwy(r).wait_recv()
-        out[r, :, 2 * WX + WZ // 2:] = kzy[slot, 1, x] + rwy[r % RECV].astype(F32)
+        stepz(r).wait_recv()
+        out[r, :, WY:WR] = kzy[r % KEEP] + rzy[from_slot(r)].astype(F32)
+
+    def swapping(r):
+        return r >= 8
+
+    def mine(r):
+        return (r % 2) == jnp.where(is_out(r), y, x)
+
+    def swap_slot(r):
+        return (r - 8) // 2
+
+    def swap0(r):
+        @pl.when(swapping(r) & ~mine(r))
+        def _():
+            k = swap_slot(r)
+            sswap[k] = out[r].astype(BF16)
+            step_swap(r).start()
+
+        @pl.when(~swapping(r) | mine(r))
+        def _():
+            share(r)
+
+    def swap1(r):
+        @pl.when(swapping(r) & mine(r))
+        def _():
+            k = swap_slot(r)
+            step_swap(r).wait_recv()
+            swapped[k] = rswap[k].astype(F32)
+            share_far(r)
+
+    def step_swap(r):
+        k = swap_slot(r)
+        return remote(sswap.at[k], rswap.at[k], send_swap(k), recv_swap(k), turned_axes(r)[2])
+
+    def send_swap(k):
+        return swap_sems.at[0, k]
+
+    def recv_swap(k):
+        return swap_sems.at[1, k]
+
+    def cols_at(start):
+        return pl.ds(pl.multiple_of(start, WR), WR)
+
+    def share_copies(r, src, who):
+        k = (r - 8) // 2
+        return [((r < 8), pltpu.make_async_copy(src, out2.at[pl.ds(pl.multiple_of(r // 2 * ROWS, ROWS), ROWS), cols_at(r % 2 * WR)], out_sem.at[0])),
+                ((r >= 8) & (r < 16), pltpu.make_async_copy(src, out1.at[:, cols_at(who * (ff // 2) + k * WR)], out_sem.at[0])),
+                (is_out(r), pltpu.make_async_copy(src, outo.at[:, cols_at(who * WR)], out_sem.at[0])),
+                ((r >= 16) & ~is_out(r), pltpu.make_async_copy(src, outq.at[:, cols_at(proj_block(who, proj_turn(r)) * WR)], out_sem.at[0]))]
+
+    def share(r):
+        for here, cp in share_copies(r, out.at[r], jnp.where(is_out(r), y, x)):
+            pl.when(here)(cp.start)
+
+    def share_far(r):
+        for here, cp in share_copies(r, swapped.at[swap_slot(r)], 1 - jnp.where(is_out(r), y, x)):
+            pl.when(here)(cp.start)
 
     def drain(r):
-        for step in steps:
-            step(r).wait_send()
+        step1(r).wait_send()
+        stepz(r).wait_send()
         chain_drain(r, csrc, cdst, SR, SL)
         chain_drain(r, zsrc, zdst, SZR, SZL)
 
@@ -748,6 +847,7 @@
             for cp in window_rows("relay"):
                 cp.start()
 
+    def others_arrive():
         @pl.when(c == 0)
         def _():
             for cp in window_rows("own"):
@@ -792,66 +892,70 @@
             for i in range(HEADS // 2):
                 window_piece("relay", i).wait_send()
 
-    def attend_pairs(i, kj, qj, bias, to_q, to_k, first):
-        cols = pl.ds(pl.multiple_of(i * 2 * dim, 2 * dim), 2 * dim)
-        k2, v2, q2, d2 = kw[kj, :, cols], vw[kj, :, cols], qw[qj, :, cols], dow[qj, :, cols]
-        for sub in range(2):
-            part = slice(sub * dim, (sub + 1) * dim)
-            k1, v1, q1, d1 = k2[:, part], v2[:, part], q2[:, part], d2[:, part]
-            log_total = stw[qj, pl.ds(2 * i + sub, 1)]
-            delta = stw[qj, pl.ds(HEADS + 2 * i + sub, 1)]
-            probs = jnp.exp(dot_nt(k1, q1) + bias[...] - log_total)
-            low_s = (probs * (dot_nt(v1, d1) - delta)).astype(BF16)
-            if to_q:
-                term = dot_tn(k1, low_s)
-                dqa[part] = term if first else dqa[part] + term
-            if to_k:
-                term = dot32(low_s, q1)
-                dka[sub] = term if first else dka[sub] + term
-                term = dot32(probs.astype(BF16), d1)
-                dva[sub] = term if first else dva[sub] + term
+    lower = lax.broadcasted_iota(jnp.int32, (1, 2 * dim), 1) < dim
+
+    def one_head(values, sub):
+        return jnp.where(lower if sub == 0 else ~lower, values, jnp.zeros_like(values))
+
+    def both_heads(terms):
+        return jnp.where(lower, terms[0], terms[1])
+
+    def weights_of(i, sub, k1, v1, qj, q2, d2, bias):
+        log_total = stw[qj, pl.ds(2 * i + sub, 1)]
+        delta = stw[qj, pl.ds(HEADS + 2 * i + sub, 1)]
+        probs = jnp.exp(dot_nt(k1, q2) + bias - log_total)
+        return probs.astype(BF16), (probs * (dot_nt(v1, d2) - delta)).astype(BF16)
+
+    def add(total_sum, term):
+        return term if total_sum is None else total_sum + term
 
     def attend_near(i):
         cols = pl.ds(pl.multiple_of(i * 2 * dim, 2 * dim), 2 * dim)
-        attend_pairs(i, 2, 0, mask.at[2 * rows:3 * rows], True, True, True)
-
-        @pl.when(blk >= 1)
-        def _():
-            attend_pairs(i, 1, 0, mask.at[rows:2 * rows], True, False, False)
-
-        @pl.when(blk >= 2)
-        def _():
-            attend_pairs(i, 0, 0, mask.at[0:rows], True, False, False)
-
-        bm[6, :, cols] = (dqa[...].T * (dim ** -0.5)).astype(BF16)
-        d_ffn[:, cols] = jnp.concatenate([dka[0], dka[1]], axis=1)
-        d_ffn[:, pl.ds(pl.multiple_of(width + i * 2 * dim, 2 * dim), 2 * dim)] = jnp.concatenate([dva[0], dva[1]], axis=1)
+        part_cols = pl.ds(pl.multiple_of(i % 4 * 2 * dim, 2 * dim), 2 * dim)
+
+        def blocks(lowest):
+            q2, d2 = qw[0, :, cols], dow[0, :, cols]
+            dq, dk, dv = None, [None, None], [None, None]
+            for kj in range(lowest, 3):
+                k2, v2 = kw[kj, :, cols], vw[kj, :, cols]
+                for sub in range(2):
+                    k1 = one_head(k2, sub)
+                    low_p, low_s = weights_of(i, sub, k1, one_head(v2, sub), 0, q2, d2, mask[kj * rows:(kj + 1) * rows])
+                    dq = add(dq, dot_tn(k1, low_s))
+                    if kj == 2:
+                        dk[sub], dv[sub] = dot32(low_s, q2), dot32(low_p, d2)
+            dpj[i // 4, :, part_cols] = (dq.T * (dim ** -0.5)).astype(BF16)
+            d_ffn[:, cols] = both_heads(dk)
+            d_ffn[:, pl.ds(pl.multiple_of(width + i * 2 * dim, 2 * dim), 2 * dim)] = both_heads(dv)
+
+        for number in range(3):
+            pl.when(blk == number if number < 2 else blk >= 2)(functools.partial(blocks, 2 - number))
 
     def attend_far(i):
         cols = pl.ds(pl.multiple_of(i * 2 * dim, 2 * dim), 2 * dim)
-        dk_sum, dv_sum = d_ffn[:, cols], d_ffn[:, pl.ds(pl.multiple_of(width + i * 2 * dim, 2 * dim), 2 * dim)]
-
-        @pl.when(blk == 3)
-        def _():
-            bm[7, :, cols] = dk_sum.astype(BF16)
-            bm[8, :, cols] = dv_sum.astype(BF16)
+        part_cols = pl.ds(pl.multiple_of(i % 4 * 2 * dim, 2 * dim), 2 * dim)
 
         @pl.when((y == 0) & (c == 1))
         def _():
             window_piece("relay", i).wait_recv()
 
-        @pl.when(blk <= 2)
-        def _():
-            attend_pairs(i, 2, 1, mask_q.at[:, 0:rows], False, True, True)
-
-        @pl.when(blk <= 1)
-        def _():
-            attend_pairs(i, 2, 2, mask_q.at[:, rows:2 * rows], False, True, False)
-
-        @pl.when(blk <= 2)
-        def _():
-            bm[7, :, cols] = (dk_sum + jnp.concatenate([dka[0], dka[1]], axis=1)).astype(BF16)
-            bm[8, :, cols] = (dv_sum + jnp.concatenate([dva[0], dva[1]], axis=1)).astype(BF16)
+        def blocks(count):
+            k2, v2 = kw[2, :, cols], vw[2, :, cols]
+            dk, dv = [None, None], [None, None]
+            for sub in range(2):
+                k1, v1 = one_head(k2, sub), one_head(v2, sub)
+                for qj in range(1, count + 1):
+                    q2, d2 = qw[qj, :, cols], dow[qj, :, cols]
+                    low_p, low_s = weights_of(i, sub, k1, v1, qj, q2, d2, mask_q[:, (qj - 1) * rows:qj * rows])
+                    dk[sub], dv[sub] = add(dk[sub], dot32(low_s, q2)), add(dv[sub], dot32(low_p, d2))
+            dk_sum, dv_sum = d_ffn[:, cols], d_ffn[:, pl.ds(pl.multiple_of(width + i * 2 * dim, 2 * dim), 2 * dim)]
+            if count > 0:
+                dk_sum, dv_sum = dk_sum + both_heads(dk), dv_sum + both_heads(dv)
+            dpj[2 + i // 4, :, part_cols] = dk_sum.astype(BF16)
+            dpj[4 + i // 4, :, part_cols] = dv_sum.astype(BF16)
+
+        for number in range(3):
+            pl.when(blk == 3 - number if number < 2 else blk <= 1)(functools.partial(blocks, number))
 
     V_IN_GAIN, V_IN_BIAS, V_QV, V_OUT, V_PA_GAIN, V_PA_BIAS, V_MID_GAIN, V_MID_BIAS, V_FC2 = (
         k * (width // 128) for k in (0, 1, 2, 4, 5, 6, 7, 8, 9))
@@ -877,7 +981,7 @@
             cp.wait()
         weights = w2b[j % PIECES]
         total[...] = total[...] + dot32(lowb[j % PIECES], weights)
-        grad = dot_nt(bm[0], weights)
+        grad = dot_nt(bm[0, 0], weights[:, 0:WR]) + dot_nt(bm[1, 0], weights[:, WR:])
         unit = normed[:, cols].astype(F32)
         d_ffn[:, cols] = grad
         put_row_at(V_FFN_GAIN, j, jnp.sum(grad * unit, axis=0, keepdims=True))
@@ -892,31 +996,39 @@
                 cp.start()
 
     def ffn_between():
-        layer_out[...] = (first[...] + total[...] + fc2_bias[...]).astype(BF16)
+        layer_held[...] = (first[...] + total[...] + fc2_bias[...]).astype(BF16)
+        layer_copy.start()
         total[...] = jnp.zeros_like(total)
         parts[2] = jnp.broadcast_to(jnp.sum(parts[0], axis=-1, keepdims=True) * (1.0 / ff), parts.shape[1:])
         parts[3] = jnp.broadcast_to(jnp.sum(parts[1], axis=-1, keepdims=True) * (1.0 / ff), parts.shape[1:])
 
-    def ffn_second(j):
+    def ffn_second(q):
+        j = pre_place(q)
+        k = q // 2
         cols = chunk_cols(j)
-        piece_col(j, w1_in, j).wait()
-        piece_slope(j).wait()
+        piece_col(q, w1_in, j).wait()
+        piece_slope(q).wait()
         grad = d_ffn[:, cols] * ffn_gain[:, cols]
         grad = scale_ffn[:, 0:1] * (grad - parts[2][:, 0:1] - normed[:, cols].astype(F32) * parts[3][:, 0:1])
-        low = (grad * slopeb[j % PIECES].astype(F32)).astype(BF16)
-        bm[1 + j // 2, :, pl.ds(pl.multiple_of((j % 2) * FC, FC), FC)] = low
+        low = (grad * slopeb[q % PIECES].astype(F32)).astype(BF16)
         put_row_at(V_FC1, j, jnp.sum(low.astype(F32), axis=0, keepdims=True))
-        total[...] = total[...] + dot_nt(low, colb[j % PIECES])
-
-        @pl.when(j % 2 == 1)
-        def _():
-            peer_b(1 + j // 2).start()
-
-        @pl.when(j + PIECES < n_ff)
-        def _():
-            piece_slope(j + PIECES).start()
-
-        start_col(j + PIECES)
+        total[...] = total[...] + dot_nt(low, colb[q % PIECES])
+
+        @pl.when(q % 2 == 0)
+        def _():
+            pre_other[k] = low
+            pre_far(k).start()
+
+        @pl.when(q % 2 == 1)
+        def _():
+            bm[2 + k, 0] = low
+            b_to_core(2 + k, 0).start()
+
+        @pl.when(q + PIECES < n_ff)
+        def _():
+            piece_slope(q + PIECES).start()
+
+        start_col(q + PIECES)
 
     def unit_rows(values):
         centered = values - jnp.mean(values, axis=-1, keepdims=True)
@@ -931,20 +1043,27 @@
         return scale * (grad - jnp.mean(grad, axis=-1, keepdims=True) - unit * jnp.mean(grad * unit, axis=-1, keepdims=True))
 
     def middle_first():
-        d_out = bm[0].astype(F32)
+        d_out = jnp.concatenate([bm[0, 0], bm[1, 0]], axis=1).astype(F32)
         put_row(V_FC2, jnp.sum(d_out, axis=0, keepdims=True))
         d_first[...] = d_out + norm_back(total[...], first[...], mid_gain[...], V_MID_GAIN, V_MID_BIAS)
         low = norm_back(d_first[...], attn[...], pa_gain[...], V_PA_GAIN, V_PA_BIAS).astype(BF16)
-        bm[5] = low
-        peer_b(5).start()
+        for who in range(2):
+            @pl.when(y == who)
+            def _():
+                bm[6, 0] = low[:, who * WR:(who + 1) * WR]
+                attn_other[...] = low[:, (1 - who) * WR:(2 - who) * WR]
+
+        b_to_core(6, 0).start()
         put_row(V_OUT, jnp.sum(low.astype(F32), axis=0, keepdims=True))
 
     def middle_second():
         for k in range(n_o):
             piece_col(n_ff + k, wo_in, k).wait()
-        total[...] = dot_nt(bm[5, :, 0:FC], colb[n_ff % PIECES])
-        for k in range(1, n_o):
-            total[...] = total[...] + dot_nt(bm[5, :, k * FC:(k + 1) * FC], colb[(n_ff + k) % PIECES])
+        for who in range(2):
+            @pl.when(y == who)
+            def _():
+                total[...] = (dot_nt(bm[6, 0], colb[(n_ff + who) % PIECES]) + dot_nt(attn_other[...], colb[(n_ff + 1 - who) % PIECES]))
+
         for k in range(n_o):
             start_col(n_ff + k + PIECES)
         attended = att[...]
@@ -973,87 +1092,134 @@
             for cp in window_rows("own"):
                 cp.start()
 
+    def proj_out(blocks):
+        for who, k in blocks:
+            @pl.when(x == who)
+            def _():
+                bm[7 + k, 0] = dpj[(0, 1, 2)[k] if who == 0 else (4, 3, 5)[k]]
+                b_to_core(7 + k, 0).start()
+
+            @pl.when(x != who)
+            def _():
+                proj_far(k).start()
+
     def input_first():
-        for i in range(6, 9):
-            peer_b(i).start()
         base_q = n_ff + n_o
         for k in range(n_q):
             piece_col(base_q + k, wq_in, k).wait()
-            at = k * FC
-            term = dot_nt(bm[6 + at // width, :, at % width:at % width + FC], colb[(base_q + k) % PIECES])
+            term = dot_nt(dpj[k], colb[(base_q + k) % PIECES])
             total[...] = term if k == 0 else total[...] + term
             start_col(base_q + k + PIECES)
 
     def input_second():
         grad = norm_back(total[...], tokens[...].astype(F32), gain[...], V_IN_GAIN, V_IN_BIAS)
-        grad_tok[...] = d_first[...] + grad
-        put_row(V_QV, jnp.sum(bm[6].astype(F32), axis=0, keepdims=True))
-        put_row(V_QV + width // 128, jnp.sum(bm[8].astype(F32), axis=0, keepdims=True))
-
-    def share(r):
-        half = pl.ds((r % 2) * ROWS, ROWS)
-        return [((r >= 0) & (r < 8), pltpu.make_async_copy(out.at[r], out2.at[pl.ds(r * ROWS, ROWS)], out_sem.at[0])),
-                ((r >= 8) & (r < 16), pltpu.make_async_copy(out.at[r], out1.at[half, pl.ds((r - 8) // 2 * WR, WR)], out_sem.at[0])),
-                ((r >= 16) & (r < 18), pltpu.make_async_copy(out.at[r], outo.at[half], out_sem.at[0])),
-                ((r >= 18) & (r < rounds), pltpu.make_async_copy(out.at[r], outq.at[half, pl.ds((r - 18) // 2 * WR, WR)], out_sem.at[0]))]
+        d_first[...] = d_first[...] + grad
+        grad_copy.start()
+        for k, block in enumerate((0, 1, 4, 5)):
+            put_row(V_QV + k * (WR // 128), jnp.sum(dpj[block].astype(F32), axis=0, keepdims=True))
 
     n_pairs = HEADS // 2
-    after = MIDDLE + n_pairs + 3
-    plan = sorted(list(zip(LAG_XY, (xy0, xy1, xy2, xy3, xy4, xy5))) + list(zip(LAG_Z, (z0, z1, z2, z3, z4, z5))),
-                  key=lambda item: -item[0])
-    last = max(LAG_XY + LAG_Z)
+    after = MIDDLE + n_pairs + FAR
+    plan = sorted(list(zip(LAG_Y, (y0, y1, y2, y3, y4))) + list(zip(LAG_Z, (z0, z1, z2, z3, z4)))
+                  + list(zip(LAG_SWAP, (swap0, swap1))), key=lambda item: -item[0])
+    last = max(LAG_Y + LAG_Z + LAG_SWAP)
+
+    def relay(b):
+        b_far(b, pre_other.at[0], x_dev).wait_recv()
+        b_to_core(b, 2).start()
+
+    def attn_relay():
+        for k in range(n_attn):
+            attn_far(k).wait_recv()
+        b_to_core(6, 2).start()
+
+    def b_arrive(b):
+        b_to_core(b, 0).wait_recv()
+        b_to_core(b, 2).wait_recv()
 
     def at_slot(s, number, work):
         @pl.when(s == number)
         def _():
             work()
 
+    def sent_drain():
+        windows_drain()
+        for g in range(10):
+            for t in range(1, 4):
+                if not local(g, t):
+                    a_load(g, t).wait_send()
+        for b in range(2):
+            cot_load(b, 1).wait_send()
+            cot_load(b, 3).wait_send()
+        for b in range(2, 10):
+            b_to_core(b, 0).wait_send()
+            b_to_core(b, 2).wait_send()
+            if b != 6:
+                b_far(b, pre_other.at[0], x_dev).wait_send()
+        for k in range(n_attn):
+            attn_far(k).wait_send()
+
     def slot_step(s, carry):
-        at_slot(s, 0, lambda: arrive(phases[0]))
-        at_slot(s, 7, lambda: arrive(phases[1]))
-        at_slot(s, 15, lambda: arrive(phases[2]))
-
-        @pl.when((s >= 8) & (s < 16) & (s % 2 == 0))
-        def _():
-            peer_b(1 + (s - 8) // 2).wait_recv()
-
-        at_slot(s, 16, lambda: peer_b(5).wait_recv())
-        at_slot(s, 18, lambda: [peer_b(i).wait_recv() for i in range(6, 9)])
-
+        at_slot(s, 0, lambda: [cot_load(b, 0).wait() for b in range(2)])
+        at_slot(s, 0, normed_load.wait)
+        for u in range(3):
+            j = 3 * s + u
+
+            @pl.when(j < n_ff)
+            def _():
+                ffn_first(j)
+
+        at_slot(s, 2, first_load.wait)
+        at_slot(s, 2, ffn_between)
+        for u in range(3):
+            j = 3 * (s - 3) + u
+
+            @pl.when((j >= 0) & (j < n_ff))
+            def _():
+                ffn_second(j)
+
+        at_slot(s, MIDDLE, attn_load.wait)
+        at_slot(s, MIDDLE, att_load.wait)
+        at_slot(s, MIDDLE, middle_first)
+        at_slot(s, MIDDLE, middle_second)
+        at_slot(s, MIDDLE, rows_arrive)
+
+        def relay_blocks(low, high, first_round, ahead):
+            k = s + ahead - FIRST - first_round
+
+            @pl.when((k >= 0) & (k < 2 * (high - low)) & (k % 2 == 0))
+            def _():
+                relay(low + k // 2)
+
+        def arrive_blocks(low, high, first_round):
+            k = s - FIRST - first_round
+
+            @pl.when((k >= 0) & (k < 2 * (high - low)) & (k % 2 == 0))
+            def _():
+                b_arrive(low + k // 2)
+
+        at_slot(s, FIRST, lambda: [[cot_load(b, 1).wait_recv(), cot_load(b, 2).wait(), cot_load(b, 3).wait_recv()] for b in range(2)])
+        for g in range(4):
+            at_slot(s, FIRST + 2 * g, functools.partial(a_arrive, g))
+        for g in range(4, 10):
+            at_slot(s, FIRST + (7, 17, 15)[(g - 4) // 2], functools.partial(a_arrive, g))
+        relay_blocks(2, 6, 8, 1)
+        at_slot(s, FIRST + 17, attn_relay)
+        relay_blocks(7, 8, 16, 1)
+        relay_blocks(8, 10, 20, 1)
+        arrive_blocks(2, 6, 8)
+        arrive_blocks(6, 7, 18)
+        arrive_blocks(7, 8, 16)
+        arrive_blocks(8, 10, 20)
+
+        at_slot(s, FIRST + rounds + 2, sent_drain)
         for lag, work in plan:
-            r = s - lag
+            r = s - lag - FIRST
 
             @pl.when((r >= 0) & (r < rounds))
             def _():
                 work(r)
 
-        r = s - last
-
-        @pl.when(r >= 0)
-        def _():
-            for here, cp in share(r):
-                pl.when(here)(cp.start)
-
-        at_slot(s, 0, normed_load.wait)
-        for u in range(3):
-            j = 3 * s + u
-
-            @pl.when(j < n_ff)
-            def _():
-                ffn_first(j)
-
-        at_slot(s, 2, ffn_between)
-        for u in range(3):
-            j = 3 * (s - 3) + u
-
-            @pl.when((j >= 0) & (j < n_ff))
-            def _():
-                ffn_second(j)
-
-        at_slot(s, MIDDLE, middle_first)
-        at_slot(s, MIDDLE, middle_second)
-        at_slot(s, MIDDLE, rows_arrive)
-        at_slot(s, MIDDLE + 2, cross_arrive)
         i = s - MIDDLE
 
         @pl.when((i >= 0) & (i < n_pairs))
@@ -1064,37 +1230,52 @@
         def _():
             attend_near(i - 1)
 
-        @pl.when((i >= 2) & (i < n_pairs + 2))
-        def _():
-            cross_relay(i - 2)
-
-        @pl.when((i >= 3) & (i < n_pairs + 3))
-        def _():
-            attend_far(i - 3)
-
+        at_slot(s, MIDDLE + FAR - 1, cross_arrive)
+        at_slot(s, MIDDLE + FAR, others_arrive)
+
+        @pl.when((i >= FAR - 1) & (i < n_pairs + FAR - 1))
+        def _():
+            cross_relay(i - (FAR - 1))
+
+        @pl.when((i >= FAR) & (i < n_pairs + FAR))
+        def _():
+            attend_far(i - FAR)
+
+        for k in range(n_attn):
+            at_slot(s, FIRST + 12 + k, attn_far(k).start)
+        at_slot(s, MIDDLE + 4, lambda: proj_out([(0, 0)]))
+        at_slot(s, MIDDLE + FAR + 3, lambda: proj_out([(1, 0), (0, 2)]))
+        at_slot(s, MIDDLE + 8, lambda: proj_out([(0, 1)]))
+        at_slot(s, after - 1, lambda: proj_out([(1, 1), (1, 2)]))
         at_slot(s, after - 1, input_first)
         at_slot(s, after, input_second)
         for i in range(8):
-            @pl.when(s == after + i)
+            @pl.when(s == after + 2 * i)
             def _():
                 vector_step(i)
 
         return carry
 
-    lax.fori_loop(0, rounds + last, slot_step, 0)
+    lax.fori_loop(0, FIRST + rounds + last, slot_step, 0)
     lax.fori_loop(rounds - SEND, rounds, lambda r, carry: (drain(r), carry)[1], 0)
-    windows_drain()
-    for phase in phases:
-        for item in phase:
-            loads(*item, False).wait_send()
-    for i in range(1, 9):
-        peer_b(i).wait_send()
+
+    def swap_drain(r, carry):
+        @pl.when(~mine(r))
+        def _():
+            step_swap(r).wait_send()
+
+        return carry
+
+    lax.fori_loop(8, rounds, swap_drain, 0)
     for i in range(7):
         for cp in vstep(i):
             cp.wait_send()
 
+    layer_copy.wait()
+    grad_copy.wait()
+
     def share_wait(r, carry):
-        share(jnp.int32(0))[0][1].wait()
+        share_copies(jnp.int32(0), out.at[0], x)[0][1].wait()
         return carry
 
     lax.fori_loop(0, rounds, share_wait, 0)
@@ -1156,41 +1337,40 @@
 ):
     tok, width = tokens.shape
     ff = w_fc1.shape[1]
-    (low_in_t, q_win, k_win, v_win, att, lse, scaled_t, attn, first, low_mid_t, normed, slope, scale_ffn, low_ffn, low_ffn_t) = forward(
+    (low_in_t, q_win, k_win, v_win, att, lse, scaled_t, attn, first, low_mid_t, normed, slope, scale_ffn, low_ffn, low_ffn_t,
+     cot_x, low_in_x, low_mid_x, scaled_y) = forward(
         lengths, tokens, ln1_gain, ln1_bias, w_qkv, qv_bias, head_scale, w_out, out_bias, lnpa_gain, lnpa_bias, ln2_gain, ln2_bias,
-        w_fc1, fc1_bias, lnf_gain, lnf_bias)
+        w_fc1, fc1_bias, lnf_gain, lnf_bias, cotangent)
     rounds = 24
     hbm, vmem, smem = (pl.BlockSpec(memory_space=space) for space in (pl.ANY, pltpu.VMEM, pltpu.SMEM))
-    a_shape = (14, 4, 2, 2, ROWS, tok)
-    b_shape = (9, tok, WR)
-    msgs = [(4, 2, ROWS, WX), (4, 2, ROWS, WX), (4, ROWS, WX), (4, ROWS, WX), (3, ROWS, 2 * WX), (3, ROWS, 2 * WX),
-            (3, 2, 2, ROWS, WZ), (3, 2, 2, ROWS, WZ), (2, ROWS, WZ // 2), (2, ROWS, WZ // 2), (ROWS, WZ // 2), (ROWS, WZ // 2)]
+    msgs = [(4, ROWS, WY), (3, ROWS, WY), (3, ROWS, WY), (3, 2, ROWS, WZ), (3, 2, ROWS, WZ), (ROWS, WZ)]
+    n_swap = 8
     sizes = (width, width, 2 * width) + (width,) * 6 + (ff, ff, ff)
     v = -(-(sum(sizes) + 128) // 8192) * 64
     dma, shape = pltpu.SemaphoreType.DMA, jax.ShapeDtypeStruct
-    f32s = [(4, 2, ROWS, WX), (4, 2, ROWS, WX), (KEEP, 4, ROWS, 2 * WX), (2, 2, ROWS, WZ), (KEEP, 2, 2, ROWS, WZ // 2),
-            (KEEP, 4, ROWS, WX), (KEEP, 4, ROWS, WX), (rounds, ROWS, WR), (v, 128), (v, 128), (v // 2 + v // 4 + v // 8 * 5, 128)]
+    f32s = [(KEEP, 4, 2, ROWS, WR), (2, ROWS, WZ), (KEEP, ROWS, WZ), (rounds, ROWS, WR), (n_swap, ROWS, WR),
+            (v, 128), (v, 128), (v // 2 + v // 4 + v // 8 * 5, 128)]
     windows = [pltpu.VMEM((3, tok, width), BF16)] * 4 + [pltpu.VMEM((3, 2 * HEADS, tok), F32)]
-    more = [(3 * tok, tok), (tok, 2 * tok), (2 * width // HEADS, tok), (2, tok, width // HEADS), (2, tok, width // HEADS),
-            (tok, width), (tok, width), (tok, ff), (4, tok, 128)]
+    more = [(3 * tok, tok), (tok, 2 * tok), (tok, width), (tok, width), (tok, ff), (4, tok, 128), (tok, width), (tok, width), (tok, width)]
     out2, out1, outo, outq, flat, grad_tokens, layer_out = pl.pallas_call(
         functools.partial(back_kernel, tok),
         out_shape=[shape((ff // 32, width), F32), shape((width // 32, ff), F32), shape((width // 32, width), F32),
                    shape((width // 32, 3 * width), F32), shape((v, 128), F32), shape((tok, width), F32), shape((tok, width), BF16)],
-        in_specs=[hbm] * 5 + [smem] + [hbm] * 3 + [vmem] * 10 + [smem, vmem] + [hbm] * 7,
-        out_specs=[hbm] * 4 + [vmem] * 3,
-        scratch_shapes=[pltpu.VMEM(a_shape, BF16), pltpu.VMEM(a_shape, BF16), pltpu.VMEM(b_shape, BF16), pltpu.VMEM(b_shape, BF16)]
-        + [pltpu.VMEM((SEND,) + m, BF16) for m in msgs]
-        + [pltpu.VMEM((RECV,) + m, BF16) for m in msgs]
+        in_specs=[hbm] * 9 + [smem] + [hbm] * 3 + [vmem] + [hbm] * 3 + [vmem] * 6 + [smem, vmem] + [hbm] * 7,
+        out_specs=[hbm] * 4 + [vmem] + [hbm] * 2,
+        scratch_shapes=[pltpu.VMEM((10, 4, 4, 2, ROWS, tok), BF16), pltpu.VMEM((10, 4, tok, WR), BF16), pltpu.VMEM((4, tok, WR), BF16),
+                        pltpu.VMEM((tok, WR), BF16), pltpu.VMEM((6, tok, WR), BF16)]
+        + [pltpu.VMEM((SEND,) + m, BF16) for m in msgs] + [pltpu.VMEM((n_swap, ROWS, WR), BF16)]
+        + [pltpu.VMEM((RECV + (2 if m[0] in (4, ROWS) else 0),) + m, BF16) for m in msgs] + [pltpu.VMEM((n_swap, ROWS, WR), BF16)]
         + [pltpu.VMEM(m, F32) for m in f32s] + windows + [pltpu.VMEM(m, F32) for m in more]
-        + [pltpu.VMEM((tok, ff), BF16), pltpu.VMEM((PIECES, FC, width), BF16), pltpu.VMEM((PIECES, width, FC), BF16),
+        + [pltpu.VMEM((tok, width), BF16), pltpu.VMEM((tok, ff), BF16), pltpu.VMEM((PIECES, FC, width), BF16), pltpu.VMEM((PIECES, width, FC), BF16),
            pltpu.VMEM((PIECES, tok, FC), BF16), pltpu.VMEM((PIECES, tok, FC), BF16),
-           dma((15,)), dma((23,)), dma((23,)), dma((12, SEND)), dma((12, RECV)), dma((10,)), dma((10,)), dma((4 + HEADS,)), dma((4 + HEADS,)),
-           dma((4,)), dma((PIECES,)), dma((PIECES,)), dma((PIECES,)), dma((PIECES,)), dma((1,))],
+           dma((10, 4)), dma((10, 4)), dma((10, 4)), dma((10, 4)), dma((6, SEND)), dma((6, RECV + 2)), dma((10,)), dma((10,)), dma((4 + HEADS,)), dma((4 + HEADS,)),
+           dma((9,)), dma((PIECES,)), dma((PIECES,)), dma((PIECES,)), dma((PIECES,)), dma((2, n_swap)), dma((2, WR * HEADS // (2 * width))), dma((1,))],
         compiler_params=pltpu.CompilerParams(collective_id=0, has_side_effects=True, vmem_limit_bytes=63 << 20),
         cost_estimate=pl.CostEstimate(flops=30 << 30, bytes_accessed=50 << 20, transcendentals=4 << 20),
-    )(blocks_first(low_ffn_t), blocks_first(low_mid_t), blocks_first(scaled_t), blocks_first(low_in_t),
-      cotangent, lengths, q_win, k_win, v_win, lse, att, attn, first, scale_ffn, tokens,
+    )(blocks_first(low_ffn_t), blocks_first(low_mid_t), blocks_first(low_mid_x), blocks_first(scaled_t), blocks_first(scaled_y),
+      blocks_first(low_in_t), blocks_first(low_in_x), cotangent, cot_x, lengths, q_win, k_win, v_win, lse, att, attn, first, scale_ffn, tokens,
       ln1_gain[None], lnpa_gain[None], ln2_gain[None], lnf_gain[None], head_scale[None], fc2_bias[None],
       normed, slope, low_ffn, w_fc2, w_fc1, w_out, w_qkv)
     return finish(layer_out, grad_tokens, out2, out1, outo, outq, flat, sizes)

time: 172 us -> 159 us (0.924)
  Pallas kernels: 171 us -> 158 us
    pallas_call x1, Pallas kernels: 130 us -> 113 us  [fast_shards(): pl.pallas_call(functools.partial(back_kernel, tok), out_shape=[shape((ff...]
    pallas_call x1, Pallas kernels: 36.5 us -> 41.3 us  [forward(): pl.pallas_call(forward_kernel, out_shape=[shape((width, rows), BF16), sha...]
where the time goes in v4:
time: 159 us
  Pallas kernels  158 us (99%)
    pallas_call x1, Pallas kernels, fast_shards(): pl.pallas_call(functools.partial(back_kernel, tok), out_shape=[shape((ff...  113 us
    pallas_call x1, Pallas kernels, forward(): pl.pallas_call(forward_kernel, out_shape=[shape((width, rows), BF16), sha...  41.3 us
    pallas_call x1, Pallas kernels, finish(): pl.pallas_call(functools.partial(finish_kernel, len(big), tuple(rows_of))...  3.65 us

profile of v4, /device:TPU:0, one launch (start us, length us, event | category | flops | bytes accessed | tf_op | source)
XLA Modules:
  0.0 158.6 jit_solution(1276677656469313732)
XLA Ops:
  0.7 41.3 %shard_map.339 = (bf16[1024,256]{1,0:T(8,128)(2,1)}, bf16[3,256,1024]{2,1,0:T(8,128)(2,1)}, bf16[3,256,1024]{2,1,0:T(8,128)(2,1)}, bf16[3,256,1024]{2,1,0:T(8,12...) custom-call(s32[1,5]{1,0:T(1,128)} %lens.3, ...), custom_call_target="tpu_custom_call" | custom-call | flops 12884901888 | bytes 41943040 | tf_op jit(solution)/shard_map/pallas_call | solution.py:353
  42.0 112.8 %shard_map.340 = (f32[128,1024]{1,0:T(8,128)}, f32[32,4096]{1,0:T(8,128)}, f32[32,1024]{1,0:T(8,128)}, f32[32,3072]{1,0:T(8,128)}, f32[192,128]{1,0:T(8,128)}, /...) custom-call(bf16[4,2,2,2,4,32,256]{6,5,4,3,2,1,0:T(8,128)(2,1)} %bitcast.64, bf16[4,2,2,2,1,32,256]{6,5,4,3,2,1,0:T(8,128)(2,1)} %bitcast.67, ...), custom_call_target="tpu_custom_call" | custom-call | flops 32212254720 | bytes 52428800 | tf_op jit(solution)/shard_map/pallas_call | solution.py:1355
  154.8 3.6 %shard_map.341 = (bf16[256,1024]{1,0:T(8,128)(2,1)}, f32[256,1024]{1,0:T(8,128)}, f32[128,1024]{1,0:T(8,128)}, f32[32,4096]{1,0:T(8,128)}, f32[32,1024]{1,0:T(8,...) custom-call(bf16[256,1024]{1,0:T(8,128)(2,1)} %get-tuple-element.83., ...), custom_call_target="tpu_custom_call" | custom-call | tf_op jit(solution)/shard_map/pallas_call | solution.py:1319

commit v5 on v4

--- a/solution.py
+++ b/solution.py
@@ -86,14 +86,15 @@
                    w1_hbm, fc1_bias, ffn_gain, ffn_bias, cot,
                    low_in_t, qw_out, kw_out, vw_out, att_out, lse, scaled_t, attn_out, first_out, low_mid_t, normed_out, slope_out,
                    scale_out, low_ffn_out, low_ffn_t, cot_x, low_in_x, low_mid_x, scaled_y,
-                   w, wo, w1, tok_y, low_in, low_y, qw, kw, vw, mask, acc, att, attn, first, low_mid, act, part, turned, normed,
+                   w, wo, w1, tok_y, low_in, low_y, qw, kw, vw, mask, acc, att, attn, first, low_mid, act, part, turned_in, turned, normed,
                    slope, low_ffn, ffn_turned, w_sem, sends, recvs, out_sem):
     dp, blk = lax.axis_index("dp"), lax.axis_index("blk")
     x, y, c = dp % 2, blk // 2, blk % 2
     core_dev, x_dev, y_dev = (dp, blk + 1 - 2 * c), (dp + 1 - 2 * x, blk), (dp, blk + 2 - 4 * y)
     rows, width = tok.shape
     dim = width // HEADS
-    half = rows // 2
+    parts_y = 4
+    half = rows // parts_y
     ff = w1.shape[1]
     n_ff = ff // FC
 
@@ -111,11 +112,11 @@
     for dev in (core_dev, x_dev, y_dev):
         pl.semaphore_signal(bar, inc=1, device_id=dev, device_id_type=MESH)
     pl.semaphore_wait(bar, 3)
-    cross = [remote(tok.at[pl.ds(i * half, half)], tok_y.at[pl.ds(i * half, half)], i, y_dev) for i in range(2)]
+    cross = [remote(tok.at[pl.ds(i * half, half)], tok_y.at[pl.ds(i * half, half)], (0, 1, 12, 13)[i], y_dev) for i in range(parts_y)]
     for cp in cross:
         cp.start()
 
-    ahead = [remote(cot, cot_x, 8, x_dev), remote(turned.at[0], low_in_x, 9, x_dev), remote(turned.at[2], low_mid_x, 10, x_dev),
+    ahead = [remote(cot, cot_x, 8, x_dev), remote(turned_in.at[:, c], low_in_x, 9, x_dev), remote(turned.at[0], low_mid_x, 10, x_dev),
              remote(turned.at[1], scaled_y, 11, y_dev)]
     ahead[0].start()
     outs = []
@@ -171,11 +172,11 @@
     def _():
         own_q.start()
 
-    turned[0] = low_in[...].T
+    turned_in[...] = low_in[...].T.reshape(turned_in.shape)
     ahead[1].start()
-    emit(turned.at[0], low_in_t)
-
-    for i in range(2):
+    emit(turned_in, low_in_t)
+
+    for i in range(parts_y):
         cross[i].wait_recv()
         low_y[i * half:(i + 1) * half] = norm_in(tok_y[i * half:(i + 1) * half].astype(F32), gain[...], bias[...]).astype(BF16)
 
@@ -210,32 +211,39 @@
     emit(kw, kw_out)
     emit(vw, vw_out)
 
+    group = 8
+
     def heads(lowest):
-        def pair(i, carry):
-            cols = pl.ds(pl.multiple_of(i * 2 * dim, 2 * dim), 2 * dim)
-            q2 = qw[0, :, cols]
-            k2 = [kw[j, :, cols] for j in range(lowest, 3)]
-            v2 = [vw[j, :, cols] for j in range(lowest, 3)]
-            for sub in range(2):
-                one_head = slice(sub * dim, (sub + 1) * dim)
-                scores = [dot_nt(k[:, one_head], q2[:, one_head]) + mask[(lowest + n) * rows:(lowest + n + 1) * rows]
-                          for n, k in enumerate(k2)]
-                top = jnp.max(scores[0], axis=0, keepdims=True)
-                for s in scores[1:]:
+        def some(i, carry):
+            scores, tops, values = [], [], []
+            for h in range(group):
+                cols = pl.ds(pl.multiple_of((i * group + h // 2 * 2) * dim, 2 * dim), 2 * dim)
+                q2 = qw[0, :, cols]
+                one = slice(h % 2 * dim, (h % 2 + 1) * dim)
+                scores.append([])
+                for j in range(lowest, 3):
+                    k = kw[j, :, cols]
+                    scores[h].append(dot_nt(k[:, one], q2[:, one]) + mask[j * rows:(j + 1) * rows])
+            for h in range(group):
+                top = jnp.max(scores[h][0], axis=0, keepdims=True)
+                for s in scores[h][1:]:
                     top = jnp.maximum(top, jnp.max(s, axis=0, keepdims=True))
+                tops.append(top)
+            for h in range(group):
+                cols = pl.ds(pl.multiple_of((i * group + h // 2 * 2) * dim, 2 * dim), 2 * dim)
                 total, out = None, None
-                for s, v in zip(scores, v2):
-                    p = jnp.exp(s - top)
+                for j, s in zip(range(lowest, 3), scores[h]):
+                    p = jnp.exp(s - tops[h])
                     one = jnp.sum(p, axis=0, keepdims=True)
-                    term = dot_tn(v[:, one_head], p.astype(BF16))
+                    term = dot_tn(vw[j, :, cols], p.astype(BF16))[h % 2 * dim:(h % 2 + 1) * dim]
                     total = one if total is None else total + one
                     out = term if out is None else out + term
-                acc[one_head] = out / total
-                lse[pl.ds(2 * i + sub, 1)] = top + jnp.log(total)
-            att[:, cols] = acc[...].T
+                acc[h * dim:(h + 1) * dim] = out / total
+                lse[pl.ds(i * group + h, 1)] = tops[h] + jnp.log(total)
+            att[:, pl.ds(pl.multiple_of(i * group * dim, group * dim), group * dim)] = acc[...].T
             return carry
 
-        lax.fori_loop(0, HEADS // 2, pair, 0)
+        lax.fori_loop(0, HEADS // group, some, 0)
 
     @pl.when(blk == 0)
     def _():
@@ -270,9 +278,9 @@
     first[...] = tok[...].astype(F32) + norm_in(attn[...], pa_gain[...], pa_bias[...])
     emit(first, first_out)
     low_mid[...] = norm_in(first[...], mid_gain[...], mid_bias[...]).astype(BF16)
-    turned[2] = low_mid[...].T
+    turned[0] = low_mid[...].T
     ahead[2].start()
-    emit(turned.at[2], low_mid_t)
+    emit(turned.at[0], low_mid_t)
     loads[7].wait()
     part[...] = jnp.zeros_like(part)
 
@@ -352,21 +360,21 @@
     dma = pltpu.SemaphoreType.DMA
     return pl.pallas_call(
         forward_kernel,
-        out_shape=[shape((width, rows), BF16), shape(window, BF16), shape(window, BF16), shape(window, BF16),
+        out_shape=[shape((16, 2, width // 32, rows), BF16), shape(window, BF16), shape(window, BF16), shape(window, BF16),
                    shape((rows, width), F32), shape((HEADS, rows), F32), shape((width, rows), BF16), shape((rows, width), F32),
                    shape((rows, width), F32), shape((width, rows), BF16), shape(wide, BF16), shape(wide, BF16),
-                   shape((rows, 128), F32), shape(wide, BF16), shape(tall, BF16), shape((rows, width), BF16), shape((width, rows), BF16),
+                   shape((rows, 128), F32), shape(wide, BF16), shape(tall, BF16), shape((rows, width), BF16), shape((16, width // 32, rows), BF16),
                    shape((width, rows), BF16), shape((width, rows), BF16)],
         in_specs=[smem, vmem, vmem, vmem, hbm, vmem, smem, hbm] + [vmem] * 5 + [hbm] + [vmem] * 3 + [hbm],
         out_specs=[hbm] * 5 + [vmem] + [hbm] * 6 + [vmem] + [hbm] * 6,
         scratch_shapes=[pltpu.VMEM((width, 3 * width), BF16), pltpu.VMEM((width, width), BF16), pltpu.VMEM((width, ff), BF16),
                         pltpu.VMEM((rows, width), BF16), pltpu.VMEM((rows, width), BF16), pltpu.VMEM((rows, width), BF16),
                         pltpu.VMEM(window, BF16), pltpu.VMEM(window, BF16), pltpu.VMEM(window, BF16),
-                        pltpu.VMEM((3 * rows, rows), F32), pltpu.VMEM((2 * width // HEADS, rows), F32),
+                        pltpu.VMEM((3 * rows, rows), F32), pltpu.VMEM((8 * width // HEADS, rows), F32),
                         pltpu.VMEM((rows, width), F32), pltpu.VMEM((rows, width), F32), pltpu.VMEM((rows, width), F32),
                         pltpu.VMEM((rows, width), BF16), pltpu.VMEM(wide, F32), pltpu.VMEM((2, rows, 128), F32),
-                        pltpu.VMEM((3, width, rows), BF16), pltpu.VMEM(wide, BF16), pltpu.VMEM(wide, BF16), pltpu.VMEM(wide, BF16),
-                        pltpu.VMEM(tall, BF16), dma((8,)), dma((12,)), dma((12,)), dma((13,))],
+                        pltpu.VMEM((16, 2, width // 32, rows), BF16), pltpu.VMEM((2, width, rows), BF16), pltpu.VMEM(wide, BF16), pltpu.VMEM(wide, BF16), pltpu.VMEM(wide, BF16),
+                        pltpu.VMEM(tall, BF16), dma((8,)), dma((14,)), dma((14,)), dma((13,))],
         compiler_params=pltpu.CompilerParams(collective_id=1, has_side_effects=True, vmem_limit_bytes=60 << 20),
         cost_estimate=pl.CostEstimate(flops=12 << 30, bytes_accessed=40 << 20, transcendentals=5 << 20),
     )(lengths, tokens, ln1_gain[None], ln1_bias[None], w_qkv, qv_bias[None], head_scale[None], w_out, out_bias[None],
@@ -383,7 +391,7 @@
 FIRST = 2
 LAG_Y = (0, 2, 4, 6, 8)
 LAG_Z = (0, 2, 4, 6, 8)
-LAG_SWAP = (9, 11)
+LAG_SWAP = (8, 10)
 MIDDLE = 6
 FAR = 3
 PIECES = 3
@@ -484,10 +492,11 @@
             return pltpu.make_async_copy(rows_of(a_own[g], g, x, c), am.at[g, 0], a_recv.at[g, 0])
         if t == 1:
             return remote(rows_of(a_own[g], g, x, 1 - c), am.at[g, 1], *sems, core_dev)
-        if g < 4:
-            return remote(rows_of(a2, g, 1 - x, c if t == 2 else 1 - c), am.at[g, t], *sems, x_dev if t == 2 else cross_dev)
+        if g < 4 or (g >= 8 and t == 3):
+            return remote(rows_of(a_own[g], g, 1 - x, c if t == 2 else 1 - c), am.at[g, t], *sems, x_dev if t == 2 else cross_dev)
         if t == 2:
-            return pltpu.make_async_copy(rows_of(a_far[g], g, x, c), am.at[g, 2], a_recv.at[g, 2])
+            part = rows_of(a_far[g], g, x, c) if g < 8 else aqx.at[:, g % 2]
+            return pltpu.make_async_copy(part, am.at[g, 2], a_recv.at[g, 2])
         return remote(rows_of(a_far[g], g, x, 1 - c), am.at[g, 3], *sems, core_dev)
 
     def cot_load(b, t):
@@ -520,7 +529,7 @@
         return remote(attn_other.at[:, cols], bm.at[6, 2, :, cols], attn_sems.at[0, k], attn_sems.at[1, k], y_dev)
 
     def proj_block(who, k):
-        return jnp.where(who == 0, k, jnp.where(k == 0, 4, jnp.where(k == 1, 3, 5)))
+        return jnp.where(who == 0, k + k // 2, jnp.where(k == 0, 4, 3 * k - 1))
 
     def proj_far(k):
         return b_far(7 + k, dpj.at[proj_block(1 - x, k)], x_dev)
@@ -563,13 +572,14 @@
             cot_load(g, 3).start()
     for g in range(4, 10):
         a_load(g, 1).start()
-        a_load(g, 3).start()
+        if g < 8:
+            a_load(g, 3).start()
 
     def is_out(r):
-        return (r >= 18) & (r < 20)
+        return (r >= 20) & (r < 22)
 
     def proj_turn(r):
-        return jnp.where(r < 18, 0, (r - 18) // 2)
+        return jnp.where(r < 20, (r - 16) // 2, 2)
 
     def place(r):
         q = r % 2
@@ -1096,7 +1106,7 @@
         for who, k in blocks:
             @pl.when(x == who)
             def _():
-                bm[7 + k, 0] = dpj[(0, 1, 2)[k] if who == 0 else (4, 3, 5)[k]]
+                bm[7 + k, 0] = dpj[((0, 1, 3), (4, 2, 5))[who][k]]
                 b_to_core(7 + k, 0).start()
 
             @pl.when(x != who)
@@ -1178,6 +1188,7 @@
             def _():
                 ffn_second(j)
 
+        at_slot(s, MIDDLE + 6, lambda: [a_load(g, 3).start() for g in (8, 9)])
         at_slot(s, MIDDLE, attn_load.wait)
         at_slot(s, MIDDLE, att_load.wait)
         at_slot(s, MIDDLE, middle_first)
@@ -1202,17 +1213,17 @@
         for g in range(4):
             at_slot(s, FIRST + 2 * g, functools.partial(a_arrive, g))
         for g in range(4, 10):
-            at_slot(s, FIRST + (7, 17, 15)[(g - 4) // 2], functools.partial(a_arrive, g))
+            at_slot(s, FIRST + (7, 19, 15)[(g - 4) // 2], functools.partial(a_arrive, g))
         relay_blocks(2, 6, 8, 1)
-        at_slot(s, FIRST + 17, attn_relay)
-        relay_blocks(7, 8, 16, 1)
-        relay_blocks(8, 10, 20, 1)
+        at_slot(s, FIRST + 19, attn_relay)
+        relay_blocks(7, 9, 16, 1)
+        relay_blocks(9, 10, 22, 1)
         arrive_blocks(2, 6, 8)
-        arrive_blocks(6, 7, 18)
-        arrive_blocks(7, 8, 16)
-        arrive_blocks(8, 10, 20)
-
-        at_slot(s, FIRST + rounds + 2, sent_drain)
+        arrive_blocks(6, 7, 20)
+        arrive_blocks(7, 9, 16)
+        arrive_blocks(9, 10, 22)
+
+        at_slot(s, FIRST + rounds + 3, sent_drain)
         for lag, work in plan:
             r = s - lag - FIRST
 
@@ -1244,13 +1255,13 @@
         for k in range(n_attn):
             at_slot(s, FIRST + 12 + k, attn_far(k).start)
         at_slot(s, MIDDLE + 4, lambda: proj_out([(0, 0)]))
-        at_slot(s, MIDDLE + FAR + 3, lambda: proj_out([(1, 0), (0, 2)]))
+        at_slot(s, MIDDLE + FAR + 3, lambda: proj_out([(1, 0), (1, 1)]))
         at_slot(s, MIDDLE + 8, lambda: proj_out([(0, 1)]))
-        at_slot(s, after - 1, lambda: proj_out([(1, 1), (1, 2)]))
+        at_slot(s, after - 1, lambda: proj_out([(0, 2), (1, 2)]))
         at_slot(s, after - 1, input_first)
         at_slot(s, after, input_second)
         for i in range(8):
-            @pl.when(s == after + 2 * i)
+            @pl.when(s == after + 2 * i + (2 if i > 3 else 0))
             def _():
                 vector_step(i)
 
@@ -1370,7 +1381,7 @@
         compiler_params=pltpu.CompilerParams(collective_id=0, has_side_effects=True, vmem_limit_bytes=63 << 20),
         cost_estimate=pl.CostEstimate(flops=30 << 30, bytes_accessed=50 << 20, transcendentals=4 << 20),
     )(blocks_first(low_ffn_t), blocks_first(low_mid_t), blocks_first(low_mid_x), blocks_first(scaled_t), blocks_first(scaled_y),
-      blocks_first(low_in_t), blocks_first(low_in_x), cotangent, cot_x, lengths, q_win, k_win, v_win, lse, att, attn, first, scale_ffn, tokens,
+      blocks_first(low_in_t.reshape(width, tok)), low_in_x.reshape(4, 2, 2, ROWS, tok), cotangent, cot_x, lengths, q_win, k_win, v_win, lse, att, attn, first, scale_ffn, tokens,
       ln1_gain[None], lnpa_gain[None], ln2_gain[None], lnf_gain[None], head_scale[None], fc2_bias[None],
       normed, slope, low_ffn, w_fc2, w_fc1, w_out, w_qkv)
     return finish(layer_out, grad_tokens, out2, out1, outo, outq, flat, sizes)

time: 159 us -> 153 us (0.962)
  Pallas kernels: 158 us -> 152 us
    pallas_call x1, Pallas kernels: 41.3 us -> 37.4 us  [forward(): pl.pallas_call(forward_kernel, out_shape=[shape((16, 2, width // 32, rows...]
    pallas_call x1, Pallas kernels: 113 us -> 110 us  [fast_shards(): pl.pallas_call(functools.partial(back_kernel, tok), out_shape=[shape((ff...]
where the time goes in v5:
time: 153 us; the launch traced here: 152 us
  Pallas kernels  152 us (99%)
    pallas_call x1, Pallas kernels, fast_shards(): pl.pallas_call(functools.partial(back_kernel, tok), out_shape=[shape((ff...  110 us
    pallas_call x1, Pallas kernels, forward(): pl.pallas_call(forward_kernel, out_shape=[shape((16, 2, width // 32, rows...  37.4 us
    pallas_call x1, Pallas kernels, finish(): pl.pallas_call(functools.partial(finish_kernel, len(big), tuple(rows_of))...  3.65 us

profile of v5, /device:TPU:0, one launch (start us, length us, event | category | flops | bytes accessed | tf_op | source)
XLA Modules:
  0.0 152.3 jit_solution(7514762740354878741)
XLA Ops:
  0.7 37.4 %shard_map.339 = (bf16[16,2,32,256]{3,2,1,0:T(8,128)(2,1)}, bf16[3,256,1024]{2,1,0:T(8,128)(2,1)}, bf16[3,256,1024]{2,1,0:T(8,128)(2,1)}, bf16[3,256,1024]{2,1,0...) custom-call(s32[1,5]{1,0:T(1,128)} %lens.3, ...), custom_call_target="tpu_custom_call" | custom-call | flops 12884901888 | bytes 41943040 | tf_op jit(solution)/shard_map/pallas_call | solution.py:361
  38.1 110.5 %shard_map.340 = (f32[128,1024]{1,0:T(8,128)}, f32[32,4096]{1,0:T(8,128)}, f32[32,1024]{1,0:T(8,128)}, f32[32,3072]{1,0:T(8,128)}, f32[192,128]{1,0:T(8,128)}, /...) custom-call(bf16[4,2,2,2,4,32,256]{6,5,4,3,2,1,0:T(8,128)(2,1)} %bitcast.64, bf16[4,2,2,2,1,32,256]{6,5,4,3,2,1,0:T(8,128)(2,1)} %bitcast.67, ...), custom_call_target="tpu_custom_call" | custom-call | flops 32212254720 | bytes 52428800 | tf_op jit(solution)/shard_map/pallas_call | solution.py:1366
  148.5 3.6 %shard_map.341 = (bf16[256,1024]{1,0:T(8,128)(2,1)}, f32[256,1024]{1,0:T(8,128)}, f32[128,1024]{1,0:T(8,128)}, f32[32,4096]{1,0:T(8,128)}, f32[32,1024]{1,0:T(8,...) custom-call(bf16[256,1024]{1,0:T(8,128)(2,1)} %get-tuple-element.83., ...), custom_call_target="tpu_custom_call" | custom-call | tf_op jit(solution)/shard_map/pallas_call | solution.py:1330

commit v6 on v5

--- a/solution.py
+++ b/solution.py
@@ -411,7 +411,7 @@
     y, c = blk // 2, blk % 2
     core_dev, x_dev, y_dev = (dp, blk + 1 - 2 * c), (dp + 1 - 2 * x, blk), (dp, blk + 2 - 4 * y)
     cross_dev = (dp + 1 - 2 * x, blk + 1 - 2 * c)
-    up_dev, down_dev = (dp + 2, blk), (dp - 2, blk)
+    up_dev, down_dev = ((dp + 2) % 8, blk), ((dp + 6) % 8, blk)
     rounds = 24
     rows, width = tokens.shape
     dim = width // HEADS
@@ -778,20 +778,22 @@
     def cols_at(start):
         return pl.ds(pl.multiple_of(start, WR), WR)
 
-    def share_copies(r, src, who):
-        k = (r - 8) // 2
-        return [((r < 8), pltpu.make_async_copy(src, out2.at[pl.ds(pl.multiple_of(r // 2 * ROWS, ROWS), ROWS), cols_at(r % 2 * WR)], out_sem.at[0])),
-                ((r >= 8) & (r < 16), pltpu.make_async_copy(src, out1.at[:, cols_at(who * (ff // 2) + k * WR)], out_sem.at[0])),
-                (is_out(r), pltpu.make_async_copy(src, outo.at[:, cols_at(who * WR)], out_sem.at[0])),
-                ((r >= 16) & ~is_out(r), pltpu.make_async_copy(src, outq.at[:, cols_at(proj_block(who, proj_turn(r)) * WR)], out_sem.at[0]))]
+    def share_out(r, src, who):
+        def go(here, place_of):
+            @pl.when(here)
+            def _():
+                pltpu.make_async_copy(src, place_of(), out_sem.at[0]).start()
+
+        go(r < 8, lambda: out2.at[pl.ds(pl.multiple_of(r // 2 * ROWS, ROWS), ROWS), cols_at(r % 2 * WR)])
+        go((r >= 8) & (r < 16), lambda: out1.at[:, cols_at(who * (ff // 2) + (r - 8) // 2 * WR)])
+        go(is_out(r), lambda: outo.at[:, cols_at(who * WR)])
+        go((r >= 16) & ~is_out(r), lambda: outq.at[:, cols_at(proj_block(who, proj_turn(r)) * WR)])
 
     def share(r):
-        for here, cp in share_copies(r, out.at[r], jnp.where(is_out(r), y, x)):
-            pl.when(here)(cp.start)
+        share_out(r, out.at[r], jnp.where(is_out(r), y, x))
 
     def share_far(r):
-        for here, cp in share_copies(r, swapped.at[swap_slot(r)], 1 - jnp.where(is_out(r), y, x)):
-            pl.when(here)(cp.start)
+        share_out(r, swapped.at[swap_slot(r)], 1 - jnp.where(is_out(r), y, x))
 
     def drain(r):
         step1(r).wait_send()
@@ -1286,7 +1288,7 @@
     grad_copy.wait()
 
     def share_wait(r, carry):
-        share_copies(jnp.int32(0), out.at[0], x)[0][1].wait()
+        pltpu.make_async_copy(out.at[0], out2.at[pl.ds(0, ROWS), pl.ds(0, WR)], out_sem.at[0]).wait()
         return carry
 
     lax.fori_loop(0, rounds, share_wait, 0)

time: 153 us -> 153 us (level)
  no operation moved by 1% of the time
where the time goes in v6:
time: 153 us; the launch traced here: 152 us
  Pallas kernels  152 us (99%)
    pallas_call x1, Pallas kernels, fast_shards(): pl.pallas_call(functools.partial(back_kernel, tok), out_shape=[shape((ff...  110 us
    pallas_call x1, Pallas kernels, forward(): pl.pallas_call(forward_kernel, out_shape=[shape((16, 2, width // 32, rows...  37.4 us
    pallas_call x1, Pallas kernels, finish(): pl.pallas_call(functools.partial(finish_kernel, len(big), tuple(rows_of))...  3.65 us

profile of v6, /device:TPU:0, one launch (start us, length us, event | category | flops | bytes accessed | tf_op | source)
XLA Modules:
  0.0 152.3 jit_solution(861057235863556921)
XLA Ops:
  0.7 37.4 %shard_map.339 = (bf16[16,2,32,256]{3,2,1,0:T(8,128)(2,1)}, bf16[3,256,1024]{2,1,0:T(8,128)(2,1)}, bf16[3,256,1024]{2,1,0:T(8,128)(2,1)}, bf16[3,256,1024]{2,1,0...) custom-call(s32[1,5]{1,0:T(1,128)} %lens.3, ...), custom_call_target="tpu_custom_call" | custom-call | flops 12884901888 | bytes 41943040 | tf_op jit(solution)/shard_map/pallas_call | solution.py:361
  38.1 110.5 %shard_map.340 = (f32[128,1024]{1,0:T(8,128)}, f32[32,4096]{1,0:T(8,128)}, f32[32,1024]{1,0:T(8,128)}, f32[32,3072]{1,0:T(8,128)}, f32[192,128]{1,0:T(8,128)}, /...) custom-call(bf16[4,2,2,2,4,32,256]{6,5,4,3,2,1,0:T(8,128)(2,1)} %bitcast.64, bf16[4,2,2,2,1,32,256]{6,5,4,3,2,1,0:T(8,128)(2,1)} %bitcast.67, ...), custom_call_target="tpu_custom_call" | custom-call | flops 32212254720 | bytes 52428800 | tf_op jit(solution)/shard_map/pallas_call | solution.py:1368
  148.5 3.6 %shard_map.341 = (bf16[256,1024]{1,0:T(8,128)(2,1)}, f32[256,1024]{1,0:T(8,128)}, f32[128,1024]{1,0:T(8,128)}, f32[32,4096]{1,0:T(8,128)}, f32[32,1024]{1,0:T(8,...) custom-call(bf16[256,1024]{1,0:T(8,128)(2,1)} %get-tuple-element.83., ...), custom_call_target="tpu_custom_call" | custom-call | tf_op jit(solution)/shard_map/pallas_call | solution.py:1332
